TPU v7x, 512 devices: a whole 4x8x8 slice. The times are simulated.
512 devices in a mesh: dp: 128 (over z, y, core), mp: 4 (over x).
Axes of the slice: x: 4, y: 8, z: 8, core: 2. Of those that a mesh axis runs over, the one named last changes fastest.
Arguments:
- query_states: bfloat16 [16384, 4096], P('dp', 'mp'), may hold values from -6 to 6
- passage_states: bfloat16 [16384, 4096], P('dp', 'mp'), may hold values from -6 to 6
- head_weight: bfloat16 [4096, 4096], P('dp', 'mp'), may hold values from -0.09375 to 0.09375
- positives: int32 [16384], P('dp'), may hold values from 0 to 127
- negatives: int32 [16384, 1], P('dp'), may hold values from 0 to 127; in each aligned block of 128 rows (0 to 127, 128 to 255, ...) at most 2 rows name the same one
Outputs:
- query_grads: float32 [16384, 4096], P('dp', 'mp')
- passage_grads: float32 [16384, 4096], P('dp', 'mp')
Inputs may be any that keep to these rules, and one draw needn't show every extreme that they name: `positives`: positives_i indexes the 128 passages of query i's own shard, in that shard's order. `negatives`: the 1 block of a query are different; block b lies on shard b. Among the 128 queries of one shard no block is named more than 2 times, and in some shards some block is named exactly 2 times.
All inputs are finite; a program needn't handle non-finite values.
Results may differ from a plain program's by a relative error of at most 0.0038.
Values may be sent and summed in bfloat16 or wider, within the bound.
No kernel may reach another device: no remote copies, remote signals or barrier semaphores. Data moves between devices by JAX's collectives and lax.ppermute only.
A program may use at most 128 MiB of HBM per device.

v0:
```python
import jax
import jax.numpy as jnp
from jax import lax
from jax.sharding import PartitionSpec as P

BLOCK = 128


SCORE_SCALE = 80.0
GRADIENT_SCALE = 2560.0
EPSILON = 1e-06
LAST_BOTH = (((1,), (1,)), ((), ()))
FIRST_BOTH = (((0,), (0,)), ((), ()))


def normalized(projected):
    inverse = lax.rsqrt(jnp.sum(projected * projected, axis=1, keepdims=True) + EPSILON)
    return (inverse, (projected * inverse).astype(jnp.bfloat16))


def row_backward(projected, inverse, grad_embedded):
    radial = jnp.sum(projected * grad_embedded, axis=1, keepdims=True)
    return (inverse * grad_embedded - projected * (inverse * inverse * inverse) * radial).astype(
        jnp.bfloat16
    )


def on_device(query_states, passage_states, head_weight, positives, negatives):
    query_count = query_states.shape[0]
    hard_count = negatives.shape[1]
    states = jnp.concatenate([query_states, passage_states], axis=0)
    full_weight = lax.all_gather(head_weight, "dp", axis=0, tiled=True)
    partial_proj = lax.dot_general(
        states, full_weight, LAST_BOTH, preferred_element_type=jnp.float32
    )
    projected = lax.psum(partial_proj, "mp")
    inverse, embedded = normalized(projected)
    query_embedded = embedded[:query_count]
    passage_embedded = embedded[query_count:]
    embed_width = embedded.shape[1]
    shards = lax.axis_size("dp")
    local_blocks = passage_embedded.shape[0] // BLOCK
    block_total = local_blocks * shards
    capacity = max(2, 2 * query_count * hard_count // block_total)
    pair_block = negatives.reshape(-1)
    pair_order = jnp.arange(pair_block.shape[0], dtype=jnp.int32)
    earlier = (pair_block[:, None] == pair_block[None, :]) & (
        pair_order[None, :] < pair_order[:, None]
    )
    slot_rank = jnp.sum(earlier.astype(jnp.int32), axis=1)
    slot_index = pair_block * capacity + slot_rank
    pair_queries = jnp.repeat(query_embedded, hard_count, axis=0)
    outgoing = (
        jnp.zeros((block_total * capacity, embed_width), jnp.bfloat16)
        .at[slot_index]
        .set(pair_queries)
    )
    outgoing = outgoing.reshape(shards, local_blocks, capacity, embed_width)
    passage_blocks = passage_embedded.reshape(local_blocks, BLOCK, embed_width)
    arrived = lax.all_to_all(outgoing, "dp", split_axis=0, concat_axis=0, tiled=True)
    scores = jnp.einsum(
        "sbie,bce->sbic", arrived, passage_blocks, preferred_element_type=jnp.float32
    )
    pair_exp = jnp.exp(SCORE_SCALE * scores)
    part_totals = jnp.sum(pair_exp, axis=3)
    part_sums = jnp.einsum(
        "sbic,bce->sbie",
        pair_exp.astype(jnp.bfloat16),
        passage_blocks,
        preferred_element_type=jnp.float32,
    )
    back_totals = lax.all_to_all(part_totals, "dp", split_axis=0, concat_axis=0, tiled=True)
    back_sums = lax.all_to_all(part_sums, "dp", split_axis=0, concat_axis=0, tiled=True)
    back_totals, back_sums, hard_exp, arrived = (back_totals, back_sums, pair_exp, arrived)
    hard_totals = back_totals.reshape(-1)[slot_index].reshape(query_count, hard_count).sum(axis=1)
    hard_sums = (
        back_sums.reshape(-1, embed_width)[slot_index]
        .reshape(query_count, hard_count, embed_width)
        .sum(axis=1)
    )
    local_exp = jnp.exp(
        SCORE_SCALE
        * lax.dot_general(
            query_embedded, passage_embedded, LAST_BOTH, preferred_element_type=jnp.float32
        )
    )
    totals = jnp.sum(local_exp, axis=1) + hard_totals
    positive_mask = (
        positives[:, None] == jnp.arange(passage_embedded.shape[0], dtype=jnp.int32)[None, :]
    ).astype(jnp.float32)
    local_coef = (GRADIENT_SCALE * (local_exp / totals[:, None] - positive_mask)).astype(
        jnp.bfloat16
    )
    query_grad = (
        jnp.dot(local_coef, passage_embedded, preferred_element_type=jnp.float32)
        + (GRADIENT_SCALE / totals)[:, None] * hard_sums
    )
    passage_grad = lax.dot_general(
        local_coef, query_embedded, FIRST_BOTH, preferred_element_type=jnp.float32
    )
    slot_totals = (
        jnp.ones((block_total * capacity,), jnp.float32)
        .at[slot_index]
        .set(jnp.repeat(totals, hard_count))
    )
    arrived_totals = lax.all_to_all(
        slot_totals.reshape(shards, local_blocks, capacity),
        "dp",
        split_axis=0,
        concat_axis=0,
        tiled=True,
    )
    hard_coef = (GRADIENT_SCALE * hard_exp / arrived_totals[..., None]).astype(jnp.bfloat16)
    remote_grad = jnp.einsum(
        "sbic,sbie->bce", hard_coef, arrived, preferred_element_type=jnp.float32
    )
    passage_grad = passage_grad + remote_grad.reshape(-1, embed_width)
    grad_embedded = jnp.concatenate([query_grad, passage_grad], axis=0)
    proj_grad = row_backward(projected, inverse, grad_embedded)
    state_grad = jnp.dot(proj_grad, full_weight, preferred_element_type=jnp.float32)
    return (state_grad[:query_count], state_grad[query_count:])


def solution(mesh):
    in_specs = (P("dp", "mp"), P("dp", "mp"), P("dp", "mp"), P("dp"), P("dp", None))
    out_specs = (P("dp", "mp"), P("dp", "mp"))
    return jax.shard_map(
        on_device, mesh=mesh, in_specs=in_specs, out_specs=out_specs, check_vma=False
    )
```

profile of v0, /device:TPU:1, one launch (start us, length us, event | category | flops | bytes accessed | tf_op | source)
XLA Modules:
  0.0 478.2 jit_solution(8180590341132450855)
XLA Ops:
  7.9 97.3 %all-gather.2.cloned.1.call-done = bf16[4096,1024]{1,0:T(8,128)(2,1)} async-done(((bf16[32,1024]{1,0:T(8,128)(2,1)}), bf16[4096,1024]{1,0:T(8,128)(2,1)}) %all-gather.2.cloned.1.call-update) | async-done | bytes 8388624 | tf_op jit(solution)/shard_map/all_gather | solution.py:32
  105.2 7.9 %fusion.30 = f32[256,4096]{1,0:T(8,128)} fusion(bf16[4096,1024]{1,0:T(8,128)(2,1)} %all-gather.2.cloned.1.call-done, bf16[128,1024]{1,0:T(8,128)(2,1)} %param.6, bf16[128,1024]{1,0:T(8,128)(2,1)} %param.5), kind=kOutput, calls=%fused_computation.38 | convolution fusion | flops 2148532224 | bytes 13107200 | tf_op jit(solution)/shard_map/dot_general | solution.py:33
  114.0 99.1 %all-reduce.2.cloned.1.call-done = f32[256,4096]{1,0:T(8,128)} async-done(((f32[256,4096]{1,0:T(8,128)}), f32[256,4096]{1,0:T(8,128)}) %all-reduce.2.cloned.1.call-update) | async-done | bytes 4194320 | tf_op jit(solution)/shard_map/psum | solution.py:36
  213.1 2.7 multiply_reduce_fusion.1
  217.0 3.6 scatter_custom_fusion
  220.6 4.4 reshape.74
  225.1 14.7 %all-to-all-start = ((bf16[128,1,2,4096]{3,2,1,0:T(2,128)(2,1)}), bf16[128,1,2,4096]{3,2,1,0:T(2,128)(2,1)}, u32[]{:S(2)}, u32[]{:S(2)}) async-start(bf16[128,1,2,4096]{3,2,1,0:T(2,128)(2,1)} %bitcast.52), calls=%async_computation | async-start | bytes 4194304 | tf_op jit(solution)/shard_map/all_to_all | solution.py:60
  239.8 50.9 %all-to-all-done = bf16[128,1,2,4096]{3,2,1,0:T(2,128)(2,1)} async-done(((bf16[128,1,2,4096]{3,2,1,0:T(2,128)(2,1)}), bf16[128,1,2,4096]{3,2,1,0:T(2,128)(2,1)}, u32[]{:S(2)}, u32[]{:S(2)}) %all-to-all-start) | async-done | bytes 2097184 | tf_op jit(solution)/shard_map/all_to_all | solution.py:60
  290.7 4.0 fusion.47
  295.5 8.8 %all-to-all-start.1 = ((f32[128,1,2]{2,1,0:T(1,128)}), f32[128,1,2]{2,1,0:T(1,128)S(1)}, u32[]{:S(2)}, u32[]{:S(2)}) async-start(f32[128,1,2]{2,1,0:T(1,128)} %copy.24), calls=%async_computation.1 | async-start | bytes 131072 | tf_op jit(solution)/shard_map/all_to_all | solution.py:72
  304.8 10.9 %all-to-all-done.1 = f32[128,1,2]{2,1,0:T(1,128)S(1)} async-done(((f32[128,1,2]{2,1,0:T(1,128)}), f32[128,1,2]{2,1,0:T(1,128)S(1)}, u32[]{:S(2)}, u32[]{:S(2)}) %all-to-all-start.1) | async-done | bytes 1056 | tf_op jit(solution)/shard_map/all_to_all | solution.py:72
  320.3 5.7 %all-to-all-start.3 = ((f32[128,1,2]{2,1,0:T(1,128)}), f32[128,1,2]{2,1,0:T(1,128)S(1)}, u32[]{:S(2)}, u32[]{:S(2)}) async-start(f32[128,1,2]{2,1,0:T(1,128)} %bitcast.14), calls=%async_computation.3 | async-start | bytes 131072 | tf_op jit(solution)/shard_map/all_to_all | solution.py:106
  326.0 2.7 convolution_bitcast_fusion
  328.7 7.3 %copy.27 = f32[128,1,2,4096]{3,2,1,0:T(2,128)} copy(f32[128,1,2,4096]{0,3,2,1:T(8,128)} %convolution_bitcast_fusion) | data formatting | bytes 8388608 | tf_op jit(solution)/shard_map/sbic,bce->sbie/transpose | solution.py:66
  336.0 1.5 all-to-all-done.3
  337.5 12.9 %all-to-all-start.2 = ((f32[128,1,2,4096]{3,2,1,0:T(2,128)}), f32[128,1,2,4096]{3,2,1,0:T(2,128)}, u32[]{:S(2)}, u32[]{:S(2)}) async-start(f32[128,1,2,4096]{3,2,1,0:T(2,128)} %copy.27), calls=%async_computation.2 | async-start | bytes 8388608 | tf_op jit(solution)/shard_map/all_to_all | solution.py:73
  350.4 4.1 convolution_bitcast_fusion.1
  354.6 1.8 convolution_add_fusion
  356.3 91.0 %all-to-all-done.2 = f32[128,1,2,4096]{3,2,1,0:T(2,128)} async-done(((f32[128,1,2,4096]{3,2,1,0:T(2,128)}), f32[128,1,2,4096]{3,2,1,0:T(2,128)}, u32[]{:S(2)}, u32[]{:S(2)}) %all-to-all-start.2) | async-done | bytes 4194336 | tf_op jit(solution)/shard_map/all_to_all | solution.py:73
  447.4 6.1 %reshape.78 = f32[256,4096]{1,0:T(8,128)} reshape(f32[128,1,2,4096]{3,2,1,0:T(2,128)} %all-to-all-done.2) | data formatting | bytes 8388608 | tf_op jit(solution)/shard_map/reshape | solution.py:77
  453.4 5.7 %gather_fusion.1 = f32[128,4096]{1,0:T(8,128)} fusion(f32[256,4096]{1,0:T(8,128)} %reshape.78, s32[1024]{0:T(1024)S(1)} %pad_clamp_fusion), kind=kCustom, calls=%fused_computation.1 | custom fusion | bytes 4194816 | tf_op jit(solution)/shard_map/gather | solution.py:77
  459.1 2.2 convolution_add_fusion.1
  461.9 2.3 multiply_reduce_fusion
  464.2 6.1 %fusion = f32[256,1024]{1,0:T(8,128)S(1)} fusion(bf16[4096,1024]{1,0:T(8,128)(2,1)} %all-gather.2.cloned.1.call-done, f32[256,4096]{1,0:T(8,128)S(1)} %copy-done.1, f32[128,4096]{1,0:T(8,128)S(1)} %copy-done.2, f32[128,4096]{1,0:T(8,128)S(1)} %convolution_add_fusion.1, f32[256]{0:T(256)S(1)} %multiply_reduce_fusion, f32[256]{0:T(256)S(1)} %get-tuple-element.6, ...), kind=kOutput, calls=%fused_computation.13 | convolution fusion | flops 2153775104 | bytes 17828864 | tf_op jit(solution)/shard_map/dot_general | solution.py:120
  (30 shorter events, 10.2 us)
Async XLA Ops:
  7.2 98.0 %all-gather.2.cloned.1.call-start = ((), (), s32[]{:S(2)}) async-start(), calls=%async_computation.4 | async-start | bytes 8454144 | tf_op jit(solution)/shard_map/all_gather | solution.py:32
  7.9 205.2 %all-reduce.2.cloned.1.call-start = ((), (), s32[]{:S(2)}) async-start(), calls=%async_computation.5 | async-start | bytes 8388608 | tf_op jit(solution)/shard_map/psum | solution.py:36
  113.1 0.7 copy-start.4
  213.1 3.4 copy-start
  225.1 65.7 %all-to-all-start = ((bf16[128,1,2,4096]{3,2,1,0:T(2,128)(2,1)}), bf16[128,1,2,4096]{3,2,1,0:T(2,128)(2,1)}, u32[]{:S(2)}, u32[]{:S(2)}) async-start(bf16[128,1,2,4096]{3,2,1,0:T(2,128)(2,1)} %bitcast.52), calls=%async_computation | async-start | bytes 4194304 | tf_op jit(solution)/shard_map/all_to_all | solution.py:60
  295.5 20.2 %all-to-all-start.1 = ((f32[128,1,2]{2,1,0:T(1,128)}), f32[128,1,2]{2,1,0:T(1,128)S(1)}, u32[]{:S(2)}, u32[]{:S(2)}) async-start(f32[128,1,2]{2,1,0:T(1,128)} %copy.24), calls=%async_computation.1 | async-start | bytes 131072 | tf_op jit(solution)/shard_map/all_to_all | solution.py:72
  320.3 17.2 %all-to-all-start.3 = ((f32[128,1,2]{2,1,0:T(1,128)}), f32[128,1,2]{2,1,0:T(1,128)S(1)}, u32[]{:S(2)}, u32[]{:S(2)}) async-start(f32[128,1,2]{2,1,0:T(1,128)} %bitcast.14), calls=%async_computation.3 | async-start | bytes 131072 | tf_op jit(solution)/shard_map/all_to_all | solution.py:106
  337.5 109.9 %all-to-all-start.2 = ((f32[128,1,2,4096]{3,2,1,0:T(2,128)}), f32[128,1,2,4096]{3,2,1,0:T(2,128)}, u32[]{:S(2)}, u32[]{:S(2)}) async-start(f32[128,1,2,4096]{3,2,1,0:T(2,128)} %copy.27), calls=%async_computation.2 | async-start | bytes 8388608 | tf_op jit(solution)/shard_map/all_to_all | solution.py:73
  350.4 4.1 copy-start.3
  459.1 2.8 copy-start.1
  461.9 2.3 copy-start.2
Sparse Core Ops, SparseCore 0:
  11.1 94.0 all-gather.1
  113.3 99.7 all-reduce.1
where the time goes:
time: 487 us; the launch traced here: 478 us
  waiting for transfers between devices  351 us (72%)
  starting transfers between devices  42.3 us (9%)
  local copies, waits for them, and re-layouts  34.6 us (7%)
  matrix products  29.3 us (6%)
  between operations  14.2 us (3%)
  other arithmetic  6.46 us (1%)
    psum x1, waiting for transfers between devices, on_device(): projected = lax.psum(partial_proj, 'mp')  99.1 us
    all_gather x1, waiting for transfers between devices, on_device(): full_weight = lax.all_gather(head_weight, 'dp', axis=0, tiled=True)  97.3 us
    all_to_all x1, waiting for transfers between devices, on_device(): lax.all_to_all(part_sums, 'dp', split_axis=0, concat_axis=0, tiled=True)  91 us
    all_to_all x1, waiting for transfers between devices, on_device(): lax.all_to_all(outgoing, 'dp', split_axis=0, concat_axis=0, tiled=True)  50.9 us
    all_to_all x1, starting transfers between devices, on_device(): lax.all_to_all(outgoing, 'dp', split_axis=0, concat_axis=0, tiled=True)  14.7 us
    all_to_all x1, starting transfers between devices, on_device(): lax.all_to_all(part_sums, 'dp', split_axis=0, concat_axis=0, tiled=True)  12.9 us
    all_to_all x1, waiting for transfers between devices, on_device(): lax.all_to_all(part_totals, 'dp', split_axis=0, concat_axis=0, tiled=True)  10.9 us
  transfers between devices with their start and end apart: 6, of which 6 were waited for; matrix products, arithmetic and copies ran while one was open for 3% of the time, Pallas kernels for 0%

commit v1 on v0

v1 whole, which is shorter than its diff:
```python
import jax
import jax.numpy as jnp
from jax import lax
from jax.sharding import PartitionSpec as P

CAPACITY = 2
SCORE_SCALE = 80.0
GRADIENT_SCALE = 2560.0
EPSILON = 1e-06
LAST_BOTH = (((1,), (1,)), ((), ()))
FIRST_BOTH = (((0,), (0,)), ((), ()))
F32 = jnp.float32
BF16 = jnp.bfloat16


def dot(a, b, dims=(((1,), (0,)), ((), ()))):
    return lax.dot_general(a, b, dims, preferred_element_type=F32)


def swap(x, axis):
    return lax.all_to_all(x, axis, split_axis=0, concat_axis=0, tiled=True)


def from_all(x, axis):
    return swap(jnp.broadcast_to(x[None], (lax.axis_size(axis),) + x.shape), axis)


def sum_all(x, axis):
    return jnp.sum(from_all(x, axis), axis=0)


def on_device(query_states, passage_states, head_weight, positives, negatives):
    pairs, width = query_states.shape
    parts = lax.axis_size("mp")
    shards = lax.axis_size("dp")
    own_rows = head_weight.shape[0] // parts
    slots = shards * CAPACITY

    weight_rows = swap(head_weight.reshape(parts, own_rows, width), "mp")
    weight_rows = weight_rows.transpose(1, 0, 2).reshape(own_rows, parts * width)
    weight = lax.all_gather(weight_rows, "dp", axis=0, tiled=True)
    states = jnp.concatenate([query_states, passage_states], axis=0)
    states = from_all(states, "mp").transpose(1, 0, 2).reshape(2 * pairs, parts * width)

    block = negatives.reshape(-1)
    order = jnp.arange(pairs, dtype=jnp.int32)
    earlier = (block[:, None] == block[None, :]) & (order[None, :] < order[:, None])
    slot = block * CAPACITY + jnp.sum(earlier.astype(jnp.int32), axis=1)
    in_slot = jnp.arange(slots, dtype=jnp.int32)[:, None] == slot[None, :]
    to_slot = in_slot.astype(BF16)
    positive_mask = (positives[:, None] == order[None, :]).astype(F32)

    projected = dot(states, weight, LAST_BOTH)
    squares = lax.psum(jnp.sum(projected * projected, axis=1), "mp")
    inverse = lax.rsqrt(squares[:, None] + EPSILON)
    embedded = (projected * inverse).astype(BF16)
    query, passage = embedded[:pairs], embedded[pairs:]
    part = query.shape[1]

    outgoing = dot(to_slot, query).astype(BF16)
    arrived = swap(outgoing.reshape(shards, CAPACITY, part), "dp").reshape(slots, part)

    local_scores = sum_all(dot(query, passage, LAST_BOTH), "mp")
    local_exp = jnp.exp(SCORE_SCALE * local_scores)
    local_totals = jnp.sum(local_exp, axis=1)
    slot_totals = jnp.sum(jnp.where(in_slot, local_totals[None, :], 0.0), axis=1)
    slot_totals = swap(slot_totals.reshape(shards, 1, CAPACITY), "dp").reshape(slots)

    hard_scores = sum_all(dot(arrived, passage, LAST_BOTH), "mp")
    hard_exp = jnp.exp(SCORE_SCALE * hard_scores)
    hard_totals = jnp.sum(hard_exp, axis=1)
    scale = GRADIENT_SCALE / (slot_totals + hard_totals)
    rounded_exp = hard_exp.astype(BF16)
    hard_radial = scale * jnp.sum(rounded_exp.astype(F32) * hard_scores, axis=1)
    back = jnp.stack([hard_totals, hard_radial], axis=1).reshape(shards, 1, 2 * CAPACITY)
    back = swap(back, "dp").reshape(slots, 2)
    hard_sums = (scale[:, None] * dot(rounded_exp, passage)).astype(BF16)
    hard_sums = swap(hard_sums.reshape(shards, CAPACITY, part), "dp").reshape(slots, part)
    hard_coef = (hard_exp * scale[:, None]).astype(BF16)

    back = jnp.sum(jnp.where(in_slot[:, :, None], back[:, None, :], 0.0), axis=0)
    totals = local_totals + back[:, 0]
    local_coef = (
        GRADIENT_SCALE * (local_exp / totals[:, None] - positive_mask)
    ).astype(BF16)
    weighted_scores = local_coef.astype(F32) * local_scores

    def state_grad(rows, grad, radial):
        inv = inverse[rows]
        proj_grad = (inv * grad - projected[rows] * (inv * inv * radial[:, None])).astype(BF16)
        partial = dot(proj_grad, weight).astype(BF16)
        partial = partial.reshape(pairs, parts, width).transpose(1, 0, 2)
        return jnp.sum(swap(partial, "mp").astype(F32), axis=0)

    passage_grad = dot(local_coef, query, FIRST_BOTH) + dot(hard_coef, arrived, FIRST_BOTH)
    passage_radial = jnp.sum(weighted_scores, axis=0) + jnp.sum(
        hard_coef.astype(F32) * hard_scores, axis=0
    )
    passage_out = state_grad(slice(pairs, None), passage_grad, passage_radial)

    query_grad = dot(local_coef, passage) + dot(to_slot, hard_sums, FIRST_BOTH)
    query_radial = jnp.sum(weighted_scores, axis=1) + back[:, 1]
    query_out = state_grad(slice(0, pairs), query_grad, query_radial)
    return (query_out, passage_out)


def solution(mesh):
    in_specs = (P("dp", "mp"), P("dp", "mp"), P("dp", "mp"), P("dp"), P("dp", None))
    out_specs = (P("dp", "mp"), P("dp", "mp"))
    return jax.shard_map(
        on_device, mesh=mesh, in_specs=in_specs, out_specs=out_specs, check_vma=False
    )
```

time: 487 us -> 291 us (0.60); the launches traced: 478 us -> 290 us
  waiting for transfers between devices: 351 us -> 171 us
  local copies, waits for them, and re-layouts: 34.6 us -> 11.3 us
  blocking collectives: 0 us -> 17.8 us
  matrix products: 29.3 us -> 18 us
  starting transfers between devices: 42.3 us -> 50.4 us
    psum x1 -> x0, waiting for transfers between devices: 99.1 us -> none  [on_device(): projected = lax.psum(partial_proj, 'mp')]
    all_to_all x4 -> x9, waiting for transfers between devices: 154 us -> 105 us  [swap(): return lax.all_to_all(x, axis, split_axis=0, concat_axis=0, tiled=True)]
    all_gather x1, waiting for transfers between devices: 97.3 us -> 66.7 us  [on_device(): weight = lax.all_gather(weight_rows, 'dp', axis=0, tiled=True)]
    dot_general x8 -> x9, matrix products: 29.3 us -> 18 us  [dot(): return lax.dot_general(a, b, dims, preferred_element_type=F32)]
    all_to_all x0 -> x1, blocking collectives: none -> 9.44 us  [swap(): return lax.all_to_all(x, axis, split_axis=0, concat_axis=0, tiled=True)]
    psum x0 -> x1, blocking collectives: none -> 8.41 us  [on_device(): squares = lax.psum(jnp.sum(projected * projected, axis=1), 'mp')]
    all_to_all x4 -> x9, starting transfers between devices: 42.2 us -> 50.4 us  [swap(): return lax.all_to_all(x, axis, split_axis=0, concat_axis=0, tiled=True)]
    transpose x1 -> x0, local copies, waits for them, and re-layouts: 7.33 us -> none  [on_device(): jnp.einsum('sbic,bce->sbie', pair_exp.astype(jnp.bfloat16), passage_block...]
  transfers between devices with their start and end apart: 6 -> 10, of which waited for: 6 -> 10; matrix products, arithmetic and copies ran while one was open for 3% -> 9% of each run, Pallas kernels for 0% -> 0%
where the time goes in v1:
time: 291 us; the launch traced here: 290 us
  waiting for transfers between devices  171 us (59%)
  starting transfers between devices  50.4 us (17%)
  matrix products  18 us (6%)
  blocking collectives  17.8 us (6%)
  between operations  14.3 us (5%)
  local copies, waits for them, and re-layouts  11.3 us (4%)
  other arithmetic  7.05 us (2%)
    all_to_all x9, waiting for transfers between devices, swap(): return lax.all_to_all(x, axis, split_axis=0, concat_axis=0, tiled=True)  105 us
    all_gather x1, waiting for transfers between devices, on_device(): weight = lax.all_gather(weight_rows, 'dp', axis=0, tiled=True)  66.7 us
    all_to_all x9, starting transfers between devices, swap(): return lax.all_to_all(x, axis, split_axis=0, concat_axis=0, tiled=True)  50.4 us
    dot_general x9, matrix products, dot(): return lax.dot_general(a, b, dims, preferred_element_type=F32)  18 us
    all_to_all x1, blocking collectives, swap(): return lax.all_to_all(x, axis, split_axis=0, concat_axis=0, tiled=True)  9.44 us
    psum x1, blocking collectives, on_device(): squares = lax.psum(jnp.sum(projected * projected, axis=1), 'mp')  8.41 us
  transfers between devices with their start and end apart: 10, of which 10 were waited for; matrix products, arithmetic and copies ran while one was open for 9% of the time, Pallas kernels for 0%

profile of v1, /device:TPU:1, one launch (start us, length us, event | category | flops | bytes accessed | tf_op | source)
XLA Modules:
  0.0 290.4 jit_solution(3712016741296000466)
XLA Ops:
  7.2 9.4 %all_to_all.50 = bf16[4,8,1024]{2,1,0:T(8,128)(2,1)} all-to-all(bf16[4,8,1024]{2,1,0:T(8,128)(2,1)} %bitcast.56), channel_id=1, replica_groups=mesh['dp'=128,'mp'=4] {'mp'}, dimensions={0} | all-to-all | bytes 131072 | tf_op jit(solution)/shard_map/all_to_all | solution.py:21
  19.4 4.5 %all-to-all-start = ((bf16[4,256,1024]{1,2,0:T(8,128)(2,1)}), bf16[4,256,1024]{1,2,0:T(8,128)(2,1)}, u32[]{:S(2)}, u32[]{:S(2)}) async-start(bf16[4,256,1024]{1,2,0:T(8,128)(2,1)} %broadcast_in_dim.33), calls=%async_computation | async-start | bytes 4194304 | tf_op jit(solution)/shard_map/all_to_all | solution.py:21
  24.1 18.9 %all-to-all-done = bf16[4,256,1024]{1,2,0:T(8,128)(2,1)} async-done(((bf16[4,256,1024]{1,2,0:T(8,128)(2,1)}), bf16[4,256,1024]{1,2,0:T(8,128)(2,1)}, u32[]{:S(2)}, u32[]{:S(2)}) %all-to-all-start) | async-done | bytes 2097184 | tf_op jit(solution)/shard_map/all_to_all | solution.py:21
  43.0 66.7 %all-gather.2.cloned.1.call-done = bf16[1024,4096]{1,0:T(8,128)(2,1)} async-done(((bf16[8,4096]{1,0:T(8,128)(2,1)}), bf16[1024,4096]{1,0:T(8,128)(2,1)}) %all-gather.2.cloned.1.call-update) | async-done | bytes 8388624 | tf_op jit(solution)/shard_map/all_gather | solution.py:41
  109.6 6.5 %multiply_reduce_fusion = (f32[256]{0:T(256)S(1)}, f32[256,1024]{1,0:T(8,128)S(1)}) fusion(bf16[256,4096]{0,1:T(8,128)(2,1)} %bitcast.1, bf16[1024,4096]{1,0:T(8,128)(2,1)} %all-gather.2.cloned.1.call-done), kind=kOutput, calls=%fused_computation.18 | convolution fusion | flops 2148007680 | bytes 11535360 | tf_op jit(solution)/shard_map/dot_general | solution.py:17
  116.1 8.4 %psum.7 = f32[256]{0:T(256)S(1)} all-reduce(f32[256]{0:T(256)S(1)} %get-tuple-element.9), channel_id=1, replica_groups=mesh['dp'=128,'mp'=4] {'mp'}, use_global_device_ids=true, to_apply=%region_1.0 | all-reduce | flops 256 | bytes 2048 | tf_op jit(solution)/shard_map/psum | solution.py:54
  125.6 3.4 %all-to-all-start.2 = ((f32[4,128,128]{2,1,0:T(8,128)}), f32[4,128,128]{2,1,0:T(8,128)S(1)}, u32[]{:S(2)}, u32[]{:S(2)}) async-start(f32[4,128,128]{2,1,0:T(8,128)} %broadcast_in_dim.34), calls=%async_computation.2 | async-start | bytes 524288 | tf_op jit(solution)/shard_map/all_to_all | solution.py:21
  130.4 4.2 %all-to-all-done.2 = f32[4,128,128]{2,1,0:T(8,128)S(1)} async-done(((f32[4,128,128]{2,1,0:T(8,128)}), f32[4,128,128]{2,1,0:T(8,128)S(1)}, u32[]{:S(2)}, u32[]{:S(2)}) %all-to-all-start.2) | async-done | bytes 262176 | tf_op jit(solution)/shard_map/all_to_all | solution.py:21
  134.6 12.4 %all-to-all-start.3 = ((bf16[128,2,1024]{2,1,0:T(2,128)(2,1)}), bf16[128,2,1024]{2,1,0:T(2,128)(2,1)S(1)}, u32[]{:S(2)}, u32[]{:S(2)}) async-start(bf16[128,2,1024]{2,1,0:T(2,128)(2,1)} %reshape.128), calls=%async_computation.3 | async-start | bytes 1048576 | tf_op jit(solution)/shard_map/all_to_all | solution.py:21
  148.0 19.5 %all-to-all-done.3 = bf16[128,2,1024]{2,1,0:T(2,128)(2,1)S(1)} async-done(((bf16[128,2,1024]{2,1,0:T(2,128)(2,1)}), bf16[128,2,1024]{2,1,0:T(2,128)(2,1)S(1)}, u32[]{:S(2)}, u32[]{:S(2)}) %all-to-all-start.3) | async-done | bytes 524320 | tf_op jit(solution)/shard_map/all_to_all | solution.py:21
  167.6 5.4 %all-to-all-start.5 = ((f32[128,1,2]{2,1,0:T(1,128)}), f32[128,1,2]{2,1,0:T(1,128)S(1)}, u32[]{:S(2)}, u32[]{:S(2)}) async-start(f32[128,1,2]{2,1,0:T(1,128)} %bitcast.8), calls=%async_computation.5 | async-start | bytes 131072 | tf_op jit(solution)/shard_map/all_to_all | solution.py:21
  173.5 10.9 %all-to-all-done.5 = f32[128,1,2]{2,1,0:T(1,128)S(1)} async-done(((f32[128,1,2]{2,1,0:T(1,128)}), f32[128,1,2]{2,1,0:T(1,128)S(1)}, u32[]{:S(2)}, u32[]{:S(2)}) %all-to-all-start.5) | async-done | bytes 1056 | tf_op jit(solution)/shard_map/all_to_all | solution.py:21
  185.2 3.5 %all-to-all-start.4 = ((f32[4,256,128]{2,1,0:T(8,128)}), f32[4,256,128]{2,1,0:T(8,128)S(1)}, u32[]{:S(2)}, u32[]{:S(2)}) async-start(f32[4,256,128]{2,1,0:T(8,128)} %broadcast_in_dim.36), calls=%async_computation.4 | async-start | bytes 1048576 | tf_op jit(solution)/shard_map/all_to_all | solution.py:21
  190.2 7.4 %all-to-all-done.4 = f32[4,256,128]{2,1,0:T(8,128)S(1)} async-done(((f32[4,256,128]{2,1,0:T(8,128)}), f32[4,256,128]{2,1,0:T(8,128)S(1)}, u32[]{:S(2)}, u32[]{:S(2)}) %all-to-all-start.4) | async-done | bytes 524320 | tf_op jit(solution)/shard_map/all_to_all | solution.py:21
  199.2 6.6 %all-to-all-start.6 = ((f32[128,1,4]{2,1,0:T(1,128)}), f32[128,1,4]{2,1,0:T(1,128)S(1)}, u32[]{:S(2)}, u32[]{:S(2)}) async-start(f32[128,1,4]{2,1,0:T(1,128)} %bitcast.10), calls=%async_computation.6 | async-start | bytes 131072 | tf_op jit(solution)/shard_map/all_to_all | solution.py:21
  207.1 10.2 %all-to-all-done.6 = f32[128,1,4]{2,1,0:T(1,128)S(1)} async-done(((f32[128,1,4]{2,1,0:T(1,128)}), f32[128,1,4]{2,1,0:T(1,128)S(1)}, u32[]{:S(2)}, u32[]{:S(2)}) %all-to-all-start.6) | async-done | bytes 2080 | tf_op jit(solution)/shard_map/all_to_all | solution.py:21
  217.3 6.8 %all-to-all-start.7 = ((bf16[128,2,1024]{2,1,0:T(2,128)(2,1)}), bf16[128,2,1024]{2,1,0:T(2,128)(2,1)}, u32[]{:S(2)}, u32[]{:S(2)}) async-start(bf16[128,2,1024]{2,1,0:T(2,128)(2,1)} %reshape.134), calls=%async_computation.7 | async-start | bytes 1048576 | tf_op jit(solution)/shard_map/all_to_all | solution.py:21
  225.4 4.9 %convolution_convert_fusion = bf16[128,4096]{1,0:T(8,128)(2,1)S(1)} fusion(bf16[1024,4096]{1,0:T(8,128)(2,1)} %all-gather.2.cloned.1.call-done, f32[128,1024]{1,0:T(8,128)S(1)} %fusion.26, f32[256,1024]{1,0:T(8,128)S(1)} %get-tuple-element.10, f32[128]{0:T(128)S(1)} %get-tuple-element.7, f32[128]{0:T(128)S(1)} %get-tuple-element.6, ...), kind=kOutput, calls=%fused_computation | convolution fusion | flops 1108590592 | bytes 10815488 | tf_op jit(solution)/shard_map/dot_general | solution.py:17
  231.4 13.0 %all-to-all-done.7 = bf16[128,2,1024]{2,1,0:T(2,128)(2,1)} async-done(((bf16[128,2,1024]{2,1,0:T(2,128)(2,1)}), bf16[128,2,1024]{2,1,0:T(2,128)(2,1)}, u32[]{:S(2)}, u32[]{:S(2)}) %all-to-all-start.7) | async-done | bytes 524320 | tf_op jit(solution)/shard_map/all_to_all | solution.py:21
  244.4 4.3 %all-to-all-start.9 = ((bf16[4,128,1024]{2,1,0:T(8,128)(2,1)}), bf16[4,128,1024]{2,1,0:T(8,128)(2,1)}, u32[]{:S(2)}, u32[]{:S(2)}) async-start(bf16[4,128,1024]{2,1,0:T(8,128)(2,1)} %bitcast.53), calls=%async_computation.9 | async-start | bytes 2097152 | tf_op jit(solution)/shard_map/all_to_all | solution.py:21
  250.2 4.9 %convolution_convert_fusion.1 = bf16[128,4096]{1,0:T(8,128)(2,1)S(1)} fusion(bf16[1024,4096]{1,0:T(8,128)(2,1)} %all-gather.2.cloned.1.call-done, f32[128,1024]{1,0:T(8,128)S(1)} %fusion.22, f32[256,1024]{1,0:T(8,128)S(1)} %get-tuple-element.10, f32[128]{0:T(128)S(1)} %fusion.37, f32[128]{0:T(128)S(1)} %get-tuple-element.8, ...), kind=kOutput, calls=%fused_computation.1 | convolution fusion | flops 1108590592 | bytes 10815488 | tf_op jit(solution)/shard_map/dot_general | solution.py:17
  256.2 8.2 %all-to-all-done.9 = bf16[4,128,1024]{2,1,0:T(8,128)(2,1)} async-done(((bf16[4,128,1024]{2,1,0:T(8,128)(2,1)}), bf16[4,128,1024]{2,1,0:T(8,128)(2,1)}, u32[]{:S(2)}, u32[]{:S(2)}) %all-to-all-start.9) | async-done | bytes 1048608 | tf_op jit(solution)/shard_map/all_to_all | solution.py:21
  264.3 3.5 %all-to-all-start.8 = ((bf16[4,128,1024]{2,1,0:T(8,128)(2,1)}), bf16[4,128,1024]{2,1,0:T(8,128)(2,1)S(1)}, u32[]{:S(2)}, u32[]{:S(2)}) async-start(bf16[4,128,1024]{2,1,0:T(8,128)(2,1)} %bitcast.50), calls=%async_computation.8 | async-start | bytes 2097152 | tf_op jit(solution)/shard_map/all_to_all | solution.py:21
  270.1 12.5 %all-to-all-done.8 = bf16[4,128,1024]{2,1,0:T(8,128)(2,1)S(1)} async-done(((bf16[4,128,1024]{2,1,0:T(8,128)(2,1)}), bf16[4,128,1024]{2,1,0:T(8,128)(2,1)S(1)}, u32[]{:S(2)}, u32[]{:S(2)}) %all-to-all-start.8) | async-done | bytes 1048608 | tf_op jit(solution)/shard_map/all_to_all | solution.py:21
  (54 shorter events, 20.1 us)
Async XLA Ops:
  7.2 16.7 %copy-start.1 = (s32[128,1]{0,1:T(1,128)S(1)}, s32[128,1]{0,1:T(1,128)}, u32[]{:S(2)}) copy-start(s32[128,1]{0,1:T(1,128)} %param.9) | copy-start | bytes 1540
  7.2 102.5 %all-gather.2.cloned.1.call-start = ((), (), s32[]{:S(2)}) async-start(), calls=%async_computation.10 | async-start | bytes 8454144 | tf_op jit(solution)/shard_map/all_gather | solution.py:41
  19.4 23.6 %all-to-all-start = ((bf16[4,256,1024]{1,2,0:T(8,128)(2,1)}), bf16[4,256,1024]{1,2,0:T(8,128)(2,1)}, u32[]{:S(2)}, u32[]{:S(2)}) async-start(bf16[4,256,1024]{1,2,0:T(8,128)(2,1)} %broadcast_in_dim.33), calls=%async_computation | async-start | bytes 4194304 | tf_op jit(solution)/shard_map/all_to_all | solution.py:21
  116.1 109.0 %copy-start = (s32[128]{0:T(128)S(1)}, s32[128]{0:T(128)}, u32[]{:S(2)}) copy-start(s32[128]{0:T(128)} %param.8) | copy-start | bytes 1540
  125.6 8.9 %all-to-all-start.2 = ((f32[4,128,128]{2,1,0:T(8,128)}), f32[4,128,128]{2,1,0:T(8,128)S(1)}, u32[]{:S(2)}, u32[]{:S(2)}) async-start(f32[4,128,128]{2,1,0:T(8,128)} %broadcast_in_dim.34), calls=%async_computation.2 | async-start | bytes 524288 | tf_op jit(solution)/shard_map/all_to_all | solution.py:21
  134.6 33.0 %all-to-all-start.3 = ((bf16[128,2,1024]{2,1,0:T(2,128)(2,1)}), bf16[128,2,1024]{2,1,0:T(2,128)(2,1)S(1)}, u32[]{:S(2)}, u32[]{:S(2)}) async-start(bf16[128,2,1024]{2,1,0:T(2,128)(2,1)} %reshape.128), calls=%async_computation.3 | async-start | bytes 1048576 | tf_op jit(solution)/shard_map/all_to_all | solution.py:21
  167.6 16.8 %all-to-all-start.5 = ((f32[128,1,2]{2,1,0:T(1,128)}), f32[128,1,2]{2,1,0:T(1,128)S(1)}, u32[]{:S(2)}, u32[]{:S(2)}) async-start(f32[128,1,2]{2,1,0:T(1,128)} %bitcast.8), calls=%async_computation.5 | async-start | bytes 131072 | tf_op jit(solution)/shard_map/all_to_all | solution.py:21
  185.2 12.4 %all-to-all-start.4 = ((f32[4,256,128]{2,1,0:T(8,128)}), f32[4,256,128]{2,1,0:T(8,128)S(1)}, u32[]{:S(2)}, u32[]{:S(2)}) async-start(f32[4,256,128]{2,1,0:T(8,128)} %broadcast_in_dim.36), calls=%async_computation.4 | async-start | bytes 1048576 | tf_op jit(solution)/shard_map/all_to_all | solution.py:21
  199.2 18.1 %all-to-all-start.6 = ((f32[128,1,4]{2,1,0:T(1,128)}), f32[128,1,4]{2,1,0:T(1,128)S(1)}, u32[]{:S(2)}, u32[]{:S(2)}) async-start(f32[128,1,4]{2,1,0:T(1,128)} %bitcast.10), calls=%async_computation.6 | async-start | bytes 131072 | tf_op jit(solution)/shard_map/all_to_all | solution.py:21
  217.3 27.1 %all-to-all-start.7 = ((bf16[128,2,1024]{2,1,0:T(2,128)(2,1)}), bf16[128,2,1024]{2,1,0:T(2,128)(2,1)}, u32[]{:S(2)}, u32[]{:S(2)}) async-start(bf16[128,2,1024]{2,1,0:T(2,128)(2,1)} %reshape.134), calls=%async_computation.7 | async-start | bytes 1048576 | tf_op jit(solution)/shard_map/all_to_all | solution.py:21
  244.4 19.9 %all-to-all-start.9 = ((bf16[4,128,1024]{2,1,0:T(8,128)(2,1)}), bf16[4,128,1024]{2,1,0:T(8,128)(2,1)}, u32[]{:S(2)}, u32[]{:S(2)}) async-start(bf16[4,128,1024]{2,1,0:T(8,128)(2,1)} %bitcast.53), calls=%async_computation.9 | async-start | bytes 2097152 | tf_op jit(solution)/shard_map/all_to_all | solution.py:21
  264.3 18.2 %all-to-all-start.8 = ((bf16[4,128,1024]{2,1,0:T(8,128)(2,1)}), bf16[4,128,1024]{2,1,0:T(8,128)(2,1)S(1)}, u32[]{:S(2)}, u32[]{:S(2)}) async-start(bf16[4,128,1024]{2,1,0:T(8,128)(2,1)} %bitcast.50), calls=%async_computation.8 | async-start | bytes 2097152 | tf_op jit(solution)/shard_map/all_to_all | solution.py:21
Sparse Core Ops, SparseCore 0:
  16.8 92.7 all-gather.1

commit v2 on v1

v2 whole, which is shorter than its diff:
```python
import math

import jax
import jax.numpy as jnp
from jax import lax
from jax.sharding import PartitionSpec as P

CAPACITY = 2
CORES = 2
EXTRA = 128
SCORE_SCALE = 80.0
GRADIENT_SCALE = 2560.0
EPSILON = 1e-06
LAST_BOTH = (((1,), (1,)), ((), ()))
FIRST_BOTH = (((0,), (0,)), ((), ()))
F32 = jnp.float32
BF16 = jnp.bfloat16


def dot(a, b, dims=(((1,), (0,)), ((), ()))):
    return lax.dot_general(a, b, dims, preferred_element_type=F32)


def swap(x, axis, groups=None):
    return lax.all_to_all(
        x, axis, split_axis=0, concat_axis=0, tiled=True, axis_index_groups=groups
    )


def from_all(x, axis):
    return swap(jnp.broadcast_to(x[None], (lax.axis_size(axis),) + x.shape), axis)


def sum_all(x, axis):
    return jnp.sum(from_all(x, axis), axis=0)


def parts_of(x, count):
    out = []
    for _ in range(count):
        part = lax.reduce_precision(x, 8, 7)
        out.append(part.astype(BF16))
        x = x - part
    return out


def columns(parts):
    stacked = jnp.stack(parts, axis=1)
    return jnp.pad(stacked, ((0, 0), (0, EXTRA - len(parts))))


def lines(shards, parts):
    side = math.isqrt(shards // CORES)

    def shard(z, y, core):
        return (z * side + y) * CORES + core

    first = [
        [shard(z, y, 0) * parts + m for m in range(parts) for y in range(side)]
        for z in range(side)
    ] + [
        [shard(z, y, 1) * parts + m for m in range(parts) for z in range(side)]
        for y in range(side)
    ]
    second = [[shard(z, y, 0) for z in range(side)] for y in range(side)] + [
        [shard(z, y, 1) for y in range(side)] for z in range(side)
    ]
    other_core = [(d, d ^ 1) for d in range(shards)]
    return side, first, second, other_core


def on_device(query_states, passage_states, head_weight, positives, negatives):
    pairs, width = query_states.shape
    parts = lax.axis_size("mp")
    shards = lax.axis_size("dp")
    slots = shards * CAPACITY
    side, first, second, other_core = lines(shards, parts)
    rows = head_weight.shape[0] // parts
    core = lax.axis_index("dp") % CORES

    line = jnp.broadcast_to(
        head_weight.reshape(parts, 1, rows, width), (parts, side, rows, width)
    ).reshape(parts * side, rows, width)
    line = swap(line, ("dp", "mp"), first).reshape(parts, side, rows, width)
    line = line.transpose(1, 2, 0, 3).reshape(side * rows, parts * width)
    weight_own = lax.all_gather(line, "dp", axis=0, tiled=True, axis_index_groups=second)
    weight_other = lax.ppermute(weight_own, "dp", other_core)
    states = jnp.concatenate([query_states, passage_states], axis=0)
    states = from_all(states, "mp").transpose(1, 0, 2).reshape(2 * pairs, parts * width)

    block = negatives.reshape(-1)
    order = jnp.arange(pairs, dtype=jnp.int32)
    earlier = (block[:, None] == block[None, :]) & (order[None, :] < order[:, None])
    slot = block * CAPACITY + jnp.sum(earlier.astype(jnp.int32), axis=1)
    in_slot = jnp.arange(slots, dtype=jnp.int32)[:, None] == slot[None, :]
    to_slot = in_slot.astype(BF16)
    positive_mask = (positives[:, None] == order[None, :]).astype(F32)

    def in_order(own, other):
        return jnp.where(core == 0, own, other), jnp.where(core == 0, other, own)

    projected_own = dot(states, weight_own, LAST_BOTH)
    projected_other = dot(states, weight_other, LAST_BOTH)
    squares = jnp.sum(projected_own * projected_own, axis=1) + jnp.sum(
        projected_other * projected_other, axis=1
    )
    projected = jnp.concatenate(in_order(projected_own, projected_other), axis=1)
    squares = sum_all(squares.reshape(-1, math.gcd(128, 2 * pairs)), "mp").reshape(-1)
    inverse = lax.rsqrt(squares[:, None] + EPSILON)
    embedded = (projected * inverse).astype(BF16)
    query, passage = embedded[:pairs], embedded[pairs:]
    part = query.shape[1]

    local_scores = sum_all(dot(query, passage, LAST_BOTH), "mp")
    local_exp = jnp.exp(SCORE_SCALE * local_scores)
    local_totals = jnp.sum(local_exp, axis=1)

    def exchange(message):
        message = message.reshape(shards, CAPACITY, part + EXTRA)
        return swap(message, "dp").reshape(slots, part + EXTRA)

    outgoing = jnp.concatenate([query, columns(parts_of(local_totals, 3))], axis=1)
    arrived = exchange(dot(to_slot, outgoing).astype(BF16))
    slot_totals = jnp.sum(arrived[:, part : part + 3].astype(F32), axis=1)
    arrived = arrived[:, :part]

    hard_scores = sum_all(dot(arrived, passage, LAST_BOTH), "mp")
    hard_exp = jnp.exp(SCORE_SCALE * hard_scores)
    hard_totals = jnp.sum(hard_exp, axis=1)
    scale = GRADIENT_SCALE / (slot_totals + hard_totals)
    rounded_exp = hard_exp.astype(BF16)
    hard_radial = scale * jnp.sum(rounded_exp.astype(F32) * hard_scores, axis=1)
    hard_sums = (scale[:, None] * dot(rounded_exp, passage)).astype(BF16)
    back = columns(parts_of(hard_totals, 3) + parts_of(hard_radial, 3))
    back = exchange(jnp.concatenate([hard_sums, back], axis=1))
    back = dot(to_slot, back, FIRST_BOTH)
    hard_coef = (hard_exp * scale[:, None]).astype(BF16)

    totals = local_totals + jnp.sum(back[:, part : part + 3], axis=1)
    local_coef = (
        GRADIENT_SCALE * (local_exp / totals[:, None] - positive_mask)
    ).astype(BF16)
    weighted_scores = local_coef.astype(F32) * local_scores

    query_grad = dot(local_coef, passage) + back[:, :part]
    query_radial = jnp.sum(weighted_scores, axis=1) + jnp.sum(
        back[:, part + 3 : part + 6], axis=1
    )
    passage_grad = dot(local_coef, query, FIRST_BOTH) + dot(hard_coef, arrived, FIRST_BOTH)
    passage_radial = jnp.sum(weighted_scores, axis=0) + jnp.sum(
        hard_coef.astype(F32) * hard_scores, axis=0
    )
    grad = jnp.concatenate([query_grad, passage_grad], axis=0)
    radial = jnp.concatenate([query_radial, passage_radial], axis=0)[:, None]
    proj_grad = (inverse * grad - projected * (inverse * inverse * radial)).astype(BF16)
    grad_own, grad_other = in_order(proj_grad[:, : part // 2], proj_grad[:, part // 2 :])
    partial = (dot(grad_own, weight_own) + dot(grad_other, weight_other)).astype(BF16)
    partial = partial.reshape(2 * pairs, parts, width).transpose(1, 0, 2)
    state_grad = jnp.sum(swap(partial, "mp").astype(F32), axis=0)
    return (state_grad[:pairs], state_grad[pairs:])


def solution(mesh):
    in_specs = (P("dp", "mp"), P("dp", "mp"), P("dp", "mp"), P("dp"), P("dp", None))
    out_specs = (P("dp", "mp"), P("dp", "mp"))
    return jax.shard_map(
        on_device, mesh=mesh, in_specs=in_specs, out_specs=out_specs, check_vma=False
    )
```

time: 291 us -> 266 us (0.914)
  blocking collectives: 17.8 us -> 89.7 us
  waiting for transfers between devices: 171 us -> 107 us
  starting transfers between devices: 50.4 us -> 26.6 us
  other arithmetic: 7.05 us -> 3.12 us
  matrix products: 18 us -> 15 us
    all_to_all x1 -> x3, blocking collectives: 9.44 us -> 89.7 us  [swap(): lax.all_to_all(x, axis, split_axis=0, concat_axis=0, tiled=True, axis_ind...]
    all_to_all x9 -> x5, waiting for transfers between devices: 105 us -> 67 us  [swap(): lax.all_to_all(x, axis, split_axis=0, concat_axis=0, tiled=True, axis_ind...]
    all_to_all x9 -> x5, starting transfers between devices: 50.4 us -> 19.7 us  [swap(): lax.all_to_all(x, axis, split_axis=0, concat_axis=0, tiled=True, axis_ind...]
    all_gather x1, waiting for transfers between devices: 66.7 us -> 39.9 us  [on_device(): lax.all_gather(line, 'dp', axis=0, tiled=True, axis_index_groups=second)]
    psum x1 -> x0, blocking collectives: 8.41 us -> none  [on_device(): squares = lax.psum(jnp.sum(projected * projected, axis=1), 'mp')]
    ppermute x0 -> x1, starting transfers between devices: none -> 6.92 us  [on_device(): weight_other = lax.ppermute(weight_own, 'dp', other_core)]
    reshape x10 -> x5, local copies, waits for them, and re-layouts: 7.34 us -> 1.92 us  [the longest x2 1.31 us: exchange(): message = message.reshape(shards, CAPACITY, part + EXTRA)]
    dot_general x9 -> x12, matrix products: 18 us -> 15 us  [dot(): return lax.dot_general(a, b, dims, preferred_element_type=F32)]
  transfers between devices with their start and end apart: 10 -> 7, of which waited for: 10 -> 6; matrix products, arithmetic and copies ran while one was open for 9% -> 2% of each run, Pallas kernels for 0% -> 0%
where the time goes in v2:
time: 266 us
  waiting for transfers between devices  107 us (40%)
  blocking collectives  89.7 us (34%)
  starting transfers between devices  26.6 us (10%)
  matrix products  15 us (6%)
  between operations  14.4 us (5%)
  local copies, waits for them, and re-layouts  10.1 us (4%)
  other arithmetic  3.12 us (1%)
    all_to_all x3, blocking collectives, swap(): lax.all_to_all(x, axis, split_axis=0, concat_axis=0, tiled=True, axis_ind...  89.7 us
    all_to_all x5, waiting for transfers between devices, swap(): lax.all_to_all(x, axis, split_axis=0, concat_axis=0, tiled=True, axis_ind...  67 us
    all_gather x1, waiting for transfers between devices, on_device(): lax.all_gather(line, 'dp', axis=0, tiled=True, axis_index_groups=second)  39.9 us
    all_to_all x5, starting transfers between devices, swap(): lax.all_to_all(x, axis, split_axis=0, concat_axis=0, tiled=True, axis_ind...  19.7 us
    dot_general x12, matrix products, dot(): return lax.dot_general(a, b, dims, preferred_element_type=F32)  15 us
    ppermute x1, starting transfers between devices, on_device(): weight_other = lax.ppermute(weight_own, 'dp', other_core)  6.92 us
  transfers between devices with their start and end apart: 7, of which 6 were waited for; matrix products, arithmetic and copies ran while one was open for 2% of the time, Pallas kernels for 0%

profile of v2, /device:TPU:1, one launch (start us, length us, event | category | flops | bytes accessed | tf_op | source)
XLA Modules:
  0.0 265.8 jit_solution(18341859052336439000)
XLA Ops:
  8.2 24.9 %all_to_all.40 = bf16[32,8,1024]{2,1,0:T(8,128)(2,1)S(1)} all-to-all(bf16[32,8,1024]{2,1,0:T(8,128)(2,1)S(1)} %bitcast.51), channel_id=1, replica_groups={{0,8,16,24,32,40,48,56,1,9,17,25,33,41,49,57,2,10,18,26,34,42,50,58,3,1..., dimensions={0} | all-to-all | bytes 1048576 | tf_op jit(solution)/shard_map/all_to_all | solution.py:25
  33.5 1.0 copy.44
  34.5 39.9 %all-gather.2.cloned.1.call-done = bf16[512,4096]{1,0:T(8,128)(2,1)} async-done(((bf16[64,4096]{1,0:T(8,128)(2,1)}), bf16[512,4096]{1,0:T(8,128)(2,1)}) %all-gather.2.cloned.1.call-update) | async-done | bytes 4194320 | tf_op jit(solution)/shard_map/all_gather | solution.py:86
  74.4 6.9 %collective-permute-start = (bf16[512,4096]{1,0:T(8,128)(2,1)}, bf16[512,4096]{1,0:T(8,128)(2,1)}, u32[]{:S(2)}, u32[]{:S(2)}) collective-permute-start(bf16[512,4096]{1,0:T(8,128)(2,1)} %all-gather.2.cloned.1.call-done), channel_id=1, source_target_pairs={{0,4},{4,0},{8,12},{12,8},{16,20},{20,16},{24,28},{28,24},{32,36},... | collective-permute-start | bytes 12582920 | tf_op jit(solution)/shard_map/ppermute | solution.py:87
  81.6 1.5 broadcast_in_dim.12
  83.1 4.0 %all-to-all-start = ((bf16[4,256,1024]{1,2,0:T(8,128)(2,1)}), bf16[4,256,1024]{1,2,0:T(8,128)(2,1)S(1)}, u32[]{:S(2)}, u32[]{:S(2)}) async-start(bf16[4,256,1024]{1,2,0:T(8,128)(2,1)} %broadcast_in_dim.12), calls=%async_computation | async-start | bytes 4194304 | tf_op jit(solution)/shard_map/all_to_all | solution.py:25
  87.1 26.2 %all-to-all-done = bf16[4,256,1024]{1,2,0:T(8,128)(2,1)S(1)} async-done(((bf16[4,256,1024]{1,2,0:T(8,128)(2,1)}), bf16[4,256,1024]{1,2,0:T(8,128)(2,1)S(1)}, u32[]{:S(2)}, u32[]{:S(2)}) %all-to-all-start) | async-done | bytes 2097184 | tf_op jit(solution)/shard_map/all_to_all | solution.py:25
  113.3 3.5 %fusion.58 = f32[256,512]{1,0:T(8,128)S(1)} fusion(bf16[256,4096]{0,1:T(8,128)(2,1)S(1)} %bitcast.47, bf16[512,4096]{1,0:T(8,128)(2,1)} %all-gather.2.cloned.1.call-done), kind=kOutput, calls=%fused_computation.107 | convolution fusion | flops 1073741824 | bytes 6815744 | tf_op jit(solution)/shard_map/dot_general | solution.py:21
  116.8 3.6 %broadcast_select_fusion.1 = (f32[256,512]{1,0:T(8,128)S(1)}, f32[256,512]{1,0:T(8,128)S(1)}, f32[256]{0:T(256)S(1)}, f32[256]{0:T(256)S(1)}) fusion(f32[256,512]{1,0:T(8,128)S(1)} %fusion.58, pred[]{:T(512)S(6)} %eq.20, bf16[256,4096]{0,1:T(8,128)(2,1)S(1)} %bitcast.48, bf16[512,4096]{1,0:T(8,128)(2,1)} %collective-permute-done), kind=kOutput, calls=%fused_computation.37 | convolution fusion | flops 1074527744 | bytes 7866369 | tf_op jit(solution)/shard_map/dot_general | solution.py:21
  121.0 3.2 %all-to-all-start.2 = ((f32[4,2,128]{2,1,0:T(2,128)}), f32[4,2,128]{2,1,0:T(2,128)S(1)}, u32[]{:S(2)}, u32[]{:S(2)}) async-start(f32[4,2,128]{2,1,0:T(2,128)} %broadcast_in_dim.15), calls=%async_computation.2 | async-start | bytes 8192 | tf_op jit(solution)/shard_map/all_to_all | solution.py:25
  124.4 3.9 %all-to-all-done.2 = f32[4,2,128]{2,1,0:T(2,128)S(1)} async-done(((f32[4,2,128]{2,1,0:T(2,128)}), f32[4,2,128]{2,1,0:T(2,128)S(1)}, u32[]{:S(2)}, u32[]{:S(2)}) %all-to-all-start.2) | async-done | bytes 4128 | tf_op jit(solution)/shard_map/all_to_all | solution.py:25
  129.5 3.4 %all-to-all-start.3 = ((f32[4,128,128]{2,1,0:T(8,128)}), f32[4,128,128]{2,1,0:T(8,128)S(1)}, u32[]{:S(2)}, u32[]{:S(2)}) async-start(f32[4,128,128]{2,1,0:T(8,128)} %broadcast_in_dim.16), calls=%async_computation.3 | async-start | bytes 524288 | tf_op jit(solution)/shard_map/all_to_all | solution.py:25
  132.9 5.4 %all-to-all-done.3 = f32[4,128,128]{2,1,0:T(8,128)S(1)} async-done(((f32[4,128,128]{2,1,0:T(8,128)}), f32[4,128,128]{2,1,0:T(8,128)S(1)}, u32[]{:S(2)}, u32[]{:S(2)}) %all-to-all-start.3) | async-done | bytes 262176 | tf_op jit(solution)/shard_map/all_to_all | solution.py:25
  139.7 35.6 %all_to_all.41 = bf16[128,2,1152]{2,1,0:T(2,128)(2,1)S(1)} all-to-all(bf16[128,2,1152]{2,1,0:T(2,128)(2,1)S(1)} %reshape.247), channel_id=1, replica_groups=mesh['dp'=128,'mp'=4] {'dp'}, dimensions={0} | all-to-all | bytes 1179648 | tf_op jit(solution)/shard_map/all_to_all | solution.py:25
  176.7 3.5 %all-to-all-start.5 = ((f32[4,256,128]{2,1,0:T(8,128)}), f32[4,256,128]{2,1,0:T(8,128)S(1)}, u32[]{:S(2)}, u32[]{:S(2)}) async-start(f32[4,256,128]{2,1,0:T(8,128)} %broadcast_in_dim.17), calls=%async_computation.5 | async-start | bytes 1048576 | tf_op jit(solution)/shard_map/all_to_all | solution.py:25
  180.3 9.7 %all-to-all-done.5 = f32[4,256,128]{2,1,0:T(8,128)S(1)} async-done(((f32[4,256,128]{2,1,0:T(8,128)}), f32[4,256,128]{2,1,0:T(8,128)S(1)}, u32[]{:S(2)}, u32[]{:S(2)}) %all-to-all-start.5) | async-done | bytes 524320 | tf_op jit(solution)/shard_map/all_to_all | solution.py:25
  191.4 1.1 reshape.249
  192.5 5.6 %all-to-all-start.6 = ((bf16[128,2,1152]{2,1,0:T(2,128)(2,1)}), bf16[128,2,1152]{2,1,0:T(2,128)(2,1)S(1)}, u32[]{:S(2)}, u32[]{:S(2)}) async-start(bf16[128,2,1152]{2,1,0:T(2,128)(2,1)} %reshape.249), calls=%async_computation.6 | async-start | bytes 1179648 | tf_op jit(solution)/shard_map/all_to_all | solution.py:25
  198.4 21.7 %all-to-all-done.6 = bf16[128,2,1152]{2,1,0:T(2,128)(2,1)S(1)} async-done(((bf16[128,2,1152]{2,1,0:T(2,128)(2,1)}), bf16[128,2,1152]{2,1,0:T(2,128)(2,1)S(1)}, u32[]{:S(2)}, u32[]{:S(2)}) %all-to-all-start.6) | async-done | bytes 589856 | tf_op jit(solution)/shard_map/all_to_all | solution.py:25
  220.3 1.1 fusion.31
  223.4 1.3 fusion.17
  224.6 3.5 %fusion = bf16[256,4096]{1,0:T(8,128)(2,1)S(1)} fusion(f32[256,4096]{1,0:T(8,128)S(1)} %fusion.17, bf16[512,4096]{1,0:T(8,128)(2,1)} %collective-permute-done, pred[]{:T(512)S(6)} %eq.20, bf16[256,1024]{1,0:T(8,128)(2,1)S(1)} %fusion.4), kind=kOutput, calls=%fused_computation.1 | convolution fusion | flops 1075970048 | bytes 11010049 | tf_op jit(solution)/shard_map/dot_general | solution.py:21
  228.3 29.2 %all_to_all.42 = bf16[4,256,1024]{2,1,0:T(8,128)(2,1)S(1)} all-to-all(bf16[4,256,1024]{2,1,0:T(8,128)(2,1)S(1)} %bitcast.45), channel_id=1, replica_groups=mesh['dp'=128,'mp'=4] {'mp'}, dimensions={0} | all-to-all | bytes 4194304 | tf_op jit(solution)/shard_map/all_to_all | solution.py:25
  257.9 1.1 fusion.57
  (67 shorter events, 10.7 us)
Async XLA Ops:
  7.2 74.2 %copy-start.1 = (bf16[128,1024]{1,0:T(8,128)(2,1)S(1)}, bf16[128,1024]{1,0:T(8,128)(2,1)}, u32[]{:S(2)}) copy-start(bf16[128,1024]{1,0:T(8,128)(2,1)} %param.6) | copy-start | bytes 786436
  7.2 74.2 %copy-start.2 = (bf16[128,1024]{1,0:T(8,128)(2,1)S(1)}, bf16[128,1024]{1,0:T(8,128)(2,1)}, u32[]{:S(2)}) copy-start(bf16[128,1024]{1,0:T(8,128)(2,1)} %param.5) | copy-start | bytes 786436
  7.2 67.2 %all-gather.2.cloned.1.call-start = ((), (), s32[]{:S(2)}) async-start(), calls=%async_computation.8 | async-start | bytes 4718592 | tf_op jit(solution)/shard_map/all_gather | solution.py:86
  74.4 42.4 %collective-permute-start = (bf16[512,4096]{1,0:T(8,128)(2,1)}, bf16[512,4096]{1,0:T(8,128)(2,1)}, u32[]{:S(2)}, u32[]{:S(2)}) collective-permute-start(bf16[512,4096]{1,0:T(8,128)(2,1)} %all-gather.2.cloned.1.call-done), channel_id=1, source_target_pairs={{0,4},{4,0},{8,12},{12,8},{16,20},{20,16},{24,28},{28,24},{32,36},... | collective-permute-start | bytes 12582920 | tf_op jit(solution)/shard_map/ppermute | solution.py:87
  83.1 30.1 %all-to-all-start = ((bf16[4,256,1024]{1,2,0:T(8,128)(2,1)}), bf16[4,256,1024]{1,2,0:T(8,128)(2,1)S(1)}, u32[]{:S(2)}, u32[]{:S(2)}) async-start(bf16[4,256,1024]{1,2,0:T(8,128)(2,1)} %broadcast_in_dim.12), calls=%async_computation | async-start | bytes 4194304 | tf_op jit(solution)/shard_map/all_to_all | solution.py:25
  116.7 7.5 %copy-start.7 = (s32[128,1]{0,1:T(1,128)S(1)}, s32[128,1]{0,1:T(1,128)}, u32[]{:S(2)}) copy-start(s32[128,1]{0,1:T(1,128)} %param.9) | copy-start | bytes 1540
  121.0 7.4 %all-to-all-start.2 = ((f32[4,2,128]{2,1,0:T(2,128)}), f32[4,2,128]{2,1,0:T(2,128)S(1)}, u32[]{:S(2)}, u32[]{:S(2)}) async-start(f32[4,2,128]{2,1,0:T(2,128)} %broadcast_in_dim.15), calls=%async_computation.2 | async-start | bytes 8192 | tf_op jit(solution)/shard_map/all_to_all | solution.py:25
  129.5 8.9 %all-to-all-start.3 = ((f32[4,128,128]{2,1,0:T(8,128)}), f32[4,128,128]{2,1,0:T(8,128)S(1)}, u32[]{:S(2)}, u32[]{:S(2)}) async-start(f32[4,128,128]{2,1,0:T(8,128)} %broadcast_in_dim.16), calls=%async_computation.3 | async-start | bytes 524288 | tf_op jit(solution)/shard_map/all_to_all | solution.py:25
  132.9 6.3 %copy-start.5 = (s32[128]{0:T(128)}, s32[128]{0:T(128)S(1)}, u32[]{:S(2)}) copy-start(s32[128]{0:T(128)S(1)} %multiply_add_fusion) | copy-start | bytes 1540
  138.5 0.5 copy-start.4
  176.7 13.3 %all-to-all-start.5 = ((f32[4,256,128]{2,1,0:T(8,128)}), f32[4,256,128]{2,1,0:T(8,128)S(1)}, u32[]{:S(2)}, u32[]{:S(2)}) async-start(f32[4,256,128]{2,1,0:T(8,128)} %broadcast_in_dim.17), calls=%async_computation.5 | async-start | bytes 1048576 | tf_op jit(solution)/shard_map/all_to_all | solution.py:25
  190.1 32.1 %copy-start.3 = (s32[128]{0:T(128)S(1)}, s32[128]{0:T(128)}, u32[]{:S(2)}) copy-start(s32[128]{0:T(128)} %param.8) | copy-start | bytes 1540
  191.4 31.7 %copy-start.6 = (f32[128]{0:T(128)S(1)}, f32[128]{0:T(128)}, u32[]{:S(2)}) copy-start(f32[128]{0:T(128)} %get-tuple-element.4) | copy-start | bytes 1540
  192.5 27.7 %all-to-all-start.6 = ((bf16[128,2,1152]{2,1,0:T(2,128)(2,1)}), bf16[128,2,1152]{2,1,0:T(2,128)(2,1)S(1)}, u32[]{:S(2)}, u32[]{:S(2)}) async-start(bf16[128,2,1152]{2,1,0:T(2,128)(2,1)} %reshape.249), calls=%async_computation.6 | async-start | bytes 1179648 | tf_op jit(solution)/shard_map/all_to_all | solution.py:25
  220.3 3.0 %copy-start = (bf16[512,4096]{1,0:T(8,128)(2,1)S(1)}, bf16[512,4096]{1,0:T(8,128)(2,1)}, u32[]{:S(2)}) copy-start(bf16[512,4096]{1,0:T(8,128)(2,1)} %all-gather.2.cloned.1.call-done) | copy-start | bytes 12582916
Sparse Core Ops, SparseCore 0:
  34.6 39.7 all-gather.1

commit v3 on v2

--- a/solution.py
+++ b/solution.py
@@ -3,11 +3,14 @@
 import jax
 import jax.numpy as jnp
 from jax import lax
+from jax.experimental import pallas as pl
+from jax.experimental.pallas import tpu as pltpu
 from jax.sharding import PartitionSpec as P
 
 CAPACITY = 2
 CORES = 2
 EXTRA = 128
+BLOCKS = 4
 SCORE_SCALE = 80.0
 GRADIENT_SCALE = 2560.0
 EPSILON = 1e-06
@@ -62,11 +65,108 @@
         [shard(z, y, 1) * parts + m for m in range(parts) for z in range(side)]
         for y in range(side)
     ]
-    second = [[shard(z, y, 0) for z in range(side)] for y in range(side)] + [
-        [shard(z, y, 1) for y in range(side)] for z in range(side)
-    ]
+
+    def swaps(odd):
+        partner = [((p + odd) ^ 1) - odd for p in range(side)]
+        partner = [p % side for p in partner]
+        out = []
+        for z in range(side):
+            for y in range(side):
+                out.append((shard(z, y, 0), shard(partner[z], y, 0)))
+                out.append((shard(z, y, 1), shard(z, partner[y], 1)))
+        return out
+
     other_core = [(d, d ^ 1) for d in range(shards)]
-    return side, first, second, other_core
+    return side, first, (swaps(0), swaps(1)), other_core
+
+
+def project_kernel(places, states, *refs):
+    groups = len(refs[:-5]) // BLOCKS
+    blocks = refs[: groups * BLOCKS]
+    weight_out, projected, squares, weight, sems = refs[groups * BLOCKS :]
+    rows = blocks[0].shape[0]
+    tile = rows * BLOCKS
+
+    def base(group):
+        return pl.multiple_of(places[group] * tile, tile)
+
+    copies = []
+    for i, block in enumerate(blocks):
+        at = pl.multiple_of(base(i // BLOCKS) + places[groups + i] * rows, rows)
+        copies.append(pltpu.make_async_copy(block, weight.at[pl.ds(at, rows)], sems.at[i]))
+        copies[-1].start()
+    total = jnp.zeros(squares.shape, F32)
+    outs = []
+    for group in range(groups):
+        for copy in copies[group * BLOCKS : (group + 1) * BLOCKS]:
+            copy.wait()
+        at = pl.ds(base(group), tile)
+        outs.append(
+            pltpu.make_async_copy(
+                weight.at[at], weight_out.at[at], sems.at[groups * BLOCKS + group]
+            )
+        )
+        outs[-1].start()
+        value = dot(states[...], weight[at, :], LAST_BOTH)
+        projected[:, at] = value
+        total = total + jnp.sum(value * value, axis=1, keepdims=True)
+    squares[...] = total
+    for out in outs:
+        out.wait()
+
+
+def project(places, states, blocks):
+    rows, depth = states.shape
+    width = sum(block.shape[0] for block in blocks)
+    vmem = pl.BlockSpec(memory_space=pltpu.VMEM)
+    anywhere = pl.BlockSpec(memory_space=pl.ANY)
+    return pl.pallas_call(
+        project_kernel,
+        out_shape=(
+            jax.ShapeDtypeStruct((width, depth), BF16),
+            jax.ShapeDtypeStruct((rows, width), F32),
+            jax.ShapeDtypeStruct((rows, 1), F32),
+        ),
+        in_specs=[pl.BlockSpec(memory_space=pltpu.SMEM), vmem] + [anywhere] * len(blocks),
+        out_specs=(anywhere, vmem, vmem),
+        scratch_shapes=[
+            pltpu.VMEM((width, depth), BF16),
+            pltpu.SemaphoreType.DMA((len(blocks) + len(blocks) // BLOCKS,)),
+        ],
+        compiler_params=pltpu.CompilerParams(vmem_limit_bytes=24 * 2**20),
+        cost_estimate=pl.CostEstimate(
+            flops=2 * rows * depth * width,
+            bytes_accessed=4 * width * depth,
+            transcendentals=0,
+        ),
+    )(places, states, *blocks)
+
+
+def spread_kernel(grad, weight, out):
+    out[0] = dot(grad[...], weight[...]).astype(BF16)
+
+
+def spread(grad, weight, parts):
+    rows, width = grad.shape
+    columns_each = weight.shape[1] // parts
+    tile = min(512, columns_each)
+    per_part = columns_each // tile
+    return pl.pallas_call(
+        spread_kernel,
+        grid=(parts * per_part,),
+        out_shape=jax.ShapeDtypeStruct((parts, rows, columns_each), BF16),
+        in_specs=[
+            pl.BlockSpec((rows, width), lambda n: (0, 0)),
+            pl.BlockSpec((width, tile), lambda n: (0, n)),
+        ],
+        out_specs=pl.BlockSpec((1, rows, tile), lambda n: (n // per_part, 0, n % per_part)),
+        compiler_params=pltpu.CompilerParams(vmem_limit_bytes=24 * 2**20),
+        cost_estimate=pl.CostEstimate(
+            flops=2 * rows * width * weight.shape[1],
+            bytes_accessed=2 * width * weight.shape[1],
+            transcendentals=0,
+        ),
+    )(grad, weight)
 
 
 def on_device(query_states, passage_states, head_weight, positives, negatives):
@@ -74,19 +174,61 @@
     parts = lax.axis_size("mp")
     shards = lax.axis_size("dp")
     slots = shards * CAPACITY
-    side, first, second, other_core = lines(shards, parts)
+    side, first, matchings, other_core = lines(shards, parts)
     rows = head_weight.shape[0] // parts
-    core = lax.axis_index("dp") % CORES
+    shard = lax.axis_index("dp")
+    core = shard % CORES
+    z, y = shard // (CORES * side), (shard // CORES) % side
 
     line = jnp.broadcast_to(
         head_weight.reshape(parts, 1, rows, width), (parts, side, rows, width)
     ).reshape(parts * side, rows, width)
     line = swap(line, ("dp", "mp"), first).reshape(parts, side, rows, width)
     line = line.transpose(1, 2, 0, 3).reshape(side * rows, parts * width)
-    weight_own = lax.all_gather(line, "dp", axis=0, tiled=True, axis_index_groups=second)
-    weight_other = lax.ppermute(weight_own, "dp", other_core)
+
+    position = jnp.where(core == 0, z, y)
+    halves = (line[: side * rows // 2], line[side * rows // 2 :])
+    own_blocks = [], []
+    held = list(halves)
+    for step in range(BLOCKS):
+        for stream in range(2):
+            came = lax.ppermute(held[stream], "dp", matchings[(step + stream) % 2])
+            if step == 0:
+                is_lower = (position + stream) % 2 == 0
+                half = halves[stream]
+                came = jnp.concatenate(
+                    [jnp.where(is_lower, half, came), jnp.where(is_lower, came, half)], axis=0
+                )
+            own_blocks[stream].append(came)
+            held[stream] = came
+    own_blocks = own_blocks[0] + own_blocks[1]
+    other_blocks = [lax.ppermute(block, "dp", other_core) for block in own_blocks]
+
+    def places_of(core, position):
+        groups, places = [], []
+        for stream in range(2):
+            groups.append(core * 2 + stream)
+            up = (position + stream) % 2
+            index = (position + stream) // 2
+            for move in (0, 2 * up - 1, 1 - 2 * up, 2):
+                places.append((index + move) % BLOCKS)
+        return groups, places
+
+    own_groups, own_places = places_of(core, position)
+    other_groups, other_places = places_of(1 - core, jnp.where(core == 0, y, z))
+    places = jnp.stack(own_groups + other_groups + own_places + other_places).astype(jnp.int32)
+
     states = jnp.concatenate([query_states, passage_states], axis=0)
-    states = from_all(states, "mp").transpose(1, 0, 2).reshape(2 * pairs, parts * width)
+    me = lax.axis_index("mp")
+    came = [states] + [
+        lax.ppermute(states, "mp", [(i, (i + k) % parts) for i in range(parts)])
+        for k in range(1, parts)
+    ]
+    came = jnp.stack(came)
+    states = jnp.concatenate(
+        [lax.dynamic_index_in_dim(came, (me - m) % parts, 0, False) for m in range(parts)],
+        axis=1,
+    )
 
     block = negatives.reshape(-1)
     order = jnp.arange(pairs, dtype=jnp.int32)
@@ -96,15 +238,7 @@
     to_slot = in_slot.astype(BF16)
     positive_mask = (positives[:, None] == order[None, :]).astype(F32)
 
-    def in_order(own, other):
-        return jnp.where(core == 0, own, other), jnp.where(core == 0, other, own)
-
-    projected_own = dot(states, weight_own, LAST_BOTH)
-    projected_other = dot(states, weight_other, LAST_BOTH)
-    squares = jnp.sum(projected_own * projected_own, axis=1) + jnp.sum(
-        projected_other * projected_other, axis=1
-    )
-    projected = jnp.concatenate(in_order(projected_own, projected_other), axis=1)
+    weight, projected, squares = project(places, states, own_blocks + other_blocks)
     squares = sum_all(squares.reshape(-1, math.gcd(128, 2 * pairs)), "mp").reshape(-1)
     inverse = lax.rsqrt(squares[:, None] + EPSILON)
     embedded = (projected * inverse).astype(BF16)
@@ -153,9 +287,7 @@
     grad = jnp.concatenate([query_grad, passage_grad], axis=0)
     radial = jnp.concatenate([query_radial, passage_radial], axis=0)[:, None]
     proj_grad = (inverse * grad - projected * (inverse * inverse * radial)).astype(BF16)
-    grad_own, grad_other = in_order(proj_grad[:, : part // 2], proj_grad[:, part // 2 :])
-    partial = (dot(grad_own, weight_own) + dot(grad_other, weight_other)).astype(BF16)
-    partial = partial.reshape(2 * pairs, parts, width).transpose(1, 0, 2)
+    partial = spread(proj_grad, weight, parts)
     state_grad = jnp.sum(swap(partial, "mp").astype(F32), axis=0)
     return (state_grad[:pairs], state_grad[pairs:])
 

time: 266 us -> 251 us (0.944)
  waiting for transfers between devices: 107 us -> 45.4 us
  starting transfers between devices: 26.6 us -> 81.3 us
  matrix products: 15 us -> 2.36 us
  Pallas kernels: 0 us -> 12.4 us
  between operations: 14.4 us -> 2.01 us
  local copies, waits for them, and re-layouts: 10.1 us -> 14.7 us
    ppermute x1 -> x19, starting transfers between devices: 6.92 us -> 65.4 us  [the longest x8 31.7 us: on_device(): lax.ppermute(block, 'dp', other_core)]
    all_gather x1 -> x0, waiting for transfers between devices: 39.9 us -> none  [on_device(): lax.all_gather(line, 'dp', axis=0, tiled=True, axis_index_groups=second)]
    all_to_all x5 -> x4, waiting for transfers between devices: 67 us -> 40.8 us  [swap(): lax.all_to_all(x, axis, split_axis=0, concat_axis=0, tiled=True, axis_ind...]
    dot_general x12 -> x8, matrix products: 15 us -> 2.36 us  [dot(): return lax.dot_general(a, b, dims, preferred_element_type=F32)]
    pallas_call x0 -> x2, Pallas kernels: none -> 12.4 us  [the longest x1 7.82 us: project(): pl.pallas_call(project_kernel, out_shape=(jax.ShapeDtypeStruct((width, de...]
    unnamed x17 -> x27, local copies, waits for them, and re-layouts: 1.49 us -> 7.39 us
    ppermute x1 -> x19, waiting for transfers between devices: 0.01 us -> 4.62 us  [the longest x8 3.34 us: on_device(): came = lax.ppermute(held[stream], 'dp', matchings[(step + stream) % 2])]
    all_to_all x5 -> x4, starting transfers between devices: 19.7 us -> 15.9 us  [swap(): lax.all_to_all(x, axis, split_axis=0, concat_axis=0, tiled=True, axis_ind...]
  transfers between devices with their start and end apart: 7 -> 23, of which waited for: 6 -> 7; matrix products, arithmetic and copies ran while one was open for 2% -> 2% of each run, Pallas kernels for 0% -> 0%
where the time goes in v3:
time: 251 us; the launch traced here: 250 us
  blocking collectives  87.6 us (35%)
  starting transfers between devices  81.3 us (32%)
  waiting for transfers between devices  45.4 us (18%)
  local copies, waits for them, and re-layouts  14.7 us (6%)
  Pallas kernels  12.4 us (5%)
  other arithmetic  4.6 us (2%)
    all_to_all x3, blocking collectives, swap(): lax.all_to_all(x, axis, split_axis=0, concat_axis=0, tiled=True, axis_ind...  87.6 us
    all_to_all x4, waiting for transfers between devices, swap(): lax.all_to_all(x, axis, split_axis=0, concat_axis=0, tiled=True, axis_ind...  40.8 us
    ppermute x8, starting transfers between devices, on_device(): lax.ppermute(block, 'dp', other_core)  31.7 us
    ppermute x8, starting transfers between devices, on_device(): came = lax.ppermute(held[stream], 'dp', matchings[(step + stream) % 2])  24.9 us
    all_to_all x4, starting transfers between devices, swap(): lax.all_to_all(x, axis, split_axis=0, concat_axis=0, tiled=True, axis_ind...  15.9 us
    ppermute x3, starting transfers between devices, on_device(): lax.ppermute(states, 'mp', [(i, (i + k) % parts) for i in range(parts)])  8.81 us
    pallas_call x1, Pallas kernels, project(): pl.pallas_call(project_kernel, out_shape=(jax.ShapeDtypeStruct((width, de...  7.82 us
    unnamed x27, local copies, waits for them, and re-layouts  7.39 us
  transfers between devices with their start and end apart: 23, of which 7 were waited for; matrix products, arithmetic and copies ran while one was open for 2% of the time, Pallas kernels for 0%

profile of v3, /device:TPU:1, one launch (start us, length us, event | category | flops | bytes accessed | tf_op | source)
XLA Modules:
  0.0 250.3 jit_solution(17936915537653722611)
XLA Ops:
  1.5 24.9 %all_to_all.35 = bf16[32,8,1024]{2,1,0:T(8,128)(2,1)S(1)} all-to-all(bf16[32,8,1024]{2,1,0:T(8,128)(2,1)S(1)} %bitcast.58), channel_id=1, replica_groups={{0,8,16,24,32,40,48,56,1,9,17,25,33,41,49,57,2,10,18,26,34,42,50,58,3,1..., dimensions={0} | all-to-all | bytes 1048576 | tf_op jit(solution)/shard_map/all_to_all | solution.py:28
  26.5 5.1 %collective-permute-start.7 = (bf16[32,4096]{1,0:T(8,128)(2,1)S(1)}, bf16[32,4096]{1,0:T(8,128)(2,1)S(1)}, u32[]{:S(2)}, u32[]{:S(2)}) collective-permute-start(bf16[32,4096]{1,0:T(8,128)(2,1)S(1)} %bitcast.59), channel_id=1, source_target_pairs={{0,448},{4,60},{8,456},{12,20},{16,464},{20,12},{24,472},{28,36},{... | collective-permute-start | bytes 786440 | tf_op jit(solution)/shard_map/ppermute | solution.py:195
  39.4 3.1 %collective-permute-start.4 = (bf16[64,4096]{1,0:T(8,128)(2,1)S(1)}, bf16[64,4096]{1,0:T(8,128)(2,1)S(1)}, u32[]{:S(2)}, u32[]{:S(2)}) collective-permute-start(bf16[64,4096]{1,0:T(8,128)(2,1)S(1)} %pad_maximum_fusion.2.refs_0_), channel_id=1, source_target_pairs={{0,448},{4,60},{8,456},{12,20},{16,464},{20,12},{24,472},{28,36},{... | collective-permute-start | bytes 1572872 | tf_op jit(solution)/shard_map/ppermute | solution.py:195
  45.9 3.8 %collective-permute-start.1 = (bf16[256,1024]{1,0:T(8,128)(2,1)}, bf16[256,1024]{1,0:T(8,128)(2,1)}, u32[]{:S(2)}, u32[]{:S(2)}) collective-permute-start(bf16[256,1024]{1,0:T(8,128)(2,1)} %constant_dynamic-update-slice_fusion), channel_id=1, source_target_pairs={{0,2},{1,3},{2,0},{3,1},{4,6},{5,7},{6,4},{7,5},{8,10},{9,11},{10,... | collective-permute-start | bytes 1572872 | tf_op jit(solution)/shard_map/ppermute | solution.py:224
  49.7 3.1 %collective-permute-start.2 = (bf16[256,1024]{1,0:T(8,128)(2,1)}, bf16[256,1024]{1,0:T(8,128)(2,1)}, u32[]{:S(2)}, u32[]{:S(2)}) collective-permute-start(bf16[256,1024]{1,0:T(8,128)(2,1)} %constant_dynamic-update-slice_fusion), channel_id=1, source_target_pairs={{0,3},{1,0},{2,1},{3,2},{4,7},{5,4},{6,5},{7,6},{8,11},{9,8},{10,9... | collective-permute-start | bytes 1572872 | tf_op jit(solution)/shard_map/ppermute | solution.py:224
  52.8 3.7 %collective-permute-start.9 = (bf16[64,4096]{1,0:T(8,128)(2,1)S(1)}, bf16[64,4096]{1,0:T(8,128)(2,1)S(1)}, u32[]{:S(2)}, u32[]{:S(2)}) collective-permute-start(bf16[64,4096]{1,0:T(8,128)(2,1)S(1)} %collective-permute-done.8.refs_5_), channel_id=1, source_target_pairs={{0,448},{4,60},{8,456},{12,20},{16,464},{20,12},{24,472},{28,36},{... | collective-permute-start | bytes 1572872 | tf_op jit(solution)/shard_map/ppermute | solution.py:195
  58.4 16.4 %collective-permute-start.15 = (bf16[64,4096]{1,0:T(8,128)(2,1)S(1)}, bf16[64,4096]{1,0:T(8,128)(2,1)}, u32[]{:S(2)}, u32[]{:S(2)}) collective-permute-start(bf16[64,4096]{1,0:T(8,128)(2,1)S(1)} %pad_maximum_fusion.3.refs_4_), channel_id=1, source_target_pairs={{0,4},{4,0},{8,12},{12,8},{16,20},{20,16},{24,28},{28,24},{32,36},... | collective-permute-start | bytes 1572872 | tf_op jit(solution)/shard_map/ppermute | solution.py:205
  76.8 2.4 collective-permute-start.16
  79.2 2.5 collective-permute-start.10
  81.7 4.6 %collective-permute-start.6 = (bf16[64,4096]{1,0:T(8,128)(2,1)S(1)}, bf16[64,4096]{1,0:T(8,128)(2,1)}, u32[]{:S(2)}, u32[]{:S(2)}) collective-permute-start(bf16[64,4096]{1,0:T(8,128)(2,1)S(1)} %collective-permute-done.5.refs_2_), channel_id=1, source_target_pairs={{0,448},{4,60},{8,456},{12,20},{16,464},{20,12},{24,472},{28,36},{... | collective-permute-start | bytes 1572872 | tf_op jit(solution)/shard_map/ppermute | solution.py:195
  101.5 7.8 %shard_map.68 = (bf16[1024,4096]{1,0:T(8,128)(2,1)S(1)}, f32[256,1024]{1,0:T(8,128)S(1)}, f32[256,1]{1,0:T(8,128)S(1)}) custom-call(s32[20]{0:T(128)S(1)} %stack.113.places, bf16[256,4096]{1,0:T(8,128)(2,1)S(1)} %pad_maximum_fusion.1.states, bf16[64,4096]{1,0:T(8,128)(2,1)S(1)} %pad_maximum_fusion.2.refs_0_, ...), custom_call_target="tpu_custom_call" | custom-call | flops 2147483648 | bytes 16777216 | tf_op jit(solution)/shard_map/pallas_call | solution.py:123
  109.3 3.2 %copy-done = bf16[1024,4096]{1,0:T(8,128)(2,1)} copy-done((bf16[1024,4096]{1,0:T(8,128)(2,1)}, bf16[1024,4096]{1,0:T(8,128)(2,1)S(1)}, u32[]{:S(2)}) %copy-start) | copy-done | bytes 8388632
  113.3 3.2 %all-to-all-start.1 = ((f32[4,2,128]{2,1,0:T(2,128)}), f32[4,2,128]{2,1,0:T(2,128)S(1)}, u32[]{:S(2)}, u32[]{:S(2)}) async-start(f32[4,2,128]{2,1,0:T(2,128)} %broadcast_in_dim.15), calls=%async_computation.1 | async-start | bytes 8192 | tf_op jit(solution)/shard_map/all_to_all | solution.py:28
  116.7 3.9 %all-to-all-done.1 = f32[4,2,128]{2,1,0:T(2,128)S(1)} async-done(((f32[4,2,128]{2,1,0:T(2,128)}), f32[4,2,128]{2,1,0:T(2,128)S(1)}, u32[]{:S(2)}, u32[]{:S(2)}) %all-to-all-start.1) | async-done | bytes 4128 | tf_op jit(solution)/shard_map/all_to_all | solution.py:28
  121.7 3.4 %all-to-all-start.2 = ((f32[4,128,128]{2,1,0:T(8,128)}), f32[4,128,128]{2,1,0:T(8,128)S(1)}, u32[]{:S(2)}, u32[]{:S(2)}) async-start(f32[4,128,128]{2,1,0:T(8,128)} %broadcast_in_dim.16), calls=%async_computation.2 | async-start | bytes 524288 | tf_op jit(solution)/shard_map/all_to_all | solution.py:28
  125.2 5.4 %all-to-all-done.2 = f32[4,128,128]{2,1,0:T(8,128)S(1)} async-done(((f32[4,128,128]{2,1,0:T(8,128)}), f32[4,128,128]{2,1,0:T(8,128)S(1)}, u32[]{:S(2)}, u32[]{:S(2)}) %all-to-all-start.2) | async-done | bytes 262176 | tf_op jit(solution)/shard_map/all_to_all | solution.py:28
  131.5 33.5 %all_to_all.36 = bf16[128,2,1152]{2,1,0:T(2,128)(2,1)S(1)} all-to-all(bf16[128,2,1152]{2,1,0:T(2,128)(2,1)S(1)} %reshape.229), channel_id=1, replica_groups=mesh['dp'=128,'mp'=4] {'dp'}, dimensions={0} | all-to-all | bytes 1179648 | tf_op jit(solution)/shard_map/all_to_all | solution.py:28
  166.4 3.5 %all-to-all-start.4 = ((f32[4,256,128]{2,1,0:T(8,128)}), f32[4,256,128]{2,1,0:T(8,128)S(1)}, u32[]{:S(2)}, u32[]{:S(2)}) async-start(f32[4,256,128]{2,1,0:T(8,128)} %broadcast_in_dim.17), calls=%async_computation.4 | async-start | bytes 1048576 | tf_op jit(solution)/shard_map/all_to_all | solution.py:28
  169.9 9.7 %all-to-all-done.4 = f32[4,256,128]{2,1,0:T(8,128)S(1)} async-done(((f32[4,256,128]{2,1,0:T(8,128)}), f32[4,256,128]{2,1,0:T(8,128)S(1)}, u32[]{:S(2)}, u32[]{:S(2)}) %all-to-all-start.4) | async-done | bytes 524320 | tf_op jit(solution)/shard_map/all_to_all | solution.py:28
  182.1 5.7 %all-to-all-start.5 = ((bf16[128,2,1152]{2,1,0:T(2,128)(2,1)}), bf16[128,2,1152]{2,1,0:T(2,128)(2,1)S(1)}, u32[]{:S(2)}, u32[]{:S(2)}) async-start(bf16[128,2,1152]{2,1,0:T(2,128)(2,1)} %reshape.231), calls=%async_computation.5 | async-start | bytes 1179648 | tf_op jit(solution)/shard_map/all_to_all | solution.py:28
  188.2 21.7 %all-to-all-done.5 = bf16[128,2,1152]{2,1,0:T(2,128)(2,1)S(1)} async-done(((bf16[128,2,1152]{2,1,0:T(2,128)(2,1)}), bf16[128,2,1152]{2,1,0:T(2,128)(2,1)S(1)}, u32[]{:S(2)}, u32[]{:S(2)}) %all-to-all-start.5) | async-done | bytes 589856 | tf_op jit(solution)/shard_map/all_to_all | solution.py:28
  211.8 3.4 %copy-done.1 = bf16[1024,4096]{1,0:T(8,128)(2,1)S(1)} copy-done((bf16[1024,4096]{1,0:T(8,128)(2,1)S(1)}, bf16[1024,4096]{1,0:T(8,128)(2,1)}, u32[]{:S(2)}) %copy-start.1) | copy-done | bytes 8388632
  215.1 4.6 %shard_map.69 = bf16[4,256,1024]{2,1,0:T(8,128)(2,1)S(1)} custom-call(bf16[256,1024]{1,0:T(8,128)(2,1)S(1)} %fusion.3.grad, bf16[1024,4096]{1,0:T(8,128)(2,1)S(1)} %copy-done.1), custom_call_target="tpu_custom_call" | custom-call | flops 2147483648 | bytes 8388608 | tf_op jit(solution)/shard_map/pallas_call | solution.py:154
  219.7 29.2 %all_to_all.37 = bf16[4,256,1024]{2,1,0:T(8,128)(2,1)S(1)} all-to-all(bf16[4,256,1024]{2,1,0:T(8,128)(2,1)S(1)} %shard_map.69), channel_id=1, replica_groups=mesh['dp'=128,'mp'=4] {'mp'}, dimensions={0} | all-to-all | bytes 4194304 | tf_op jit(solution)/shard_map/all_to_all | solution.py:28
  (113 shorter events, 40.5 us)
Async XLA Ops:
  26.5 8.9 %collective-permute-start.7 = (bf16[32,4096]{1,0:T(8,128)(2,1)S(1)}, bf16[32,4096]{1,0:T(8,128)(2,1)S(1)}, u32[]{:S(2)}, u32[]{:S(2)}) collective-permute-start(bf16[32,4096]{1,0:T(8,128)(2,1)S(1)} %bitcast.59), channel_id=1, source_target_pairs={{0,448},{4,60},{8,456},{12,20},{16,464},{20,12},{24,472},{28,36},{... | collective-permute-start | bytes 786440 | tf_op jit(solution)/shard_map/ppermute | solution.py:195
  31.7 7.5 %collective-permute-start.3 = (bf16[32,4096]{1,0:T(8,128)(2,1)S(1)}, bf16[32,4096]{1,0:T(8,128)(2,1)S(1)}, u32[]{:S(2)}, u32[]{:S(2)}) collective-permute-start(bf16[32,4096]{1,0:T(8,128)(2,1)S(1)} %bitcast.61), channel_id=1, source_target_pairs={{0,64},{4,12},{8,72},{12,4},{16,80},{20,28},{24,88},{28,20},{32,96... | collective-permute-start | bytes 786440 | tf_op jit(solution)/shard_map/ppermute | solution.py:195
  35.4 17.3 %collective-permute-start.8 = (bf16[64,4096]{1,0:T(8,128)(2,1)S(1)}, bf16[64,4096]{1,0:T(8,128)(2,1)S(1)}, u32[]{:S(2)}, u32[]{:S(2)}) collective-permute-start(bf16[64,4096]{1,0:T(8,128)(2,1)S(1)} %pad_maximum_fusion.3.refs_4_), channel_id=1, source_target_pairs={{0,64},{4,12},{8,72},{12,4},{16,80},{20,28},{24,88},{28,20},{32,96... | collective-permute-start | bytes 1572872 | tf_op jit(solution)/shard_map/ppermute | solution.py:195
  39.4 17.1 %collective-permute-start.4 = (bf16[64,4096]{1,0:T(8,128)(2,1)S(1)}, bf16[64,4096]{1,0:T(8,128)(2,1)S(1)}, u32[]{:S(2)}, u32[]{:S(2)}) collective-permute-start(bf16[64,4096]{1,0:T(8,128)(2,1)S(1)} %pad_maximum_fusion.2.refs_0_), channel_id=1, source_target_pairs={{0,448},{4,60},{8,456},{12,20},{16,464},{20,12},{24,472},{28,36},{... | collective-permute-start | bytes 1572872 | tf_op jit(solution)/shard_map/ppermute | solution.py:195
  43.9 14.5 %collective-permute-start = (bf16[256,1024]{1,0:T(8,128)(2,1)}, bf16[256,1024]{1,0:T(8,128)(2,1)}, u32[]{:S(2)}, u32[]{:S(2)}) collective-permute-start(bf16[256,1024]{1,0:T(8,128)(2,1)} %constant_dynamic-update-slice_fusion), channel_id=1, source_target_pairs={{0,1},{1,2},{2,3},{3,0},{4,5},{5,6},{6,7},{7,4},{8,9},{9,10},{10,1... | collective-permute-start | bytes 1572872 | tf_op jit(solution)/shard_map/ppermute | solution.py:224
  45.9 28.9 %collective-permute-start.1 = (bf16[256,1024]{1,0:T(8,128)(2,1)}, bf16[256,1024]{1,0:T(8,128)(2,1)}, u32[]{:S(2)}, u32[]{:S(2)}) collective-permute-start(bf16[256,1024]{1,0:T(8,128)(2,1)} %constant_dynamic-update-slice_fusion), channel_id=1, source_target_pairs={{0,2},{1,3},{2,0},{3,1},{4,6},{5,7},{6,4},{7,5},{8,10},{9,11},{10,... | collective-permute-start | bytes 1572872 | tf_op jit(solution)/shard_map/ppermute | solution.py:224
  49.7 27.1 %collective-permute-start.2 = (bf16[256,1024]{1,0:T(8,128)(2,1)}, bf16[256,1024]{1,0:T(8,128)(2,1)}, u32[]{:S(2)}, u32[]{:S(2)}) collective-permute-start(bf16[256,1024]{1,0:T(8,128)(2,1)} %constant_dynamic-update-slice_fusion), channel_id=1, source_target_pairs={{0,3},{1,0},{2,1},{3,2},{4,7},{5,4},{6,5},{7,6},{8,11},{9,8},{10,9... | collective-permute-start | bytes 1572872 | tf_op jit(solution)/shard_map/ppermute | solution.py:224
  52.8 26.4 %collective-permute-start.9 = (bf16[64,4096]{1,0:T(8,128)(2,1)S(1)}, bf16[64,4096]{1,0:T(8,128)(2,1)S(1)}, u32[]{:S(2)}, u32[]{:S(2)}) collective-permute-start(bf16[64,4096]{1,0:T(8,128)(2,1)S(1)} %collective-permute-done.8.refs_5_), channel_id=1, source_target_pairs={{0,448},{4,60},{8,456},{12,20},{16,464},{20,12},{24,472},{28,36},{... | collective-permute-start | bytes 1572872 | tf_op jit(solution)/shard_map/ppermute | solution.py:195
  56.5 25.2 %collective-permute-start.5 = (bf16[64,4096]{1,0:T(8,128)(2,1)S(1)}, bf16[64,4096]{1,0:T(8,128)(2,1)S(1)}, u32[]{:S(2)}, u32[]{:S(2)}) collective-permute-start(bf16[64,4096]{1,0:T(8,128)(2,1)S(1)} %collective-permute-done.4.refs_1_), channel_id=1, source_target_pairs={{0,64},{4,12},{8,72},{12,4},{16,80},{20,28},{24,88},{28,20},{32,96... | collective-permute-start | bytes 1572872 | tf_op jit(solution)/shard_map/ppermute | solution.py:195
  58.4 30.3 %collective-permute-start.15 = (bf16[64,4096]{1,0:T(8,128)(2,1)S(1)}, bf16[64,4096]{1,0:T(8,128)(2,1)}, u32[]{:S(2)}, u32[]{:S(2)}) collective-permute-start(bf16[64,4096]{1,0:T(8,128)(2,1)S(1)} %pad_maximum_fusion.3.refs_4_), channel_id=1, source_target_pairs={{0,4},{4,0},{8,12},{12,8},{16,20},{20,16},{24,28},{28,24},{32,36},... | collective-permute-start | bytes 1572872 | tf_op jit(solution)/shard_map/ppermute | solution.py:205
  74.8 16.2 %collective-permute-start.11 = (bf16[64,4096]{1,0:T(8,128)(2,1)S(1)}, bf16[64,4096]{1,0:T(8,128)(2,1)}, u32[]{:S(2)}, u32[]{:S(2)}) collective-permute-start(bf16[64,4096]{1,0:T(8,128)(2,1)S(1)} %pad_maximum_fusion.2.refs_0_), channel_id=1, source_target_pairs={{0,4},{4,0},{8,12},{12,8},{16,20},{20,16},{24,28},{28,24},{32,36},... | collective-permute-start | bytes 1572872 | tf_op jit(solution)/shard_map/ppermute | solution.py:205
  76.8 16.3 %collective-permute-start.16 = (bf16[64,4096]{1,0:T(8,128)(2,1)S(1)}, bf16[64,4096]{1,0:T(8,128)(2,1)}, u32[]{:S(2)}, u32[]{:S(2)}) collective-permute-start(bf16[64,4096]{1,0:T(8,128)(2,1)S(1)} %collective-permute-done.8.refs_5_), channel_id=1, source_target_pairs={{0,4},{4,0},{8,12},{12,8},{16,20},{20,16},{24,28},{28,24},{32,36},... | collective-permute-start | bytes 1572872 | tf_op jit(solution)/shard_map/ppermute | solution.py:205
  79.2 16.2 %collective-permute-start.10 = (bf16[64,4096]{1,0:T(8,128)(2,1)S(1)}, bf16[64,4096]{1,0:T(8,128)(2,1)}, u32[]{:S(2)}, u32[]{:S(2)}) collective-permute-start(bf16[64,4096]{1,0:T(8,128)(2,1)S(1)} %collective-permute-done.9.refs_6_), channel_id=1, source_target_pairs={{0,64},{4,12},{8,72},{12,4},{16,80},{20,28},{24,88},{28,20},{32,96... | collective-permute-start | bytes 1572872 | tf_op jit(solution)/shard_map/ppermute | solution.py:195
  81.7 15.7 %collective-permute-start.6 = (bf16[64,4096]{1,0:T(8,128)(2,1)S(1)}, bf16[64,4096]{1,0:T(8,128)(2,1)}, u32[]{:S(2)}, u32[]{:S(2)}) collective-permute-start(bf16[64,4096]{1,0:T(8,128)(2,1)S(1)} %collective-permute-done.5.refs_2_), channel_id=1, source_target_pairs={{0,448},{4,60},{8,456},{12,20},{16,464},{20,12},{24,472},{28,36},{... | collective-permute-start | bytes 1572872 | tf_op jit(solution)/shard_map/ppermute | solution.py:195
  88.7 11.5 %collective-permute-start.12 = (bf16[64,4096]{1,0:T(8,128)(2,1)S(1)}, bf16[64,4096]{1,0:T(8,128)(2,1)S(1)}, u32[]{:S(2)}, u32[]{:S(2)}) collective-permute-start(bf16[64,4096]{1,0:T(8,128)(2,1)S(1)} %collective-permute-done.4.refs_1_), channel_id=1, source_target_pairs={{0,4},{4,0},{8,12},{12,8},{16,20},{20,16},{24,28},{28,24},{32,36},... | collective-permute-start | bytes 1572872 | tf_op jit(solution)/shard_map/ppermute | solution.py:205
  91.0 9.2 %collective-permute-start.17 = (bf16[64,4096]{1,0:T(8,128)(2,1)S(1)}, bf16[64,4096]{1,0:T(8,128)(2,1)S(1)}, u32[]{:S(2)}, u32[]{:S(2)}) collective-permute-start(bf16[64,4096]{1,0:T(8,128)(2,1)S(1)} %collective-permute-done.9.refs_6_), channel_id=1, source_target_pairs={{0,4},{4,0},{8,12},{12,8},{16,20},{20,16},{24,28},{28,24},{32,36},... | collective-permute-start | bytes 1572872 | tf_op jit(solution)/shard_map/ppermute | solution.py:205
  93.1 7.1 %collective-permute-start.13 = (bf16[64,4096]{1,0:T(8,128)(2,1)S(1)}, bf16[64,4096]{1,0:T(8,128)(2,1)S(1)}, u32[]{:S(2)}, u32[]{:S(2)}) collective-permute-start(bf16[64,4096]{1,0:T(8,128)(2,1)S(1)} %collective-permute-done.5.refs_2_), channel_id=1, source_target_pairs={{0,4},{4,0},{8,12},{12,8},{16,20},{20,16},{24,28},{28,24},{32,36},... | collective-permute-start | bytes 1572872 | tf_op jit(solution)/shard_map/ppermute | solution.py:205
  95.4 4.8 %collective-permute-start.18 = (bf16[64,4096]{1,0:T(8,128)(2,1)}, bf16[64,4096]{1,0:T(8,128)(2,1)S(1)}, u32[]{:S(2)}, u32[]{:S(2)}) collective-permute-start(bf16[64,4096]{1,0:T(8,128)(2,1)} %collective-permute-done.10.refs_7_), channel_id=1, source_target_pairs={{0,4},{4,0},{8,12},{12,8},{16,20},{20,16},{24,28},{28,24},{32,36},... | collective-permute-start | bytes 1572872 | tf_op jit(solution)/shard_map/ppermute | solution.py:205
  97.4 4.0 %collective-permute-start.14 = (bf16[64,4096]{1,0:T(8,128)(2,1)}, bf16[64,4096]{1,0:T(8,128)(2,1)S(1)}, u32[]{:S(2)}, u32[]{:S(2)}) collective-permute-start(bf16[64,4096]{1,0:T(8,128)(2,1)} %collective-permute-done.6.refs_3_), channel_id=1, source_target_pairs={{0,4},{4,0},{8,12},{12,8},{16,20},{20,16},{24,28},{28,24},{32,36},... | collective-permute-start | bytes 1572872 | tf_op jit(solution)/shard_map/ppermute | solution.py:205
  113.3 7.4 %all-to-all-start.1 = ((f32[4,2,128]{2,1,0:T(2,128)}), f32[4,2,128]{2,1,0:T(2,128)S(1)}, u32[]{:S(2)}, u32[]{:S(2)}) async-start(f32[4,2,128]{2,1,0:T(2,128)} %broadcast_in_dim.15), calls=%async_computation.1 | async-start | bytes 8192 | tf_op jit(solution)/shard_map/all_to_all | solution.py:28
  121.7 8.9 %all-to-all-start.2 = ((f32[4,128,128]{2,1,0:T(8,128)}), f32[4,128,128]{2,1,0:T(8,128)S(1)}, u32[]{:S(2)}, u32[]{:S(2)}) async-start(f32[4,128,128]{2,1,0:T(8,128)} %broadcast_in_dim.16), calls=%async_computation.2 | async-start | bytes 524288 | tf_op jit(solution)/shard_map/all_to_all | solution.py:28
  166.4 13.3 %all-to-all-start.4 = ((f32[4,256,128]{2,1,0:T(8,128)}), f32[4,256,128]{2,1,0:T(8,128)S(1)}, u32[]{:S(2)}, u32[]{:S(2)}) async-start(f32[4,256,128]{2,1,0:T(8,128)} %broadcast_in_dim.17), calls=%async_computation.4 | async-start | bytes 1048576 | tf_op jit(solution)/shard_map/all_to_all | solution.py:28
  181.0 29.1 %copy-start.10 = (s32[128]{0:T(128)S(1)}, s32[128]{0:T(128)}, u32[]{:S(2)}) copy-start(s32[128]{0:T(128)} %copy-done.9) | copy-start | bytes 1540
  182.1 27.8 %all-to-all-start.5 = ((bf16[128,2,1152]{2,1,0:T(2,128)(2,1)}), bf16[128,2,1152]{2,1,0:T(2,128)(2,1)S(1)}, u32[]{:S(2)}, u32[]{:S(2)}) async-start(bf16[128,2,1152]{2,1,0:T(2,128)(2,1)} %reshape.231), calls=%async_computation.5 | async-start | bytes 1179648 | tf_op jit(solution)/shard_map/all_to_all | solution.py:28
  (12 other events, 97.7 us)

commit v4 on v2

v4 whole, which is shorter than its diff:
```python
import math

import jax
import jax.numpy as jnp
from jax import lax
from jax.experimental import pallas as pl
from jax.experimental.pallas import tpu as pltpu
from jax.sharding import PartitionSpec as P

CAPACITY = 2
CORES = 2
EXTRA = 128
BLOCKS = 4
SCORE_SCALE = 80.0
GRADIENT_SCALE = 2560.0
EPSILON = 1e-06
LAST_BOTH = (((1,), (1,)), ((), ()))
FIRST_BOTH = (((0,), (0,)), ((), ()))
F32 = jnp.float32
BF16 = jnp.bfloat16


def dot(a, b, dims=(((1,), (0,)), ((), ()))):
    return lax.dot_general(a, b, dims, preferred_element_type=F32)


def swap(x, axis, groups=None):
    return lax.all_to_all(
        x, axis, split_axis=0, concat_axis=0, tiled=True, axis_index_groups=groups
    )


def from_all(x, axis):
    return swap(jnp.broadcast_to(x[None], (lax.axis_size(axis),) + x.shape), axis)


def sum_all(x, axis):
    return jnp.sum(from_all(x, axis), axis=0)


def parts_of(x, count):
    out = []
    for _ in range(count):
        part = lax.reduce_precision(x, 8, 7)
        out.append(part.astype(BF16))
        x = x - part
    return out


def columns(parts):
    stacked = jnp.stack(parts, axis=1)
    return jnp.pad(stacked, ((0, 0), (0, EXTRA - len(parts))))


def lines(shards, parts):
    side = math.isqrt(shards // CORES)

    def shard(z, y, core):
        return (z * side + y) * CORES + core

    first = [
        [shard(z, y, 0) * parts + m for m in range(parts) for y in range(side)]
        for z in range(side)
    ] + [
        [shard(z, y, 1) * parts + m for m in range(parts) for z in range(side)]
        for y in range(side)
    ]

    def swaps(odd):
        partner = [((p + odd) ^ 1) - odd for p in range(side)]
        partner = [p % side for p in partner]
        out = []
        for z in range(side):
            for y in range(side):
                out.append((shard(z, y, 0), shard(partner[z], y, 0)))
                out.append((shard(z, y, 1), shard(z, partner[y], 1)))
        return out

    other_core = [(d, d ^ 1) for d in range(shards)]
    return side, first, (swaps(0), swaps(1)), other_core


def project_kernel(places, states, *refs):
    arrays, (weight_out, projected, squares, weight, sems) = refs[:-5], refs[-5:]
    rows = weight.shape[0] // (2 * BLOCKS)
    tile, width = rows * BLOCKS, states.shape[2]
    copies, count = ([], []), 0
    for array, streams in zip(arrays, block_streams(len(arrays))):
        for i, stream in enumerate(streams):
            at = pl.multiple_of(stream * tile + places[count] * rows, rows)
            copy = pltpu.make_async_copy(
                array.at[pl.ds(i * rows, rows)], weight.at[pl.ds(at, rows)], sems.at[count]
            )
            copy.start()
            copies[stream].append(copy)
            count += 1
    total = jnp.zeros(squares.shape, F32)
    outs = []
    for stream in range(2):
        for copy in copies[stream]:
            copy.wait()
        at = pl.ds(stream * tile, tile)
        outs.append(
            pltpu.make_async_copy(weight.at[at], weight_out.at[at], sems.at[count + stream])
        )
        outs[-1].start()
        value = dot(states[0], weight[at, :width], LAST_BOTH)
        for part in range(1, states.shape[0]):
            columns_at = pl.ds(part * width, width)
            value = value + dot(states[part], weight[at, columns_at], LAST_BOTH)
        projected[:, at] = value
        total = total + jnp.sum(value * value, axis=1, keepdims=True)
    squares[...] = total
    for out in outs:
        out.wait()


def block_streams(arrays):
    return [[0], [1]] * BLOCKS


def project(places, states, arrays):
    parts, rows, each = states.shape
    depth = parts * each
    width = sum(array.shape[0] for array in arrays)
    vmem = pl.BlockSpec(memory_space=pltpu.VMEM)
    return pl.pallas_call(
        project_kernel,
        out_shape=(
            jax.ShapeDtypeStruct((width, depth), BF16),
            jax.ShapeDtypeStruct((rows, width), F32),
            jax.ShapeDtypeStruct((rows, 1), F32),
        ),
        in_specs=[pl.BlockSpec(memory_space=pltpu.SMEM), vmem]
        + [pl.BlockSpec(memory_space=pl.ANY)] * len(arrays),
        out_specs=(pl.BlockSpec(memory_space=pltpu.HBM), vmem, vmem),
        scratch_shapes=[
            pltpu.VMEM((width, depth), BF16),
            pltpu.SemaphoreType.DMA((2 * BLOCKS + 2,)),
        ],
        compiler_params=pltpu.CompilerParams(vmem_limit_bytes=52 * 2**20),
        cost_estimate=pl.CostEstimate(
            flops=2 * rows * depth * width,
            bytes_accessed=4 * width * depth,
            transcendentals=0,
        ),
    )(places, states, *arrays)


def spread_kernel(grad_own, grad_other, weight_own, weight_other, out):
    value = dot(grad_own[...], weight_own[...]) + dot(grad_other[...], weight_other[...])
    out[0] = value.astype(BF16)


def spread(grad_own, grad_other, weight_own, weight_other, parts):
    rows, width = grad_own.shape
    columns_each = weight_own.shape[1] // parts
    tile = min(512, columns_each)
    per_part = columns_each // tile
    return pl.pallas_call(
        spread_kernel,
        grid=(parts * per_part,),
        out_shape=jax.ShapeDtypeStruct((parts, rows, columns_each), BF16),
        in_specs=[pl.BlockSpec((rows, width), lambda n: (0, 0))] * 2
        + [pl.BlockSpec((width, tile), lambda n: (0, n))] * 2,
        out_specs=pl.BlockSpec((1, rows, tile), lambda n: (n // per_part, 0, n % per_part)),
        compiler_params=pltpu.CompilerParams(vmem_limit_bytes=24 * 2**20),
        cost_estimate=pl.CostEstimate(
            flops=4 * rows * width * weight_own.shape[1],
            bytes_accessed=4 * width * weight_own.shape[1],
            transcendentals=0,
        ),
    )(grad_own, grad_other, weight_own, weight_other)


def on_device(query_states, passage_states, head_weight, positives, negatives):
    pairs, width = query_states.shape
    parts = lax.axis_size("mp")
    shards = lax.axis_size("dp")
    side, first, matchings, other_core = lines(shards, parts)
    rows = head_weight.shape[0] // parts
    shard = lax.axis_index("dp")
    core = shard % CORES
    z, y = shard // (CORES * side), (shard // CORES) % side

    line = jnp.broadcast_to(
        head_weight.reshape(parts, 1, rows, width), (parts, side, rows, width)
    ).reshape(parts * side, rows, width)
    line = swap(line, ("dp", "mp"), first).reshape(parts, side, rows, width)
    line = line.transpose(1, 2, 0, 3).reshape(side * rows, parts * width)

    position = jnp.where(core == 0, z, y)
    halves = (line[: side * rows // 2], line[side * rows // 2 :])
    states = jnp.concatenate([query_states, passage_states], axis=0)
    states, *halves = lax.optimization_barrier((states, *halves))
    states = from_all(states, "mp")
    own_blocks = [], []
    other_arrays = []
    held = halves
    for step in range(BLOCKS):
        came = [
            lax.ppermute(held[stream], "dp", matchings[(step + stream) % 2])
            for stream in range(2)
        ]
        if step == 0:
            came = lax.optimization_barrier(came)
            for stream in range(2):
                is_lower = (position + stream) % 2 == 0
                half, other = halves[stream], came[stream]
                came[stream] = jnp.concatenate(
                    [jnp.where(is_lower, half, other), jnp.where(is_lower, other, half)], axis=0
                )
        else:
            (*came, other_arrays) = lax.optimization_barrier((*came, other_arrays))
            other_arrays += [lax.ppermute(block, "dp", other_core) for block in held]
        for stream in range(2):
            own_blocks[stream].append(came[stream])
        held = came
    other_arrays += [lax.ppermute(block, "dp", other_core) for block in held]
    own_arrays = [blocks[step] for step in range(BLOCKS) for blocks in own_blocks]

    def places_of(position):
        out = []
        for move in (lambda up: 0, lambda up: 2 * up - 1, lambda up: 1 - 2 * up, lambda up: 2):
            for stream in range(2):
                at = position + stream
                out.append((at // 2 + move(at % 2)) % BLOCKS)
        return jnp.stack(out).astype(jnp.int32)

    own_places = places_of(position)
    other_places = places_of(jnp.where(core == 0, y, z))

    block = negatives.reshape(-1)
    order = jnp.arange(pairs, dtype=jnp.int32)
    earlier = (block[:, None] == block[None, :]) & (order[None, :] < order[:, None])
    slot = block * CAPACITY + jnp.sum(earlier.astype(jnp.int32), axis=1)
    slots = shards * CAPACITY
    in_slot = jnp.arange(slots, dtype=jnp.int32)[:, None] == slot[None, :]
    to_slot = in_slot.astype(BF16)
    positive_mask = (positives[:, None] == order[None, :]).astype(F32)

    def in_order(own, other):
        return jnp.where(core == 0, own, other), jnp.where(core == 0, other, own)

    weight_own, projected_own, squares = project(own_places, states, own_arrays)
    weight_other, projected_other, more = project(other_places, states, other_arrays)
    squares = squares + more
    projected = jnp.concatenate(in_order(projected_own, projected_other), axis=1)
    squares = sum_all(squares.reshape(-1, math.gcd(128, 2 * pairs)), "mp").reshape(-1)
    inverse = lax.rsqrt(squares[:, None] + EPSILON)
    embedded = (projected * inverse).astype(BF16)
    query, passage = embedded[:pairs], embedded[pairs:]
    part = query.shape[1]

    def exchange(message):
        columns_each = message.shape[1]
        message = message.reshape(shards, CAPACITY, columns_each)
        return swap(message, "dp").reshape(slots, columns_each)

    arrived = exchange(dot(to_slot, query).astype(BF16))

    scores = jnp.concatenate([arrived, query], axis=0)
    scores = sum_all(dot(scores, passage, LAST_BOTH), "mp")
    exps = jnp.exp(SCORE_SCALE * scores)
    hard_scores, local_scores = scores[:slots], scores[slots:]
    hard_exp, local_exp = exps[:slots], exps[slots:]
    sums = jnp.sum(exps, axis=1)
    hard_totals, local_totals = sums[:slots], sums[slots:]

    scale = GRADIENT_SCALE / hard_totals
    rounded_exp = hard_exp.astype(BF16)
    hard_radial = jnp.sum(rounded_exp.astype(F32) * hard_scores, axis=1) * scale
    hard_sums = (scale[:, None] * dot(rounded_exp, passage)).astype(BF16)
    totals_out = jnp.sum(jnp.where(in_slot, local_totals[None, :], 0.0), axis=1)
    back = columns(parts_of(hard_totals, 3) + parts_of(hard_radial, 3) + parts_of(totals_out, 3))
    back = exchange(jnp.concatenate([hard_sums, back], axis=1))
    slot_totals = jnp.sum(back[:, part + 6 : part + 9].astype(F32), axis=1) + hard_totals
    back = dot(to_slot, back, FIRST_BOTH)
    hard_coef = ((GRADIENT_SCALE * hard_exp) / slot_totals[:, None]).astype(BF16)

    query_hard_totals = jnp.sum(back[:, part : part + 3], axis=1)
    totals = local_totals + query_hard_totals
    share = (query_hard_totals / totals)[:, None]
    local_coef = (
        GRADIENT_SCALE * (local_exp / totals[:, None] - positive_mask)
    ).astype(BF16)
    weighted_scores = local_coef.astype(F32) * local_scores

    query_grad = dot(local_coef, passage) + share * back[:, :part]
    query_radial = jnp.sum(weighted_scores, axis=1) + share[:, 0] * jnp.sum(
        back[:, part + 3 : part + 6], axis=1
    )
    passage_grad = dot(local_coef, query, FIRST_BOTH) + dot(hard_coef, arrived, FIRST_BOTH)
    passage_radial = jnp.sum(weighted_scores, axis=0) + jnp.sum(
        hard_coef.astype(F32) * hard_scores, axis=0
    )
    grad = jnp.concatenate([query_grad, passage_grad], axis=0)
    radial = jnp.concatenate([query_radial, passage_radial], axis=0)[:, None]
    proj_grad = (inverse * grad - projected * (inverse * inverse * radial)).astype(BF16)
    half = part // 2
    grad_own, grad_other = in_order(proj_grad[:, :half], proj_grad[:, half:])
    partial = spread(grad_own, grad_other, weight_own, weight_other, parts)
    state_grad = jnp.sum(swap(partial, "mp").astype(F32), axis=0)
    return (state_grad[:pairs], state_grad[pairs:])


def solution(mesh):
    in_specs = (P("dp", "mp"), P("dp", "mp"), P("dp", "mp"), P("dp"), P("dp", None))
    out_specs = (P("dp", "mp"), P("dp", "mp"))
    return jax.shard_map(
        on_device, mesh=mesh, in_specs=in_specs, out_specs=out_specs, check_vma=False
    )
```

time: 266 us -> 237 us (0.89)
  waiting for transfers between devices: 107 us -> 47.3 us
  starting transfers between devices: 26.6 us -> 81.8 us
  blocking collectives: 89.7 us -> 71.6 us
  Pallas kernels: 0 us -> 16.8 us
  between operations: 14.4 us -> 1.79 us
  matrix products: 15 us -> 3.31 us
    ppermute x1 -> x16, starting transfers between devices: 6.92 us -> 49.4 us  [the longest x8 25.8 us: on_device(): lax.ppermute(held[stream], 'dp', matchings[(step + stream) % 2])]
    all_gather x1 -> x0, waiting for transfers between devices: 39.9 us -> none  [on_device(): lax.all_gather(line, 'dp', axis=0, tiled=True, axis_index_groups=second)]
    all_to_all x5 -> x4, waiting for transfers between devices: 67 us -> 34.9 us  [swap(): lax.all_to_all(x, axis, split_axis=0, concat_axis=0, tiled=True, axis_ind...]
    all_to_all x3, blocking collectives: 89.7 us -> 71.6 us  [swap(): lax.all_to_all(x, axis, split_axis=0, concat_axis=0, tiled=True, axis_ind...]
    pallas_call x0 -> x3, Pallas kernels: none -> 16.8 us  [the longest x2 12.3 us: project(): pl.pallas_call(project_kernel, out_shape=(jax.ShapeDtypeStruct((width, de...]
    all_to_all x5 -> x4, starting transfers between devices: 19.7 us -> 32.4 us  [swap(): lax.all_to_all(x, axis, split_axis=0, concat_axis=0, tiled=True, axis_ind...]
    ppermute x1 -> x16, waiting for transfers between devices: 0.01 us -> 12.4 us  [the longest x8 12.4 us: on_device(): lax.ppermute(held[stream], 'dp', matchings[(step + stream) % 2])]
    dot_general x12 -> x7, matrix products: 15 us -> 3.31 us  [dot(): return lax.dot_general(a, b, dims, preferred_element_type=F32)]
  transfers between devices with their start and end apart: 7 -> 20, of which waited for: 6 -> 8; matrix products, arithmetic and copies ran while one was open for 2% -> 1% of each run, Pallas kernels for 0% -> 3%
where the time goes in v4:
time: 237 us; the launch traced here: 235 us
  starting transfers between devices  81.8 us (35%)
  blocking collectives  71.6 us (30%)
  waiting for transfers between devices  47.3 us (20%)
  Pallas kernels  16.8 us (7%)
  local copies, waits for them, and re-layouts  9.18 us (4%)
  other arithmetic  3.61 us (2%)
  matrix products  3.31 us (1%)
    all_to_all x3, blocking collectives, swap(): lax.all_to_all(x, axis, split_axis=0, concat_axis=0, tiled=True, axis_ind...  71.6 us
    all_to_all x4, waiting for transfers between devices, swap(): lax.all_to_all(x, axis, split_axis=0, concat_axis=0, tiled=True, axis_ind...  34.9 us
    all_to_all x4, starting transfers between devices, swap(): lax.all_to_all(x, axis, split_axis=0, concat_axis=0, tiled=True, axis_ind...  32.4 us
    ppermute x8, starting transfers between devices, on_device(): lax.ppermute(held[stream], 'dp', matchings[(step + stream) % 2])  25.8 us
    ppermute x8, starting transfers between devices, on_device(): other_arrays += [lax.ppermute(block, 'dp', other_core) for block in held]  23.6 us
    ppermute x8, waiting for transfers between devices, on_device(): lax.ppermute(held[stream], 'dp', matchings[(step + stream) % 2])  12.4 us
    pallas_call x2, Pallas kernels, project(): pl.pallas_call(project_kernel, out_shape=(jax.ShapeDtypeStruct((width, de...  12.3 us
  transfers between devices with their start and end apart: 20, of which 8 were waited for; matrix products, arithmetic and copies ran while one was open for 1% of the time, Pallas kernels for 3%

profile of v4, /device:TPU:1, one launch (start us, length us, event | category | flops | bytes accessed | tf_op | source)
XLA Modules:
  0.0 235.4 jit_solution(13125613844881137077)
XLA Ops:
  2.3 13.7 %all-to-all-start = ((bf16[32,8,1024]{2,1,0:T(8,128)(2,1)}), bf16[32,8,1024]{2,1,0:T(8,128)(2,1)S(1)}, u32[]{:S(2)}, u32[]{:S(2)}) async-start(bf16[32,8,1024]{2,1,0:T(8,128)(2,1)} %bitcast.9), calls=%async_computation | async-start | bytes 1048576 | tf_op jit(solution)/shard_map/all_to_all | solution.py:28
  17.1 10.3 %all-to-all-done = bf16[32,8,1024]{2,1,0:T(8,128)(2,1)S(1)} async-done(((bf16[32,8,1024]{2,1,0:T(8,128)(2,1)}), bf16[32,8,1024]{2,1,0:T(8,128)(2,1)S(1)}, u32[]{:S(2)}, u32[]{:S(2)}) %all-to-all-start) | async-done | bytes 524320 | tf_op jit(solution)/shard_map/all_to_all | solution.py:28
  27.5 3.2 %collective-permute-start = (bf16[32,4096]{1,0:T(8,128)(2,1)S(1)}, bf16[32,4096]{1,0:T(8,128)(2,1)S(1)}, u32[]{:S(2)}, u32[]{:S(2)}) collective-permute-start(bf16[32,4096]{1,0:T(8,128)(2,1)S(1)} %bitcast.36), channel_id=1, source_target_pairs={{0,64},{4,12},{8,72},{12,4},{16,80},{20,28},{24,88},{28,20},{32,96... | collective-permute-start | bytes 786440 | tf_op jit(solution)/shard_map/ppermute | solution.py:202
  30.7 4.9 %collective-permute-start.1 = (bf16[32,4096]{1,0:T(8,128)(2,1)S(1)}, bf16[32,4096]{1,0:T(8,128)(2,1)S(1)}, u32[]{:S(2)}, u32[]{:S(2)}) collective-permute-start(bf16[32,4096]{1,0:T(8,128)(2,1)S(1)} %bitcast.38), channel_id=1, source_target_pairs={{0,448},{4,60},{8,456},{12,20},{16,464},{20,12},{24,472},{28,36},{... | collective-permute-start | bytes 786440 | tf_op jit(solution)/shard_map/ppermute | solution.py:202
  35.7 3.6 %collective-permute-done.1 = bf16[32,4096]{1,0:T(8,128)(2,1)S(1)} collective-permute-done((bf16[32,4096]{1,0:T(8,128)(2,1)S(1)}, bf16[32,4096]{1,0:T(8,128)(2,1)S(1)}, u32[]{:S(2)}, u32[]{:S(2)}) %collective-permute-start.1) | collective-permute-done | bytes 262176 | tf_op jit(solution)/shard_map/ppermute | solution.py:202
  41.4 4.9 %collective-permute-start.2 = (bf16[64,4096]{1,0:T(8,128)(2,1)S(1)}, bf16[64,4096]{1,0:T(8,128)(2,1)S(1)}, u32[]{:S(2)}, u32[]{:S(2)}) collective-permute-start(bf16[64,4096]{1,0:T(8,128)(2,1)S(1)} %pad_maximum_fusion.2.refs_0_), channel_id=1, source_target_pairs={{0,448},{4,60},{8,456},{12,20},{16,464},{20,12},{24,472},{28,36},{... | collective-permute-start | bytes 1572872 | tf_op jit(solution)/shard_map/ppermute | solution.py:202
  47.9 4.6 %all-to-all-start.1 = ((bf16[4,256,1024]{2,1,0:T(8,128)(2,1)}), bf16[4,256,1024]{2,1,0:T(8,128)(2,1)}, u32[]{:S(2)}, u32[]{:S(2)}) async-start(bf16[4,256,1024]{2,1,0:T(8,128)(2,1)} %broadcast_in_dim.22), calls=%async_computation.1 | async-start | bytes 4194304 | tf_op jit(solution)/shard_map/all_to_all | solution.py:28
  52.6 7.2 %collective-permute-start.7 = (bf16[64,4096]{1,0:T(8,128)(2,1)S(1)}, bf16[64,4096]{1,0:T(8,128)(2,1)S(1)}, u32[]{:S(2)}, u32[]{:S(2)}) collective-permute-start(bf16[64,4096]{1,0:T(8,128)(2,1)S(1)} %pad_maximum_fusion.3.refs_1_), channel_id=1, source_target_pairs={{0,4},{4,0},{8,12},{12,8},{16,20},{20,16},{24,28},{28,24},{32,36},... | collective-permute-start | bytes 1572872 | tf_op jit(solution)/shard_map/ppermute | solution.py:215
  61.8 4.3 %collective-permute-start.4 = (bf16[64,4096]{1,0:T(8,128)(2,1)S(1)}, bf16[64,4096]{1,0:T(8,128)(2,1)}, u32[]{:S(2)}, u32[]{:S(2)}) collective-permute-start(bf16[64,4096]{1,0:T(8,128)(2,1)S(1)} %collective-permute-done.2.refs_2_), channel_id=1, source_target_pairs={{0,64},{4,12},{8,72},{12,4},{16,80},{20,28},{24,88},{28,20},{32,96... | collective-permute-start | bytes 1572872 | tf_op jit(solution)/shard_map/ppermute | solution.py:202
  70.4 2.4 %collective-permute-start.11 = (bf16[64,4096]{1,0:T(8,128)(2,1)S(1)}, bf16[64,4096]{1,0:T(8,128)(2,1)S(1)}, u32[]{:S(2)}, u32[]{:S(2)}) collective-permute-start(bf16[64,4096]{1,0:T(8,128)(2,1)S(1)} %collective-permute-done.3.refs_3_), channel_id=1, source_target_pairs={{0,4},{4,0},{8,12},{12,8},{16,20},{20,16},{24,28},{28,24},{32,36},... | collective-permute-start | bytes 1572872 | tf_op jit(solution)/shard_map/ppermute | solution.py:215
  73.1 4.6 %collective-permute-done.5.refs_5_ = bf16[64,4096]{1,0:T(8,128)(2,1)} collective-permute-done((bf16[64,4096]{1,0:T(8,128)(2,1)S(1)}, bf16[64,4096]{1,0:T(8,128)(2,1)}, u32[]{:S(2)}, u32[]{:S(2)}) %collective-permute-start.5) | collective-permute-done | bytes 524320 | tf_op jit(solution)/shard_map/ppermute | solution.py:202
  81.9 2.7 %collective-permute-start.12 = (bf16[64,4096]{1,0:T(8,128)(2,1)}, bf16[64,4096]{1,0:T(8,128)(2,1)}, u32[]{:S(2)}, u32[]{:S(2)}) collective-permute-start(bf16[64,4096]{1,0:T(8,128)(2,1)} %collective-permute-done.4.refs_4_), channel_id=1, source_target_pairs={{0,4},{4,0},{8,12},{12,8},{16,20},{20,16},{24,28},{28,24},{32,36},... | collective-permute-start | bytes 1572872 | tf_op jit(solution)/shard_map/ppermute | solution.py:215
  86.6 2.4 %collective-permute-done.8.refs_6_ = bf16[64,4096]{1,0:T(8,128)(2,1)} collective-permute-done((bf16[64,4096]{1,0:T(8,128)(2,1)}, bf16[64,4096]{1,0:T(8,128)(2,1)}, u32[]{:S(2)}, u32[]{:S(2)}) %collective-permute-start.8) | collective-permute-done | bytes 524320 | tf_op jit(solution)/shard_map/ppermute | solution.py:202
  90.5 3.6 %collective-permute-start.14 = (bf16[64,4096]{1,0:T(8,128)(2,1)}, bf16[64,4096]{1,0:T(8,128)(2,1)}, u32[]{:S(2)}, u32[]{:S(2)}) collective-permute-start(bf16[64,4096]{1,0:T(8,128)(2,1)} %collective-permute-done.8.refs_6_), channel_id=1, source_target_pairs={{0,4},{4,0},{8,12},{12,8},{16,20},{20,16},{24,28},{28,24},{32,36},... | collective-permute-start | bytes 1572872 | tf_op jit(solution)/shard_map/ppermute | solution.py:219
  96.9 6.1 %shard_map.68 = (bf16[512,4096]{1,0:T(8,128)(2,1)}, f32[256,512]{1,0:T(8,128)S(1)}, f32[256,1]{1,0:T(8,128)S(1)}) custom-call(s32[8]{0:T(128)S(1)} %stack.86.places, bf16[4,256,1024]{2,1,0:T(8,128)(2,1)} %all-to-all-done.1.states, bf16[64,4096]{1,0:T(8,128)(2,1)S(1)} %pad_maximum_fusion.2.refs_0_, bf16[64,4096]{1,0:T(8,128)(2,1)S(1)} %pad_maximum_fusion.3.refs_1_, ...), custom_call_target="tpu_custom_call" | custom-call | flops 1073741824 | bytes 8388608 | tf_op jit(solution)/shard_map/pallas_call | solution.py:127
  103.0 6.1 %shard_map.69 = (bf16[512,4096]{1,0:T(8,128)(2,1)}, f32[256,512]{1,0:T(8,128)S(1)}, f32[256,1]{1,0:T(8,128)S(1)}) custom-call(s32[8]{0:T(128)S(1)} %stack.95.places, bf16[4,256,1024]{2,1,0:T(8,128)(2,1)} %all-to-all-done.1.states, bf16[64,4096]{1,0:T(8,128)(2,1)S(1)} %collective-permute-done.6.refs_0_, bf16[64,4096]{1,0:T(8,128)(2,1)S(1)} %collective-permute-done.7.refs_1_, ...), custom_call_target="tpu_custom_call" | custom-call | flops 1073741824 | bytes 8388608 | tf_op jit(solution)/shard_map/pallas_call | solution.py:127
  109.9 4.5 %all-to-all-start.2 = ((f32[4,2,128]{2,1,0:T(2,128)}), f32[4,2,128]{2,1,0:T(2,128)S(1)}, u32[]{:S(2)}, u32[]{:S(2)}) async-start(f32[4,2,128]{2,1,0:T(2,128)} %broadcast_in_dim.24), calls=%async_computation.2 | async-start | bytes 8192 | tf_op jit(solution)/shard_map/all_to_all | solution.py:28
  114.5 4.0 %all-to-all-done.2 = f32[4,2,128]{2,1,0:T(2,128)S(1)} async-done(((f32[4,2,128]{2,1,0:T(2,128)}), f32[4,2,128]{2,1,0:T(2,128)S(1)}, u32[]{:S(2)}, u32[]{:S(2)}) %all-to-all-start.2) | async-done | bytes 4128 | tf_op jit(solution)/shard_map/all_to_all | solution.py:28
  120.0 9.6 %all-to-all-start.3 = ((bf16[128,2,1024]{2,1,0:T(2,128)(2,1)}), bf16[128,2,1024]{2,1,0:T(2,128)(2,1)S(1)}, u32[]{:S(2)}, u32[]{:S(2)}) async-start(bf16[128,2,1024]{2,1,0:T(2,128)(2,1)} %reshape.120), calls=%async_computation.3 | async-start | bytes 1048576 | tf_op jit(solution)/shard_map/all_to_all | solution.py:28
  129.6 20.6 %all-to-all-done.3 = bf16[128,2,1024]{2,1,0:T(2,128)(2,1)S(1)} async-done(((bf16[128,2,1024]{2,1,0:T(2,128)(2,1)}), bf16[128,2,1024]{2,1,0:T(2,128)(2,1)S(1)}, u32[]{:S(2)}, u32[]{:S(2)}) %all-to-all-start.3) | async-done | bytes 524320 | tf_op jit(solution)/shard_map/all_to_all | solution.py:28
  151.2 15.2 %all_to_all.35 = f32[4,384,128]{2,1,0:T(8,128)S(1)} all-to-all(f32[4,384,128]{2,1,0:T(8,128)S(1)} %broadcast_in_dim.25), channel_id=1, replica_groups=mesh['dp'=128,'mp'=4] {'mp'}, dimensions={0} | all-to-all | bytes 1572864 | tf_op jit(solution)/shard_map/all_to_all | solution.py:28
  167.7 27.2 %all_to_all.36 = bf16[128,2,1152]{2,1,0:T(2,128)(2,1)S(1)} all-to-all(bf16[128,2,1152]{2,1,0:T(2,128)(2,1)S(1)} %reshape.122), channel_id=1, replica_groups=mesh['dp'=128,'mp'=4] {'dp'}, dimensions={0} | all-to-all | bytes 1179648 | tf_op jit(solution)/shard_map/all_to_all | solution.py:28
  200.2 4.5 %shard_map.70 = bf16[4,256,1024]{2,1,0:T(8,128)(2,1)S(1)} custom-call(bf16[256,512]{1,0:T(8,128)(2,1)S(1)} %get-tuple-element.62.grad_own, bf16[256,512]{1,0:T(8,128)(2,1)S(1)} %get-tuple-element.61.grad_other, bf16[512,4096]{1,0:T(8,128)(2,1)S(1)} %copy-done, bf16[512,4096]{1,0:T(8,128)(2,1)S(1)} %copy-done.1), custom_call_target="tpu_custom_call" | custom-call | flops 2147483648 | bytes 8388608 | tf_op jit(solution)/shard_map/pallas_call | solution.py:160
  204.8 29.2 %all_to_all.37 = bf16[4,256,1024]{2,1,0:T(8,128)(2,1)S(1)} all-to-all(bf16[4,256,1024]{2,1,0:T(8,128)(2,1)S(1)} %shard_map.70), channel_id=1, replica_groups=mesh['dp'=128,'mp'=4] {'mp'}, dimensions={0} | all-to-all | bytes 4194304 | tf_op jit(solution)/shard_map/all_to_all | solution.py:28
  (102 shorter events, 34.1 us)
Async XLA Ops:
  2.3 25.1 %all-to-all-start = ((bf16[32,8,1024]{2,1,0:T(8,128)(2,1)}), bf16[32,8,1024]{2,1,0:T(8,128)(2,1)S(1)}, u32[]{:S(2)}, u32[]{:S(2)}) async-start(bf16[32,8,1024]{2,1,0:T(8,128)(2,1)} %bitcast.9), calls=%async_computation | async-start | bytes 1048576 | tf_op jit(solution)/shard_map/all_to_all | solution.py:28
  27.5 8.2 %collective-permute-start = (bf16[32,4096]{1,0:T(8,128)(2,1)S(1)}, bf16[32,4096]{1,0:T(8,128)(2,1)S(1)}, u32[]{:S(2)}, u32[]{:S(2)}) collective-permute-start(bf16[32,4096]{1,0:T(8,128)(2,1)S(1)} %bitcast.36), channel_id=1, source_target_pairs={{0,64},{4,12},{8,72},{12,4},{16,80},{20,28},{24,88},{28,20},{32,96... | collective-permute-start | bytes 786440 | tf_op jit(solution)/shard_map/ppermute | solution.py:202
  30.7 8.6 %collective-permute-start.1 = (bf16[32,4096]{1,0:T(8,128)(2,1)S(1)}, bf16[32,4096]{1,0:T(8,128)(2,1)S(1)}, u32[]{:S(2)}, u32[]{:S(2)}) collective-permute-start(bf16[32,4096]{1,0:T(8,128)(2,1)S(1)} %bitcast.38), channel_id=1, source_target_pairs={{0,448},{4,60},{8,456},{12,20},{16,464},{20,12},{24,472},{28,36},{... | collective-permute-start | bytes 786440 | tf_op jit(solution)/shard_map/ppermute | solution.py:202
  39.5 22.3 %collective-permute-start.3 = (bf16[64,4096]{1,0:T(8,128)(2,1)S(1)}, bf16[64,4096]{1,0:T(8,128)(2,1)S(1)}, u32[]{:S(2)}, u32[]{:S(2)}) collective-permute-start(bf16[64,4096]{1,0:T(8,128)(2,1)S(1)} %pad_maximum_fusion.3.refs_1_), channel_id=1, source_target_pairs={{0,64},{4,12},{8,72},{12,4},{16,80},{20,28},{24,88},{28,20},{32,96... | collective-permute-start | bytes 1572872 | tf_op jit(solution)/shard_map/ppermute | solution.py:202
  41.4 20.3 %collective-permute-start.2 = (bf16[64,4096]{1,0:T(8,128)(2,1)S(1)}, bf16[64,4096]{1,0:T(8,128)(2,1)S(1)}, u32[]{:S(2)}, u32[]{:S(2)}) collective-permute-start(bf16[64,4096]{1,0:T(8,128)(2,1)S(1)} %pad_maximum_fusion.2.refs_0_), channel_id=1, source_target_pairs={{0,448},{4,60},{8,456},{12,20},{16,464},{20,12},{24,472},{28,36},{... | collective-permute-start | bytes 1572872 | tf_op jit(solution)/shard_map/ppermute | solution.py:202
  47.9 48.7 %copy-start.8 = (s32[128,1]{0,1:T(1,128)S(1)}, s32[128,1]{0,1:T(1,128)}, u32[]{:S(2)}) copy-start(s32[128,1]{0,1:T(1,128)} %param.9) | copy-start | bytes 1540
  47.9 48.9 %all-to-all-start.1 = ((bf16[4,256,1024]{2,1,0:T(8,128)(2,1)}), bf16[4,256,1024]{2,1,0:T(8,128)(2,1)}, u32[]{:S(2)}, u32[]{:S(2)}) async-start(bf16[4,256,1024]{2,1,0:T(8,128)(2,1)} %broadcast_in_dim.22), calls=%async_computation.1 | async-start | bytes 4194304 | tf_op jit(solution)/shard_map/all_to_all | solution.py:28
  52.6 17.9 %collective-permute-start.7 = (bf16[64,4096]{1,0:T(8,128)(2,1)S(1)}, bf16[64,4096]{1,0:T(8,128)(2,1)S(1)}, u32[]{:S(2)}, u32[]{:S(2)}) collective-permute-start(bf16[64,4096]{1,0:T(8,128)(2,1)S(1)} %pad_maximum_fusion.3.refs_1_), channel_id=1, source_target_pairs={{0,4},{4,0},{8,12},{12,8},{16,20},{20,16},{24,28},{28,24},{32,36},... | collective-permute-start | bytes 1572872 | tf_op jit(solution)/shard_map/ppermute | solution.py:215
  59.8 13.0 %collective-permute-start.6 = (bf16[64,4096]{1,0:T(8,128)(2,1)S(1)}, bf16[64,4096]{1,0:T(8,128)(2,1)S(1)}, u32[]{:S(2)}, u32[]{:S(2)}) collective-permute-start(bf16[64,4096]{1,0:T(8,128)(2,1)S(1)} %pad_maximum_fusion.2.refs_0_), channel_id=1, source_target_pairs={{0,4},{4,0},{8,12},{12,8},{16,20},{20,16},{24,28},{28,24},{32,36},... | collective-permute-start | bytes 1572872 | tf_op jit(solution)/shard_map/ppermute | solution.py:215
  61.7 35.1 %copy-start.3 = (bf16[64,4096]{1,0:T(8,128)(2,1)}, bf16[64,4096]{1,0:T(8,128)(2,1)S(1)}, u32[]{:S(2)}) copy-start(bf16[64,4096]{1,0:T(8,128)(2,1)S(1)} %collective-permute-done.3.refs_3_) | copy-start | bytes 1572868
  61.8 35.1 %copy-start.4 = (bf16[64,4096]{1,0:T(8,128)(2,1)}, bf16[64,4096]{1,0:T(8,128)(2,1)S(1)}, u32[]{:S(2)}) copy-start(bf16[64,4096]{1,0:T(8,128)(2,1)S(1)} %collective-permute-done.2.refs_2_) | copy-start | bytes 1572868
  61.8 11.3 %collective-permute-start.4 = (bf16[64,4096]{1,0:T(8,128)(2,1)S(1)}, bf16[64,4096]{1,0:T(8,128)(2,1)}, u32[]{:S(2)}, u32[]{:S(2)}) collective-permute-start(bf16[64,4096]{1,0:T(8,128)(2,1)S(1)} %collective-permute-done.2.refs_2_), channel_id=1, source_target_pairs={{0,64},{4,12},{8,72},{12,4},{16,80},{20,28},{24,88},{28,20},{32,96... | collective-permute-start | bytes 1572872 | tf_op jit(solution)/shard_map/ppermute | solution.py:202
  66.1 11.5 %collective-permute-start.5 = (bf16[64,4096]{1,0:T(8,128)(2,1)S(1)}, bf16[64,4096]{1,0:T(8,128)(2,1)}, u32[]{:S(2)}, u32[]{:S(2)}) collective-permute-start(bf16[64,4096]{1,0:T(8,128)(2,1)S(1)} %collective-permute-done.3.refs_3_), channel_id=1, source_target_pairs={{0,448},{4,60},{8,456},{12,20},{16,464},{20,12},{24,472},{28,36},{... | collective-permute-start | bytes 1572872 | tf_op jit(solution)/shard_map/ppermute | solution.py:202
  68.5 16.2 %collective-permute-start.10 = (bf16[64,4096]{1,0:T(8,128)(2,1)S(1)}, bf16[64,4096]{1,0:T(8,128)(2,1)S(1)}, u32[]{:S(2)}, u32[]{:S(2)}) collective-permute-start(bf16[64,4096]{1,0:T(8,128)(2,1)S(1)} %collective-permute-done.2.refs_2_), channel_id=1, source_target_pairs={{0,4},{4,0},{8,12},{12,8},{16,20},{20,16},{24,28},{28,24},{32,36},... | collective-permute-start | bytes 1572872 | tf_op jit(solution)/shard_map/ppermute | solution.py:215
  70.4 16.2 %collective-permute-start.11 = (bf16[64,4096]{1,0:T(8,128)(2,1)S(1)}, bf16[64,4096]{1,0:T(8,128)(2,1)S(1)}, u32[]{:S(2)}, u32[]{:S(2)}) collective-permute-start(bf16[64,4096]{1,0:T(8,128)(2,1)S(1)} %collective-permute-done.3.refs_3_), channel_id=1, source_target_pairs={{0,4},{4,0},{8,12},{12,8},{16,20},{20,16},{24,28},{28,24},{32,36},... | collective-permute-start | bytes 1572872 | tf_op jit(solution)/shard_map/ppermute | solution.py:215
  77.6 11.4 %collective-permute-start.8 = (bf16[64,4096]{1,0:T(8,128)(2,1)}, bf16[64,4096]{1,0:T(8,128)(2,1)}, u32[]{:S(2)}, u32[]{:S(2)}) collective-permute-start(bf16[64,4096]{1,0:T(8,128)(2,1)} %collective-permute-done.4.refs_4_), channel_id=1, source_target_pairs={{0,448},{4,60},{8,456},{12,20},{16,464},{20,12},{24,472},{28,36},{... | collective-permute-start | bytes 1572872 | tf_op jit(solution)/shard_map/ppermute | solution.py:202
  80.0 10.5 %collective-permute-start.9 = (bf16[64,4096]{1,0:T(8,128)(2,1)}, bf16[64,4096]{1,0:T(8,128)(2,1)}, u32[]{:S(2)}, u32[]{:S(2)}) collective-permute-start(bf16[64,4096]{1,0:T(8,128)(2,1)} %collective-permute-done.5.refs_5_), channel_id=1, source_target_pairs={{0,64},{4,12},{8,72},{12,4},{16,80},{20,28},{24,88},{28,20},{32,96... | collective-permute-start | bytes 1572872 | tf_op jit(solution)/shard_map/ppermute | solution.py:202
  81.9 21.1 %collective-permute-start.12 = (bf16[64,4096]{1,0:T(8,128)(2,1)}, bf16[64,4096]{1,0:T(8,128)(2,1)}, u32[]{:S(2)}, u32[]{:S(2)}) collective-permute-start(bf16[64,4096]{1,0:T(8,128)(2,1)} %collective-permute-done.4.refs_4_), channel_id=1, source_target_pairs={{0,4},{4,0},{8,12},{12,8},{16,20},{20,16},{24,28},{28,24},{32,36},... | collective-permute-start | bytes 1572872 | tf_op jit(solution)/shard_map/ppermute | solution.py:215
  84.7 18.3 %collective-permute-start.13 = (bf16[64,4096]{1,0:T(8,128)(2,1)}, bf16[64,4096]{1,0:T(8,128)(2,1)}, u32[]{:S(2)}, u32[]{:S(2)}) collective-permute-start(bf16[64,4096]{1,0:T(8,128)(2,1)} %collective-permute-done.5.refs_5_), channel_id=1, source_target_pairs={{0,4},{4,0},{8,12},{12,8},{16,20},{20,16},{24,28},{28,24},{32,36},... | collective-permute-start | bytes 1572872 | tf_op jit(solution)/shard_map/ppermute | solution.py:215
  90.5 12.5 %collective-permute-start.14 = (bf16[64,4096]{1,0:T(8,128)(2,1)}, bf16[64,4096]{1,0:T(8,128)(2,1)}, u32[]{:S(2)}, u32[]{:S(2)}) collective-permute-start(bf16[64,4096]{1,0:T(8,128)(2,1)} %collective-permute-done.8.refs_6_), channel_id=1, source_target_pairs={{0,4},{4,0},{8,12},{12,8},{16,20},{20,16},{24,28},{28,24},{32,36},... | collective-permute-start | bytes 1572872 | tf_op jit(solution)/shard_map/ppermute | solution.py:219
  94.1 8.9 %collective-permute-start.15 = (bf16[64,4096]{1,0:T(8,128)(2,1)}, bf16[64,4096]{1,0:T(8,128)(2,1)}, u32[]{:S(2)}, u32[]{:S(2)}) collective-permute-start(bf16[64,4096]{1,0:T(8,128)(2,1)} %collective-permute-done.9.refs_7_), channel_id=1, source_target_pairs={{0,4},{4,0},{8,12},{12,8},{16,20},{20,16},{24,28},{28,24},{32,36},... | collective-permute-start | bytes 1572872 | tf_op jit(solution)/shard_map/ppermute | solution.py:219
  109.9 8.6 %all-to-all-start.2 = ((f32[4,2,128]{2,1,0:T(2,128)}), f32[4,2,128]{2,1,0:T(2,128)S(1)}, u32[]{:S(2)}, u32[]{:S(2)}) async-start(f32[4,2,128]{2,1,0:T(2,128)} %broadcast_in_dim.24), calls=%async_computation.2 | async-start | bytes 8192 | tf_op jit(solution)/shard_map/all_to_all | solution.py:28
  120.0 30.2 %all-to-all-start.3 = ((bf16[128,2,1024]{2,1,0:T(2,128)(2,1)}), bf16[128,2,1024]{2,1,0:T(2,128)(2,1)S(1)}, u32[]{:S(2)}, u32[]{:S(2)}) async-start(bf16[128,2,1024]{2,1,0:T(2,128)(2,1)} %reshape.120), calls=%async_computation.3 | async-start | bytes 1048576 | tf_op jit(solution)/shard_map/all_to_all | solution.py:28
  195.4 3.2 %copy-start.1 = (bf16[512,4096]{1,0:T(8,128)(2,1)S(1)}, bf16[512,4096]{1,0:T(8,128)(2,1)}, u32[]{:S(2)}) copy-start(bf16[512,4096]{1,0:T(8,128)(2,1)} %get-tuple-element.47.weight_other) | copy-start | bytes 12582916
  (5 other events, 10.0 us)

commit v5 on v4

--- a/solution.py
+++ b/solution.py
@@ -80,71 +80,74 @@
     return side, first, (swaps(0), swaps(1)), other_core
 
 
-def project_kernel(places, states, *refs):
-    arrays, (weight_out, projected, squares, weight, sems) = refs[:-5], refs[-5:]
-    rows = weight.shape[0] // (2 * BLOCKS)
-    tile, width = rows * BLOCKS, states.shape[2]
-    copies, count = ([], []), 0
-    for array, streams in zip(arrays, block_streams(len(arrays))):
-        for i, stream in enumerate(streams):
-            at = pl.multiple_of(stream * tile + places[count] * rows, rows)
-            copy = pltpu.make_async_copy(
-                array.at[pl.ds(i * rows, rows)], weight.at[pl.ds(at, rows)], sems.at[count]
-            )
-            copy.start()
-            copies[stream].append(copy)
-            count += 1
-    total = jnp.zeros(squares.shape, F32)
-    outs = []
-    for stream in range(2):
-        for copy in copies[stream]:
-            copy.wait()
-        at = pl.ds(stream * tile, tile)
-        outs.append(
-            pltpu.make_async_copy(weight.at[at], weight_out.at[at], sems.at[count + stream])
-        )
-        outs[-1].start()
-        value = dot(states[0], weight[at, :width], LAST_BOTH)
-        for part in range(1, states.shape[0]):
-            columns_at = pl.ds(part * width, width)
-            value = value + dot(states[part], weight[at, columns_at], LAST_BOTH)
-        projected[:, at] = value
-        total = total + jnp.sum(value * value, axis=1, keepdims=True)
-    squares[...] = total
-    for out in outs:
-        out.wait()
-
-
-def block_streams(arrays):
-    return [[0], [1]] * BLOCKS
-
-
-def project(places, states, arrays):
-    parts, rows, each = states.shape
-    depth = parts * each
-    width = sum(array.shape[0] for array in arrays)
-    vmem = pl.BlockSpec(memory_space=pltpu.VMEM)
+def place_kernel(places, *refs):
+    blocks, (weight, sems) = refs[:-2], refs[-2:]
+    rows = blocks[0].shape[0]
+    copies = []
+    for i, block in enumerate(blocks):
+        at = pl.multiple_of(places[i] * rows, rows)
+        copies.append(pltpu.make_async_copy(block, weight.at[pl.ds(at, rows)], sems.at[i]))
+        copies[-1].start()
+    for copy in copies:
+        copy.wait()
+
+
+def place(places, blocks):
+    rows, depth = blocks[0].shape
+    anywhere = pl.BlockSpec(memory_space=pl.ANY)
+    return pl.pallas_call(
+        place_kernel,
+        out_shape=jax.ShapeDtypeStruct((len(blocks) * rows, depth), BF16),
+        in_specs=[pl.BlockSpec(memory_space=pltpu.SMEM)] + [anywhere] * len(blocks),
+        out_specs=pl.BlockSpec(memory_space=pltpu.VMEM),
+        scratch_shapes=[pltpu.SemaphoreType.DMA((len(blocks),))],
+        compiler_params=pltpu.CompilerParams(vmem_limit_bytes=16 * 2**20),
+    )(places, *blocks)
+
+
+def project_kernel(states, weight, projected, squares):
+    value = dot(states[0], weight[:, : states.shape[2]], LAST_BOTH)
+    for part in range(1, states.shape[0]):
+        at = pl.ds(part * states.shape[2], states.shape[2])
+        value = value + dot(states[part], weight[:, at], LAST_BOTH)
+    projected[...] = value
+    total = jnp.sum(value * value, axis=1, keepdims=True)
+
+    @pl.when(pl.program_id(0) == 0)
+    def _():
+        squares[...] = total
+
+    @pl.when(pl.program_id(0) > 0)
+    def _():
+        squares[...] += total
+
+
+def project(states, weight):
+    parts, rows, _ = states.shape
+    width, depth = weight.shape
+    tile = min(256, width)
     return pl.pallas_call(
         project_kernel,
+        grid=(width // tile,),
         out_shape=(
-            jax.ShapeDtypeStruct((width, depth), BF16),
             jax.ShapeDtypeStruct((rows, width), F32),
             jax.ShapeDtypeStruct((rows, 1), F32),
         ),
-        in_specs=[pl.BlockSpec(memory_space=pltpu.SMEM), vmem]
-        + [pl.BlockSpec(memory_space=pl.ANY)] * len(arrays),
-        out_specs=(pl.BlockSpec(memory_space=pltpu.HBM), vmem, vmem),
-        scratch_shapes=[
-            pltpu.VMEM((width, depth), BF16),
-            pltpu.SemaphoreType.DMA((2 * BLOCKS + 2,)),
+        in_specs=[
+            pl.BlockSpec(states.shape, lambda n: (0, 0, 0)),
+            pl.BlockSpec((tile, depth), lambda n: (n, 0)),
         ],
-        compiler_params=pltpu.CompilerParams(vmem_limit_bytes=52 * 2**20),
+        out_specs=(
+            pl.BlockSpec((rows, tile), lambda n: (0, n)),
+            pl.BlockSpec((rows, 1), lambda n: (0, 0)),
+        ),
+        compiler_params=pltpu.CompilerParams(vmem_limit_bytes=24 * 2**20),
         cost_estimate=pl.CostEstimate(
             flops=2 * rows * depth * width,
-            bytes_accessed=4 * width * depth,
+            bytes_accessed=2 * width * depth,
             transcendentals=0,
         ),
-    )(places, states, *arrays)
+    )(states, weight)
 
 
 def spread_kernel(grad_own, grad_other, weight_own, weight_other, out):
@@ -155,7 +158,7 @@
 def spread(grad_own, grad_other, weight_own, weight_other, parts):
     rows, width = grad_own.shape
     columns_each = weight_own.shape[1] // parts
-    tile = min(512, columns_each)
+    tile = min(1024, columns_each)
     per_part = columns_each // tile
     return pl.pallas_call(
         spread_kernel,
@@ -194,41 +197,30 @@
     states = jnp.concatenate([query_states, passage_states], axis=0)
     states, *halves = lax.optimization_barrier((states, *halves))
     states = from_all(states, "mp")
-    own_blocks = [], []
-    other_arrays = []
+    blocks, places = [], []
     held = halves
     for step in range(BLOCKS):
         came = [
             lax.ppermute(held[stream], "dp", matchings[(step + stream) % 2])
             for stream in range(2)
         ]
-        if step == 0:
+        if step < BLOCKS - 1:
             came = lax.optimization_barrier(came)
-            for stream in range(2):
-                is_lower = (position + stream) % 2 == 0
+        else:
+            (*came, states) = lax.optimization_barrier((*came, states))
+        for stream in range(2):
+            at, is_upper = (position + stream) // 2, (position + stream) % 2
+            if step == 0:
                 half, other = halves[stream], came[stream]
                 came[stream] = jnp.concatenate(
-                    [jnp.where(is_lower, half, other), jnp.where(is_lower, other, half)], axis=0
+                    [jnp.where(is_upper, other, half), jnp.where(is_upper, half, other)], axis=0
                 )
-        else:
-            (*came, other_arrays) = lax.optimization_barrier((*came, other_arrays))
-            other_arrays += [lax.ppermute(block, "dp", other_core) for block in held]
-        for stream in range(2):
-            own_blocks[stream].append(came[stream])
+            move = (0, 2 * is_upper - 1, 1 - 2 * is_upper, 2)[step]
+            places.append(stream * BLOCKS + (at + move) % BLOCKS)
+        blocks += came
         held = came
-    other_arrays += [lax.ppermute(block, "dp", other_core) for block in held]
-    own_arrays = [blocks[step] for step in range(BLOCKS) for blocks in own_blocks]
-
-    def places_of(position):
-        out = []
-        for move in (lambda up: 0, lambda up: 2 * up - 1, lambda up: 1 - 2 * up, lambda up: 2):
-            for stream in range(2):
-                at = position + stream
-                out.append((at // 2 + move(at % 2)) % BLOCKS)
-        return jnp.stack(out).astype(jnp.int32)
-
-    own_places = places_of(position)
-    other_places = places_of(jnp.where(core == 0, y, z))
+    weight_own = place(jnp.stack(places).astype(jnp.int32), blocks)
+    weight_other = lax.ppermute(weight_own, "dp", other_core)
 
     block = negatives.reshape(-1)
     order = jnp.arange(pairs, dtype=jnp.int32)
@@ -242,8 +234,8 @@
     def in_order(own, other):
         return jnp.where(core == 0, own, other), jnp.where(core == 0, other, own)
 
-    weight_own, projected_own, squares = project(own_places, states, own_arrays)
-    weight_other, projected_other, more = project(other_places, states, other_arrays)
+    projected_own, squares = project(states, weight_own)
+    projected_other, more = project(states, weight_other)
     squares = squares + more
     projected = jnp.concatenate(in_order(projected_own, projected_other), axis=1)
     squares = sum_all(squares.reshape(-1, math.gcd(128, 2 * pairs)), "mp").reshape(-1)

time: 237 us -> 228 us (0.962)
  starting transfers between devices: 81.8 us -> 65.4 us
  waiting for transfers between devices: 47.3 us -> 62.8 us
  Pallas kernels: 16.8 us -> 9.4 us
    ppermute x8 -> x1, starting transfers between devices: 23.6 us -> 9.6 us  [on_device(): weight_other = lax.ppermute(weight_own, 'dp', other_core)]
    ppermute x8, waiting for transfers between devices: 12.4 us -> 23.2 us  [on_device(): lax.ppermute(held[stream], 'dp', matchings[(step + stream) % 2])]
    pallas_call x2 -> x3, Pallas kernels: 12.3 us -> 5.96 us  [the longest x2 3.44 us: project(): pl.pallas_call(project_kernel, grid=(width // tile,), out_shape=(jax.Shap...]
    ppermute x8 -> x1, waiting for transfers between devices: 0.02 us -> 4.82 us  [on_device(): weight_other = lax.ppermute(weight_own, 'dp', other_core)]
  transfers between devices with their start and end apart: 20 -> 13, of which waited for: 8 -> 10; matrix products, arithmetic and copies ran while one was open for 1% -> 1% of each run, Pallas kernels for 3% -> 1%
where the time goes in v5:
time: 228 us; the launch traced here: 227 us
  blocking collectives  71.5 us (31%)
  starting transfers between devices  65.4 us (29%)
  waiting for transfers between devices  62.8 us (28%)
  Pallas kernels  9.4 us (4%)
  local copies, waits for them, and re-layouts  9.38 us (4%)
  other arithmetic  3.61 us (2%)
  matrix products  3.25 us (1%)
    all_to_all x3, blocking collectives, swap(): lax.all_to_all(x, axis, split_axis=0, concat_axis=0, tiled=True, axis_ind...  71.5 us
    all_to_all x4, waiting for transfers between devices, swap(): lax.all_to_all(x, axis, split_axis=0, concat_axis=0, tiled=True, axis_ind...  34.9 us
    all_to_all x4, starting transfers between devices, swap(): lax.all_to_all(x, axis, split_axis=0, concat_axis=0, tiled=True, axis_ind...  31.3 us
    ppermute x8, starting transfers between devices, on_device(): lax.ppermute(held[stream], 'dp', matchings[(step + stream) % 2])  24.5 us
    ppermute x8, waiting for transfers between devices, on_device(): lax.ppermute(held[stream], 'dp', matchings[(step + stream) % 2])  23.2 us
    ppermute x1, starting transfers between devices, on_device(): weight_other = lax.ppermute(weight_own, 'dp', other_core)  9.6 us
    ppermute x1, waiting for transfers between devices, on_device(): weight_other = lax.ppermute(weight_own, 'dp', other_core)  4.82 us
  transfers between devices with their start and end apart: 13, of which 10 were waited for; matrix products, arithmetic and copies ran while one was open for 1% of the time, Pallas kernels for 1%

profile of v5, /device:TPU:1, one launch (start us, length us, event | category | flops | bytes accessed | tf_op | source)
XLA Modules:
  0.0 226.7 jit_solution(10388198750102035567)
XLA Ops:
  2.3 13.7 %all-to-all-start = ((bf16[32,8,1024]{2,1,0:T(8,128)(2,1)}), bf16[32,8,1024]{2,1,0:T(8,128)(2,1)S(1)}, u32[]{:S(2)}, u32[]{:S(2)}) async-start(bf16[32,8,1024]{2,1,0:T(8,128)(2,1)} %bitcast.1), calls=%async_computation | async-start | bytes 1048576 | tf_op jit(solution)/shard_map/all_to_all | solution.py:28
  17.1 10.3 %all-to-all-done = bf16[32,8,1024]{2,1,0:T(8,128)(2,1)S(1)} async-done(((bf16[32,8,1024]{2,1,0:T(8,128)(2,1)}), bf16[32,8,1024]{2,1,0:T(8,128)(2,1)S(1)}, u32[]{:S(2)}, u32[]{:S(2)}) %all-to-all-start) | async-done | bytes 524320 | tf_op jit(solution)/shard_map/all_to_all | solution.py:28
  27.5 3.2 %collective-permute-start = (bf16[32,4096]{1,0:T(8,128)(2,1)S(1)}, bf16[32,4096]{1,0:T(8,128)(2,1)S(1)}, u32[]{:S(2)}, u32[]{:S(2)}) collective-permute-start(bf16[32,4096]{1,0:T(8,128)(2,1)S(1)} %bitcast.30), channel_id=1, source_target_pairs={{0,64},{4,12},{8,72},{12,4},{16,80},{20,28},{24,88},{28,20},{32,96... | collective-permute-start | bytes 786440 | tf_op jit(solution)/shard_map/ppermute | solution.py:204
  30.7 4.9 %collective-permute-start.1 = (bf16[32,4096]{1,0:T(8,128)(2,1)S(1)}, bf16[32,4096]{1,0:T(8,128)(2,1)S(1)}, u32[]{:S(2)}, u32[]{:S(2)}) collective-permute-start(bf16[32,4096]{1,0:T(8,128)(2,1)S(1)} %bitcast.28), channel_id=1, source_target_pairs={{0,448},{4,60},{8,456},{12,20},{16,464},{20,12},{24,472},{28,36},{... | collective-permute-start | bytes 786440 | tf_op jit(solution)/shard_map/ppermute | solution.py:204
  35.7 3.6 %collective-permute-done.1 = bf16[32,4096]{1,0:T(8,128)(2,1)S(1)} collective-permute-done((bf16[32,4096]{1,0:T(8,128)(2,1)S(1)}, bf16[32,4096]{1,0:T(8,128)(2,1)S(1)}, u32[]{:S(2)}, u32[]{:S(2)}) %collective-permute-start.1) | collective-permute-done | bytes 262176 | tf_op jit(solution)/shard_map/ppermute | solution.py:204
  39.5 4.9 %collective-permute-start.2 = (bf16[64,4096]{1,0:T(8,128)(2,1)S(1)}, bf16[64,4096]{1,0:T(8,128)(2,1)}, u32[]{:S(2)}, u32[]{:S(2)}) collective-permute-start(bf16[64,4096]{1,0:T(8,128)(2,1)S(1)} %pad_maximum_fusion.2.refs_0_), channel_id=1, source_target_pairs={{0,448},{4,60},{8,456},{12,20},{16,464},{20,12},{24,472},{28,36},{... | collective-permute-start | bytes 1572872 | tf_op jit(solution)/shard_map/ppermute | solution.py:204
  47.9 3.6 %all-to-all-start.1 = ((bf16[4,256,1024]{2,1,0:T(8,128)(2,1)}), bf16[4,256,1024]{2,1,0:T(8,128)(2,1)S(1)}, u32[]{:S(2)}, u32[]{:S(2)}) async-start(bf16[4,256,1024]{2,1,0:T(8,128)(2,1)} %broadcast_in_dim.22), calls=%async_computation.1 | async-start | bytes 4194304 | tf_op jit(solution)/shard_map/all_to_all | solution.py:28
  51.6 3.2 %collective-permute-done.3.refs_3_ = bf16[64,4096]{1,0:T(8,128)(2,1)} collective-permute-done((bf16[64,4096]{1,0:T(8,128)(2,1)S(1)}, bf16[64,4096]{1,0:T(8,128)(2,1)}, u32[]{:S(2)}, u32[]{:S(2)}) %collective-permute-start.3) | collective-permute-done | bytes 524320 | tf_op jit(solution)/shard_map/ppermute | solution.py:204
  56.6 2.5 %collective-permute-start.5 = (bf16[64,4096]{1,0:T(8,128)(2,1)}, bf16[64,4096]{1,0:T(8,128)(2,1)}, u32[]{:S(2)}, u32[]{:S(2)}) collective-permute-start(bf16[64,4096]{1,0:T(8,128)(2,1)} %collective-permute-done.3.refs_3_), channel_id=1, source_target_pairs={{0,448},{4,60},{8,456},{12,20},{16,464},{20,12},{24,472},{28,36},{... | collective-permute-start | bytes 1572872 | tf_op jit(solution)/shard_map/ppermute | solution.py:204
  59.2 6.0 %collective-permute-done.4.refs_4_ = bf16[64,4096]{1,0:T(8,128)(2,1)} collective-permute-done((bf16[64,4096]{1,0:T(8,128)(2,1)}, bf16[64,4096]{1,0:T(8,128)(2,1)}, u32[]{:S(2)}, u32[]{:S(2)}) %collective-permute-start.4) | collective-permute-done | bytes 524320 | tf_op jit(solution)/shard_map/ppermute | solution.py:204
  65.1 3.1 %collective-permute-done.5.refs_5_ = bf16[64,4096]{1,0:T(8,128)(2,1)} collective-permute-done((bf16[64,4096]{1,0:T(8,128)(2,1)}, bf16[64,4096]{1,0:T(8,128)(2,1)}, u32[]{:S(2)}, u32[]{:S(2)}) %collective-permute-start.5) | collective-permute-done | bytes 524320 | tf_op jit(solution)/shard_map/ppermute | solution.py:204
  70.8 2.7 %collective-permute-start.7 = (bf16[64,4096]{1,0:T(8,128)(2,1)}, bf16[64,4096]{1,0:T(8,128)(2,1)}, u32[]{:S(2)}, u32[]{:S(2)}) collective-permute-start(bf16[64,4096]{1,0:T(8,128)(2,1)} %collective-permute-done.5.refs_5_), channel_id=1, source_target_pairs={{0,64},{4,12},{8,72},{12,4},{16,80},{20,28},{24,88},{28,20},{32,96... | collective-permute-start | bytes 1572872 | tf_op jit(solution)/shard_map/ppermute | solution.py:204
  73.8 5.9 %collective-permute-done.6.refs_6_ = bf16[64,4096]{1,0:T(8,128)(2,1)} collective-permute-done((bf16[64,4096]{1,0:T(8,128)(2,1)}, bf16[64,4096]{1,0:T(8,128)(2,1)}, u32[]{:S(2)}, u32[]{:S(2)}) %collective-permute-start.6) | collective-permute-done | bytes 524320 | tf_op jit(solution)/shard_map/ppermute | solution.py:204
  81.0 2.5 %shard_map.68.weight.weight_own = bf16[512,4096]{1,0:T(8,128)(2,1)S(1)} custom-call(s32[8]{0:T(128)S(1)} %stack.59.places, bf16[64,4096]{1,0:T(8,128)(2,1)S(1)} %pad_maximum_fusion.2.refs_0_, bf16[64,4096]{1,0:T(8,128)(2,1)S(1)} %pad_maximum_fusion.3.refs_1_, bf16[64,4096]{1,0:T(8,128)(2,1)} %collective-permute-done.2.refs_2_, ...), custom_call_target="tpu_custom_call" | custom-call | tf_op jit(solution)/shard_map/pallas_call | solution.py:98
  83.6 9.6 %collective-permute-start.8 = (bf16[512,4096]{1,0:T(8,128)(2,1)S(1)}, bf16[512,4096]{1,0:T(8,128)(2,1)S(1)}, u32[]{:S(2)}, u32[]{:S(2)}) collective-permute-start(bf16[512,4096]{1,0:T(8,128)(2,1)S(1)} %shard_map.68.weight.weight_own), channel_id=1, source_target_pairs={{0,4},{4,0},{8,12},{12,8},{16,20},{20,16},{24,28},{28,24},{32,36},... | collective-permute-start | bytes 12582920 | tf_op jit(solution)/shard_map/ppermute | solution.py:223
  95.1 4.8 %collective-permute-done.8.weight.weight_other = bf16[512,4096]{1,0:T(8,128)(2,1)S(1)} collective-permute-done((bf16[512,4096]{1,0:T(8,128)(2,1)S(1)}, bf16[512,4096]{1,0:T(8,128)(2,1)S(1)}, u32[]{:S(2)}, u32[]{:S(2)}) %collective-permute-start.8) | collective-permute-done | bytes 4194336 | tf_op jit(solution)/shard_map/ppermute | solution.py:223
  102.6 3.2 %all-to-all-start.2 = ((f32[4,2,128]{2,1,0:T(2,128)}), f32[4,2,128]{2,1,0:T(2,128)S(1)}, u32[]{:S(2)}, u32[]{:S(2)}) async-start(f32[4,2,128]{2,1,0:T(2,128)} %broadcast_in_dim.24), calls=%async_computation.2 | async-start | bytes 8192 | tf_op jit(solution)/shard_map/all_to_all | solution.py:28
  106.0 4.0 %all-to-all-done.2 = f32[4,2,128]{2,1,0:T(2,128)S(1)} async-done(((f32[4,2,128]{2,1,0:T(2,128)}), f32[4,2,128]{2,1,0:T(2,128)S(1)}, u32[]{:S(2)}, u32[]{:S(2)}) %all-to-all-start.2) | async-done | bytes 4128 | tf_op jit(solution)/shard_map/all_to_all | solution.py:28
  111.5 10.7 %all-to-all-start.3 = ((bf16[128,2,1024]{2,1,0:T(2,128)(2,1)}), bf16[128,2,1024]{2,1,0:T(2,128)(2,1)S(1)}, u32[]{:S(2)}, u32[]{:S(2)}) async-start(bf16[128,2,1024]{2,1,0:T(2,128)(2,1)} %reshape.120), calls=%async_computation.3 | async-start | bytes 1048576 | tf_op jit(solution)/shard_map/all_to_all | solution.py:28
  122.2 20.6 %all-to-all-done.3 = bf16[128,2,1024]{2,1,0:T(2,128)(2,1)S(1)} async-done(((bf16[128,2,1024]{2,1,0:T(2,128)(2,1)}), bf16[128,2,1024]{2,1,0:T(2,128)(2,1)S(1)}, u32[]{:S(2)}, u32[]{:S(2)}) %all-to-all-start.3) | async-done | bytes 524320 | tf_op jit(solution)/shard_map/all_to_all | solution.py:28
  143.8 15.2 %all_to_all.35 = f32[4,384,128]{2,1,0:T(8,128)S(1)} all-to-all(f32[4,384,128]{2,1,0:T(8,128)S(1)} %broadcast_in_dim.25), channel_id=1, replica_groups=mesh['dp'=128,'mp'=4] {'mp'}, dimensions={0} | all-to-all | bytes 1572864 | tf_op jit(solution)/shard_map/all_to_all | solution.py:28
  160.3 27.1 %all_to_all.36 = bf16[128,2,1152]{2,1,0:T(2,128)(2,1)S(1)} all-to-all(bf16[128,2,1152]{2,1,0:T(2,128)(2,1)S(1)} %reshape.122), channel_id=1, replica_groups=mesh['dp'=128,'mp'=4] {'dp'}, dimensions={0} | all-to-all | bytes 1179648 | tf_op jit(solution)/shard_map/all_to_all | solution.py:28
  192.6 3.4 %shard_map.71 = bf16[4,256,1024]{2,1,0:T(8,128)(2,1)S(1)} custom-call(bf16[256,512]{1,0:T(8,128)(2,1)S(1)} %get-tuple-element.48.grad_own, bf16[256,512]{1,0:T(8,128)(2,1)S(1)} %get-tuple-element.47.grad_other, bf16[512,4096]{1,0:T(8,128)(2,1)S(1)} %copy-done.1, bf16[512,4096]{1,0:T(8,128)(2,1)S(1)} %copy-done.3), custom_call_target="tpu_custom_call" | custom-call | flops 2147483648 | bytes 8388608 | tf_op jit(solution)/shard_map/pallas_call | solution.py:163
  196.1 29.2 %all_to_all.37 = bf16[4,256,1024]{2,1,0:T(8,128)(2,1)S(1)} all-to-all(bf16[4,256,1024]{2,1,0:T(8,128)(2,1)S(1)} %shard_map.71), channel_id=1, replica_groups=mesh['dp'=128,'mp'=4] {'mp'}, dimensions={0} | all-to-all | bytes 4194304 | tf_op jit(solution)/shard_map/all_to_all | solution.py:28
  (84 shorter events, 27.4 us)
Async XLA Ops:
  2.3 25.1 %all-to-all-start = ((bf16[32,8,1024]{2,1,0:T(8,128)(2,1)}), bf16[32,8,1024]{2,1,0:T(8,128)(2,1)S(1)}, u32[]{:S(2)}, u32[]{:S(2)}) async-start(bf16[32,8,1024]{2,1,0:T(8,128)(2,1)} %bitcast.1), calls=%async_computation | async-start | bytes 1048576 | tf_op jit(solution)/shard_map/all_to_all | solution.py:28
  27.5 8.2 %collective-permute-start = (bf16[32,4096]{1,0:T(8,128)(2,1)S(1)}, bf16[32,4096]{1,0:T(8,128)(2,1)S(1)}, u32[]{:S(2)}, u32[]{:S(2)}) collective-permute-start(bf16[32,4096]{1,0:T(8,128)(2,1)S(1)} %bitcast.30), channel_id=1, source_target_pairs={{0,64},{4,12},{8,72},{12,4},{16,80},{20,28},{24,88},{28,20},{32,96... | collective-permute-start | bytes 786440 | tf_op jit(solution)/shard_map/ppermute | solution.py:204
  30.7 8.6 %collective-permute-start.1 = (bf16[32,4096]{1,0:T(8,128)(2,1)S(1)}, bf16[32,4096]{1,0:T(8,128)(2,1)S(1)}, u32[]{:S(2)}, u32[]{:S(2)}) collective-permute-start(bf16[32,4096]{1,0:T(8,128)(2,1)S(1)} %bitcast.28), channel_id=1, source_target_pairs={{0,448},{4,60},{8,456},{12,20},{16,464},{20,12},{24,472},{28,36},{... | collective-permute-start | bytes 786440 | tf_op jit(solution)/shard_map/ppermute | solution.py:204
  39.5 12.1 %collective-permute-start.2 = (bf16[64,4096]{1,0:T(8,128)(2,1)S(1)}, bf16[64,4096]{1,0:T(8,128)(2,1)}, u32[]{:S(2)}, u32[]{:S(2)}) collective-permute-start(bf16[64,4096]{1,0:T(8,128)(2,1)S(1)} %pad_maximum_fusion.2.refs_0_), channel_id=1, source_target_pairs={{0,448},{4,60},{8,456},{12,20},{16,464},{20,12},{24,472},{28,36},{... | collective-permute-start | bytes 1572872 | tf_op jit(solution)/shard_map/ppermute | solution.py:204
  44.4 10.3 %collective-permute-start.3 = (bf16[64,4096]{1,0:T(8,128)(2,1)S(1)}, bf16[64,4096]{1,0:T(8,128)(2,1)}, u32[]{:S(2)}, u32[]{:S(2)}) collective-permute-start(bf16[64,4096]{1,0:T(8,128)(2,1)S(1)} %pad_maximum_fusion.3.refs_1_), channel_id=1, source_target_pairs={{0,64},{4,12},{8,72},{12,4},{16,80},{20,28},{24,88},{28,20},{32,96... | collective-permute-start | bytes 1572872 | tf_op jit(solution)/shard_map/ppermute | solution.py:204
  47.9 25.8 %all-to-all-start.1 = ((bf16[4,256,1024]{2,1,0:T(8,128)(2,1)}), bf16[4,256,1024]{2,1,0:T(8,128)(2,1)S(1)}, u32[]{:S(2)}, u32[]{:S(2)}) async-start(bf16[4,256,1024]{2,1,0:T(8,128)(2,1)} %broadcast_in_dim.22), calls=%async_computation.1 | async-start | bytes 4194304 | tf_op jit(solution)/shard_map/all_to_all | solution.py:28
  54.7 10.4 %collective-permute-start.4 = (bf16[64,4096]{1,0:T(8,128)(2,1)}, bf16[64,4096]{1,0:T(8,128)(2,1)}, u32[]{:S(2)}, u32[]{:S(2)}) collective-permute-start(bf16[64,4096]{1,0:T(8,128)(2,1)} %collective-permute-done.2.refs_2_), channel_id=1, source_target_pairs={{0,64},{4,12},{8,72},{12,4},{16,80},{20,28},{24,88},{28,20},{32,96... | collective-permute-start | bytes 1572872 | tf_op jit(solution)/shard_map/ppermute | solution.py:204
  56.6 11.6 %collective-permute-start.5 = (bf16[64,4096]{1,0:T(8,128)(2,1)}, bf16[64,4096]{1,0:T(8,128)(2,1)}, u32[]{:S(2)}, u32[]{:S(2)}) collective-permute-start(bf16[64,4096]{1,0:T(8,128)(2,1)} %collective-permute-done.3.refs_3_), channel_id=1, source_target_pairs={{0,448},{4,60},{8,456},{12,20},{16,464},{20,12},{24,472},{28,36},{... | collective-permute-start | bytes 1572872 | tf_op jit(solution)/shard_map/ppermute | solution.py:204
  68.3 11.4 %collective-permute-start.6 = (bf16[64,4096]{1,0:T(8,128)(2,1)}, bf16[64,4096]{1,0:T(8,128)(2,1)}, u32[]{:S(2)}, u32[]{:S(2)}) collective-permute-start(bf16[64,4096]{1,0:T(8,128)(2,1)} %collective-permute-done.4.refs_4_), channel_id=1, source_target_pairs={{0,448},{4,60},{8,456},{12,20},{16,464},{20,12},{24,472},{28,36},{... | collective-permute-start | bytes 1572872 | tf_op jit(solution)/shard_map/ppermute | solution.py:204
  70.8 10.2 %collective-permute-start.7 = (bf16[64,4096]{1,0:T(8,128)(2,1)}, bf16[64,4096]{1,0:T(8,128)(2,1)}, u32[]{:S(2)}, u32[]{:S(2)}) collective-permute-start(bf16[64,4096]{1,0:T(8,128)(2,1)} %collective-permute-done.5.refs_5_), channel_id=1, source_target_pairs={{0,64},{4,12},{8,72},{12,4},{16,80},{20,28},{24,88},{28,20},{32,96... | collective-permute-start | bytes 1572872 | tf_op jit(solution)/shard_map/ppermute | solution.py:204
  73.8 19.4 %copy-start.6 = (s32[128,1]{0,1:T(1,128)S(1)}, s32[128,1]{0,1:T(1,128)}, u32[]{:S(2)}) copy-start(s32[128,1]{0,1:T(1,128)} %param.9) | copy-start | bytes 1540
  83.6 11.5 %copy-start = (bf16[512,4096]{1,0:T(8,128)(2,1)}, bf16[512,4096]{1,0:T(8,128)(2,1)S(1)}, u32[]{:S(2)}) copy-start(bf16[512,4096]{1,0:T(8,128)(2,1)S(1)} %shard_map.68.weight.weight_own) | copy-start | bytes 12582916
  83.6 16.4 %collective-permute-start.8 = (bf16[512,4096]{1,0:T(8,128)(2,1)S(1)}, bf16[512,4096]{1,0:T(8,128)(2,1)S(1)}, u32[]{:S(2)}, u32[]{:S(2)}) collective-permute-start(bf16[512,4096]{1,0:T(8,128)(2,1)S(1)} %shard_map.68.weight.weight_own), channel_id=1, source_target_pairs={{0,4},{4,0},{8,12},{12,8},{16,20},{20,16},{24,28},{28,24},{32,36},... | collective-permute-start | bytes 12582920 | tf_op jit(solution)/shard_map/ppermute | solution.py:223
  100.0 2.0 copy-start.2
  102.6 7.4 %all-to-all-start.2 = ((f32[4,2,128]{2,1,0:T(2,128)}), f32[4,2,128]{2,1,0:T(2,128)S(1)}, u32[]{:S(2)}, u32[]{:S(2)}) async-start(f32[4,2,128]{2,1,0:T(2,128)} %broadcast_in_dim.24), calls=%async_computation.2 | async-start | bytes 8192 | tf_op jit(solution)/shard_map/all_to_all | solution.py:28
  111.5 31.3 %all-to-all-start.3 = ((bf16[128,2,1024]{2,1,0:T(2,128)(2,1)}), bf16[128,2,1024]{2,1,0:T(2,128)(2,1)S(1)}, u32[]{:S(2)}, u32[]{:S(2)}) async-start(bf16[128,2,1024]{2,1,0:T(2,128)(2,1)} %reshape.120), calls=%async_computation.3 | async-start | bytes 1048576 | tf_op jit(solution)/shard_map/all_to_all | solution.py:28
  142.9 0.8 copy-start.4
  187.4 2.6 %copy-start.5 = (s32[128]{0:T(128)S(1)}, s32[128]{0:T(128)}, u32[]{:S(2)}) copy-start(s32[128]{0:T(128)} %param.8) | copy-start | bytes 1540
  187.8 3.2 %copy-start.3 = (bf16[512,4096]{1,0:T(8,128)(2,1)S(1)}, bf16[512,4096]{1,0:T(8,128)(2,1)}, u32[]{:S(2)}) copy-start(bf16[512,4096]{1,0:T(8,128)(2,1)} %copy-done.2) | copy-start | bytes 12582916
  190.4 2.2 copy-start.1

commit v6 on v5

--- a/solution.py
+++ b/solution.py
@@ -150,14 +150,21 @@
     )(states, weight)
 
 
-def spread_kernel(grad_own, grad_other, weight_own, weight_other, out):
-    value = dot(grad_own[...], weight_own[...]) + dot(grad_other[...], weight_other[...])
+def spread_kernel(grad_own, grad_other, *refs):
+    weights, out = refs[:-1], refs[-1]
+    depth = weights[0].shape[0]
+    value = jnp.zeros(out.shape[1:], F32)
+    for i, weight in enumerate(weights):
+        grad = (grad_own, grad_other)[i // 2]
+        at = pl.ds(i % 2 * depth, depth)
+        value = value + dot(grad[:, at], weight[...])
     out[0] = value.astype(BF16)
 
 
-def spread(grad_own, grad_other, weight_own, weight_other, parts):
+def spread(grad_own, grad_other, weights, parts):
     rows, width = grad_own.shape
-    columns_each = weight_own.shape[1] // parts
+    depth, columns_all = weights[0].shape
+    columns_each = columns_all // parts
     tile = min(1024, columns_each)
     per_part = columns_each // tile
     return pl.pallas_call(
@@ -165,15 +172,15 @@
         grid=(parts * per_part,),
         out_shape=jax.ShapeDtypeStruct((parts, rows, columns_each), BF16),
         in_specs=[pl.BlockSpec((rows, width), lambda n: (0, 0))] * 2
-        + [pl.BlockSpec((width, tile), lambda n: (0, n))] * 2,
+        + [pl.BlockSpec((depth, tile), lambda n: (0, n))] * len(weights),
         out_specs=pl.BlockSpec((1, rows, tile), lambda n: (n // per_part, 0, n % per_part)),
         compiler_params=pltpu.CompilerParams(vmem_limit_bytes=24 * 2**20),
         cost_estimate=pl.CostEstimate(
-            flops=4 * rows * width * weight_own.shape[1],
-            bytes_accessed=4 * width * weight_own.shape[1],
+            flops=4 * rows * width * columns_all,
+            bytes_accessed=4 * width * columns_all,
             transcendentals=0,
         ),
-    )(grad_own, grad_other, weight_own, weight_other)
+    )(grad_own, grad_other, *weights)
 
 
 def on_device(query_states, passage_states, head_weight, positives, negatives):
@@ -197,30 +204,34 @@
     states = jnp.concatenate([query_states, passage_states], axis=0)
     states, *halves = lax.optimization_barrier((states, *halves))
     states = from_all(states, "mp")
-    blocks, places = [], []
+    blocks, places = ([], []), ([], [])
     held = halves
     for step in range(BLOCKS):
-        came = [
+        first, second = [
             lax.ppermute(held[stream], "dp", matchings[(step + stream) % 2])
             for stream in range(2)
         ]
+        first, _ = lax.optimization_barrier((first, held[1]))
         if step < BLOCKS - 1:
-            came = lax.optimization_barrier(came)
+            second, _ = lax.optimization_barrier((second, first))
         else:
-            (*came, states) = lax.optimization_barrier((*came, states))
-        for stream in range(2):
+            second, states, _ = lax.optimization_barrier((second, states, first))
+        held = []
+        for stream, came in enumerate((first, second)):
             at, is_upper = (position + stream) // 2, (position + stream) % 2
             if step == 0:
-                half, other = halves[stream], came[stream]
-                came[stream] = jnp.concatenate(
-                    [jnp.where(is_upper, other, half), jnp.where(is_upper, half, other)], axis=0
+                half = halves[stream]
+                came = jnp.concatenate(
+                    [jnp.where(is_upper, came, half), jnp.where(is_upper, half, came)], axis=0
                 )
             move = (0, 2 * is_upper - 1, 1 - 2 * is_upper, 2)[step]
-            places.append(stream * BLOCKS + (at + move) % BLOCKS)
-        blocks += came
-        held = came
-    weight_own = place(jnp.stack(places).astype(jnp.int32), blocks)
-    weight_other = lax.ppermute(weight_own, "dp", other_core)
+            places[stream].append((at + move) % BLOCKS)
+            blocks[stream].append(came)
+            held.append(came)
+    weights = [
+        place(jnp.stack(places[stream]).astype(jnp.int32), blocks[stream]) for stream in range(2)
+    ]
+    weights += [lax.ppermute(weight, "dp", other_core) for weight in weights]
 
     block = negatives.reshape(-1)
     order = jnp.arange(pairs, dtype=jnp.int32)
@@ -234,10 +245,10 @@
     def in_order(own, other):
         return jnp.where(core == 0, own, other), jnp.where(core == 0, other, own)
 
-    projected_own, squares = project(states, weight_own)
-    projected_other, more = project(states, weight_other)
-    squares = squares + more
-    projected = jnp.concatenate(in_order(projected_own, projected_other), axis=1)
+    projected, squares = zip(*[project(states, weight) for weight in weights])
+    squares = sum(squares)
+    own, other = jnp.concatenate(projected[:2], axis=1), jnp.concatenate(projected[2:], axis=1)
+    projected = jnp.concatenate(in_order(own, other), axis=1)
     squares = sum_all(squares.reshape(-1, math.gcd(128, 2 * pairs)), "mp").reshape(-1)
     inverse = lax.rsqrt(squares[:, None] + EPSILON)
     embedded = (projected * inverse).astype(BF16)
@@ -291,7 +302,7 @@
     proj_grad = (inverse * grad - projected * (inverse * inverse * radial)).astype(BF16)
     half = part // 2
     grad_own, grad_other = in_order(proj_grad[:, :half], proj_grad[:, half:])
-    partial = spread(grad_own, grad_other, weight_own, weight_other, parts)
+    partial = spread(grad_own, grad_other, weights, parts)
     state_grad = jnp.sum(swap(partial, "mp").astype(F32), axis=0)
     return (state_grad[:pairs], state_grad[pairs:])
 

time: 228 us -> 221 us (0.969)
  waiting for transfers between devices: 62.8 us -> 46.5 us
  starting transfers between devices: 65.4 us -> 71.9 us
    ppermute x8, waiting for transfers between devices: 23.2 us -> 10.8 us  [on_device(): lax.ppermute(held[stream], 'dp', matchings[(step + stream) % 2])]
    ppermute x8, starting transfers between devices: 24.5 us -> 28.5 us  [on_device(): lax.ppermute(held[stream], 'dp', matchings[(step + stream) % 2])]
    ppermute x1 -> x2, waiting for transfers between devices: 4.82 us -> 0.91 us  [on_device(): weights += [lax.ppermute(weight, 'dp', other_core) for weight in weights]]
    ppermute x1 -> x2, starting transfers between devices: 9.6 us -> 12.2 us  [on_device(): weights += [lax.ppermute(weight, 'dp', other_core) for weight in weights]]
  transfers between devices with their start and end apart: 13 -> 14, of which waited for: 10 -> 8; matrix products, arithmetic and copies ran while one was open for 1% -> 2% of each run, Pallas kernels for 1% -> 2%
where the time goes in v6:
time: 221 us; the launch traced here: 220 us
  starting transfers between devices  71.9 us (33%)
  blocking collectives  71.4 us (32%)
  waiting for transfers between devices  46.5 us (21%)
  local copies, waits for them, and re-layouts  10.7 us (5%)
  Pallas kernels  10.7 us (5%)
  other arithmetic  3.78 us (2%)
  matrix products  3.28 us (1%)
    all_to_all x3, blocking collectives, swap(): lax.all_to_all(x, axis, split_axis=0, concat_axis=0, tiled=True, axis_ind...  71.4 us
    all_to_all x4, waiting for transfers between devices, swap(): lax.all_to_all(x, axis, split_axis=0, concat_axis=0, tiled=True, axis_ind...  34.8 us
    all_to_all x4, starting transfers between devices, swap(): lax.all_to_all(x, axis, split_axis=0, concat_axis=0, tiled=True, axis_ind...  31.2 us
    ppermute x8, starting transfers between devices, on_device(): lax.ppermute(held[stream], 'dp', matchings[(step + stream) % 2])  28.5 us
    ppermute x2, starting transfers between devices, on_device(): weights += [lax.ppermute(weight, 'dp', other_core) for weight in weights]  12.2 us
    ppermute x8, waiting for transfers between devices, on_device(): lax.ppermute(held[stream], 'dp', matchings[(step + stream) % 2])  10.8 us
  transfers between devices with their start and end apart: 14, of which 8 were waited for; matrix products, arithmetic and copies ran while one was open for 2% of the time, Pallas kernels for 2%

profile of v6, /device:TPU:1, one launch (start us, length us, event | category | flops | bytes accessed | tf_op | source)
XLA Modules:
  0.0 219.7 jit_solution(7734539756246130837)
XLA Ops:
  2.3 13.7 %all-to-all-start = ((bf16[32,8,1024]{2,1,0:T(8,128)(2,1)}), bf16[32,8,1024]{2,1,0:T(8,128)(2,1)S(1)}, u32[]{:S(2)}, u32[]{:S(2)}) async-start(bf16[32,8,1024]{2,1,0:T(8,128)(2,1)} %bitcast.1), calls=%async_computation | async-start | bytes 1048576 | tf_op jit(solution)/shard_map/all_to_all | solution.py:28
  17.1 10.3 %all-to-all-done = bf16[32,8,1024]{2,1,0:T(8,128)(2,1)S(1)} async-done(((bf16[32,8,1024]{2,1,0:T(8,128)(2,1)}), bf16[32,8,1024]{2,1,0:T(8,128)(2,1)S(1)}, u32[]{:S(2)}, u32[]{:S(2)}) %all-to-all-start) | async-done | bytes 524320 | tf_op jit(solution)/shard_map/all_to_all | solution.py:28
  27.5 3.2 %collective-permute-start.1 = (bf16[32,4096]{1,0:T(8,128)(2,1)S(1)}, bf16[32,4096]{1,0:T(8,128)(2,1)S(1)}, u32[]{:S(2)}, u32[]{:S(2)}) collective-permute-start(bf16[32,4096]{1,0:T(8,128)(2,1)S(1)} %bitcast.30), channel_id=1, source_target_pairs={{0,64},{4,12},{8,72},{12,4},{16,80},{20,28},{24,88},{28,20},{32,96... | collective-permute-start | bytes 786440 | tf_op jit(solution)/shard_map/ppermute | solution.py:211
  30.8 4.9 %collective-permute-start = (bf16[32,4096]{1,0:T(8,128)(2,1)S(1)}, bf16[32,4096]{1,0:T(8,128)(2,1)S(1)}, u32[]{:S(2)}, u32[]{:S(2)}) collective-permute-start(bf16[32,4096]{1,0:T(8,128)(2,1)S(1)} %bitcast.28), channel_id=1, source_target_pairs={{0,448},{4,60},{8,456},{12,20},{16,464},{20,12},{24,472},{28,36},{... | collective-permute-start | bytes 786440 | tf_op jit(solution)/shard_map/ppermute | solution.py:211
  35.8 4.0 %collective-permute-start.3 = (bf16[64,4096]{1,0:T(8,128)(2,1)S(1)}, bf16[64,4096]{1,0:T(8,128)(2,1)}, u32[]{:S(2)}, u32[]{:S(2)}) collective-permute-start(bf16[64,4096]{1,0:T(8,128)(2,1)S(1)} %pad_maximum_fusion.3.refs_0_), channel_id=1, source_target_pairs={{0,448},{4,60},{8,456},{12,20},{16,464},{20,12},{24,472},{28,36},{... | collective-permute-start | bytes 1572872 | tf_op jit(solution)/shard_map/ppermute | solution.py:211
  43.5 3.6 %all-to-all-start.1 = ((bf16[4,256,1024]{2,1,0:T(8,128)(2,1)}), bf16[4,256,1024]{2,1,0:T(8,128)(2,1)S(1)}, u32[]{:S(2)}, u32[]{:S(2)}) async-start(bf16[4,256,1024]{2,1,0:T(8,128)(2,1)} %broadcast_in_dim.22), calls=%async_computation.1 | async-start | bytes 4194304 | tf_op jit(solution)/shard_map/all_to_all | solution.py:28
  47.3 3.1 %collective-permute-start.5 = (bf16[64,4096]{1,0:T(8,128)(2,1)}, bf16[64,4096]{1,0:T(8,128)(2,1)}, u32[]{:S(2)}, u32[]{:S(2)}) collective-permute-start(bf16[64,4096]{1,0:T(8,128)(2,1)} %collective-permute-done.3.refs_1_), channel_id=1, source_target_pairs={{0,64},{4,12},{8,72},{12,4},{16,80},{20,28},{24,88},{28,20},{32,96... | collective-permute-start | bytes 1572872 | tf_op jit(solution)/shard_map/ppermute | solution.py:211
  50.5 4.5 %collective-permute-start.4 = (bf16[64,4096]{1,0:T(8,128)(2,1)}, bf16[64,4096]{1,0:T(8,128)(2,1)}, u32[]{:S(2)}, u32[]{:S(2)}) collective-permute-start(bf16[64,4096]{1,0:T(8,128)(2,1)} %collective-permute-done.2.refs_1_), channel_id=1, source_target_pairs={{0,448},{4,60},{8,456},{12,20},{16,464},{20,12},{24,472},{28,36},{... | collective-permute-start | bytes 1572872 | tf_op jit(solution)/shard_map/ppermute | solution.py:211
  55.0 2.8 %collective-permute-done.5.refs_2_ = bf16[64,4096]{1,0:T(8,128)(2,1)} collective-permute-done((bf16[64,4096]{1,0:T(8,128)(2,1)}, bf16[64,4096]{1,0:T(8,128)(2,1)}, u32[]{:S(2)}, u32[]{:S(2)}) %collective-permute-start.5) | collective-permute-done | bytes 524320 | tf_op jit(solution)/shard_map/ppermute | solution.py:211
  57.8 4.3 %collective-permute-start.7 = (bf16[64,4096]{1,0:T(8,128)(2,1)}, bf16[64,4096]{1,0:T(8,128)(2,1)}, u32[]{:S(2)}, u32[]{:S(2)}) collective-permute-start(bf16[64,4096]{1,0:T(8,128)(2,1)} %collective-permute-done.5.refs_2_), channel_id=1, source_target_pairs={{0,448},{4,60},{8,456},{12,20},{16,464},{20,12},{24,472},{28,36},{... | collective-permute-start | bytes 1572872 | tf_op jit(solution)/shard_map/ppermute | solution.py:211
  62.1 2.5 %collective-permute-start.6 = (bf16[64,4096]{1,0:T(8,128)(2,1)}, bf16[64,4096]{1,0:T(8,128)(2,1)}, u32[]{:S(2)}, u32[]{:S(2)}) collective-permute-start(bf16[64,4096]{1,0:T(8,128)(2,1)} %collective-permute-done.4.refs_2_), channel_id=1, source_target_pairs={{0,64},{4,12},{8,72},{12,4},{16,80},{20,28},{24,88},{28,20},{32,96... | collective-permute-start | bytes 1572872 | tf_op jit(solution)/shard_map/ppermute | solution.py:211
  64.9 4.5 %collective-permute-done.7.refs_3_ = bf16[64,4096]{1,0:T(8,128)(2,1)} collective-permute-done((bf16[64,4096]{1,0:T(8,128)(2,1)}, bf16[64,4096]{1,0:T(8,128)(2,1)}, u32[]{:S(2)}, u32[]{:S(2)}) %collective-permute-start.7) | collective-permute-done | bytes 524320 | tf_op jit(solution)/shard_map/ppermute | solution.py:211
  69.4 3.3 %collective-permute-done.6.refs_3_ = bf16[64,4096]{1,0:T(8,128)(2,1)} collective-permute-done((bf16[64,4096]{1,0:T(8,128)(2,1)}, bf16[64,4096]{1,0:T(8,128)(2,1)}, u32[]{:S(2)}, u32[]{:S(2)}) %collective-permute-start.6) | collective-permute-done | bytes 524320 | tf_op jit(solution)/shard_map/ppermute | solution.py:211
  72.6 2.0 shard_map.70.weight.refs_1_
  74.6 10.2 %collective-permute-start.9 = (bf16[256,4096]{1,0:T(8,128)(2,1)S(1)}, bf16[256,4096]{1,0:T(8,128)(2,1)S(1)}, u32[]{:S(2)}, u32[]{:S(2)}) collective-permute-start(bf16[256,4096]{1,0:T(8,128)(2,1)S(1)} %shard_map.70.weight.refs_1_), channel_id=1, source_target_pairs={{0,4},{4,0},{8,12},{12,8},{16,20},{20,16},{24,28},{28,24},{32,36},... | collective-permute-start | bytes 6291464 | tf_op jit(solution)/shard_map/ppermute | solution.py:234
  85.0 2.0 shard_map.68.weight.refs_0_
  95.1 4.4 %all-to-all-start.2 = ((f32[4,2,128]{2,1,0:T(2,128)}), f32[4,2,128]{2,1,0:T(2,128)S(1)}, u32[]{:S(2)}, u32[]{:S(2)}) async-start(f32[4,2,128]{2,1,0:T(2,128)} %broadcast_in_dim.24), calls=%async_computation.2 | async-start | bytes 8192 | tf_op jit(solution)/shard_map/all_to_all | solution.py:28
  99.7 3.9 %all-to-all-done.2 = f32[4,2,128]{2,1,0:T(2,128)S(1)} async-done(((f32[4,2,128]{2,1,0:T(2,128)}), f32[4,2,128]{2,1,0:T(2,128)S(1)}, u32[]{:S(2)}, u32[]{:S(2)}) %all-to-all-start.2) | async-done | bytes 4128 | tf_op jit(solution)/shard_map/all_to_all | solution.py:28
  105.1 9.5 %all-to-all-start.3 = ((bf16[128,2,1024]{2,1,0:T(2,128)(2,1)}), bf16[128,2,1024]{2,1,0:T(2,128)(2,1)S(1)}, u32[]{:S(2)}, u32[]{:S(2)}) async-start(bf16[128,2,1024]{2,1,0:T(2,128)(2,1)} %reshape.120), calls=%async_computation.3 | async-start | bytes 1048576 | tf_op jit(solution)/shard_map/all_to_all | solution.py:28
  114.6 20.6 %all-to-all-done.3 = bf16[128,2,1024]{2,1,0:T(2,128)(2,1)S(1)} async-done(((bf16[128,2,1024]{2,1,0:T(2,128)(2,1)}), bf16[128,2,1024]{2,1,0:T(2,128)(2,1)S(1)}, u32[]{:S(2)}, u32[]{:S(2)}) %all-to-all-start.3) | async-done | bytes 524320 | tf_op jit(solution)/shard_map/all_to_all | solution.py:28
  136.2 15.2 %all_to_all.35 = f32[4,384,128]{2,1,0:T(8,128)S(1)} all-to-all(f32[4,384,128]{2,1,0:T(8,128)S(1)} %broadcast_in_dim.25), channel_id=1, replica_groups=mesh['dp'=128,'mp'=4] {'mp'}, dimensions={0} | all-to-all | bytes 1572864 | tf_op jit(solution)/shard_map/all_to_all | solution.py:28
  152.8 27.1 %all_to_all.36 = bf16[128,2,1152]{2,1,0:T(2,128)(2,1)S(1)} all-to-all(bf16[128,2,1152]{2,1,0:T(2,128)(2,1)S(1)} %reshape.122), channel_id=1, replica_groups=mesh['dp'=128,'mp'=4] {'dp'}, dimensions={0} | all-to-all | bytes 1179648 | tf_op jit(solution)/shard_map/all_to_all | solution.py:28
  185.6 3.5 %shard_map.74 = bf16[4,256,1024]{2,1,0:T(8,128)(2,1)S(1)} custom-call(bf16[256,512]{1,0:T(8,128)(2,1)S(1)} %get-tuple-element.56.grad_own, bf16[256,512]{1,0:T(8,128)(2,1)S(1)} %get-tuple-element.55.grad_other, bf16[256,4096]{1,0:T(8,128)(2,1)S(1)} %copy-done.3, bf16[256,4096]{1,0:T(8,128)(2,1)S(1)} %copy-done.1, bf16[256,4096]{1,0:T(8,128)(2,1)S(1)} %copy-done.7, ...), custom_call_target="tpu_custom_call" | custom-call | flops 2147483648 | bytes 8388608 | tf_op jit(solution)/shard_map/pallas_call | solution.py:170
  189.1 29.2 %all_to_all.37 = bf16[4,256,1024]{2,1,0:T(8,128)(2,1)S(1)} all-to-all(bf16[4,256,1024]{2,1,0:T(8,128)(2,1)S(1)} %shard_map.74), channel_id=1, replica_groups=mesh['dp'=128,'mp'=4] {'mp'}, dimensions={0} | all-to-all | bytes 4194304 | tf_op jit(solution)/shard_map/all_to_all | solution.py:28
  (102 shorter events, 26.1 us)
Async XLA Ops:
  2.3 25.1 %all-to-all-start = ((bf16[32,8,1024]{2,1,0:T(8,128)(2,1)}), bf16[32,8,1024]{2,1,0:T(8,128)(2,1)S(1)}, u32[]{:S(2)}, u32[]{:S(2)}) async-start(bf16[32,8,1024]{2,1,0:T(8,128)(2,1)} %bitcast.1), calls=%async_computation | async-start | bytes 1048576 | tf_op jit(solution)/shard_map/all_to_all | solution.py:28
  27.5 8.2 %collective-permute-start.1 = (bf16[32,4096]{1,0:T(8,128)(2,1)S(1)}, bf16[32,4096]{1,0:T(8,128)(2,1)S(1)}, u32[]{:S(2)}, u32[]{:S(2)}) collective-permute-start(bf16[32,4096]{1,0:T(8,128)(2,1)S(1)} %bitcast.30), channel_id=1, source_target_pairs={{0,64},{4,12},{8,72},{12,4},{16,80},{20,28},{24,88},{28,20},{32,96... | collective-permute-start | bytes 786440 | tf_op jit(solution)/shard_map/ppermute | solution.py:211
  30.8 9.0 %collective-permute-start = (bf16[32,4096]{1,0:T(8,128)(2,1)S(1)}, bf16[32,4096]{1,0:T(8,128)(2,1)S(1)}, u32[]{:S(2)}, u32[]{:S(2)}) collective-permute-start(bf16[32,4096]{1,0:T(8,128)(2,1)S(1)} %bitcast.28), channel_id=1, source_target_pairs={{0,448},{4,60},{8,456},{12,20},{16,464},{20,12},{24,472},{28,36},{... | collective-permute-start | bytes 786440 | tf_op jit(solution)/shard_map/ppermute | solution.py:211
  35.8 11.5 %collective-permute-start.3 = (bf16[64,4096]{1,0:T(8,128)(2,1)S(1)}, bf16[64,4096]{1,0:T(8,128)(2,1)}, u32[]{:S(2)}, u32[]{:S(2)}) collective-permute-start(bf16[64,4096]{1,0:T(8,128)(2,1)S(1)} %pad_maximum_fusion.3.refs_0_), channel_id=1, source_target_pairs={{0,448},{4,60},{8,456},{12,20},{16,464},{20,12},{24,472},{28,36},{... | collective-permute-start | bytes 1572872 | tf_op jit(solution)/shard_map/ppermute | solution.py:211
  39.9 10.5 %collective-permute-start.2 = (bf16[64,4096]{1,0:T(8,128)(2,1)S(1)}, bf16[64,4096]{1,0:T(8,128)(2,1)}, u32[]{:S(2)}, u32[]{:S(2)}) collective-permute-start(bf16[64,4096]{1,0:T(8,128)(2,1)S(1)} %pad_maximum_fusion.2.refs_0_), channel_id=1, source_target_pairs={{0,64},{4,12},{8,72},{12,4},{16,80},{20,28},{24,88},{28,20},{32,96... | collective-permute-start | bytes 1572872 | tf_op jit(solution)/shard_map/ppermute | solution.py:211
  43.5 25.9 %all-to-all-start.1 = ((bf16[4,256,1024]{2,1,0:T(8,128)(2,1)}), bf16[4,256,1024]{2,1,0:T(8,128)(2,1)S(1)}, u32[]{:S(2)}, u32[]{:S(2)}) async-start(bf16[4,256,1024]{2,1,0:T(8,128)(2,1)} %broadcast_in_dim.22), calls=%async_computation.1 | async-start | bytes 4194304 | tf_op jit(solution)/shard_map/all_to_all | solution.py:28
  47.3 10.4 %collective-permute-start.5 = (bf16[64,4096]{1,0:T(8,128)(2,1)}, bf16[64,4096]{1,0:T(8,128)(2,1)}, u32[]{:S(2)}, u32[]{:S(2)}) collective-permute-start(bf16[64,4096]{1,0:T(8,128)(2,1)} %collective-permute-done.3.refs_1_), channel_id=1, source_target_pairs={{0,64},{4,12},{8,72},{12,4},{16,80},{20,28},{24,88},{28,20},{32,96... | collective-permute-start | bytes 1572872 | tf_op jit(solution)/shard_map/ppermute | solution.py:211
  50.5 11.6 %collective-permute-start.4 = (bf16[64,4096]{1,0:T(8,128)(2,1)}, bf16[64,4096]{1,0:T(8,128)(2,1)}, u32[]{:S(2)}, u32[]{:S(2)}) collective-permute-start(bf16[64,4096]{1,0:T(8,128)(2,1)} %collective-permute-done.2.refs_1_), channel_id=1, source_target_pairs={{0,448},{4,60},{8,456},{12,20},{16,464},{20,12},{24,472},{28,36},{... | collective-permute-start | bytes 1572872 | tf_op jit(solution)/shard_map/ppermute | solution.py:211
  57.8 11.6 %collective-permute-start.7 = (bf16[64,4096]{1,0:T(8,128)(2,1)}, bf16[64,4096]{1,0:T(8,128)(2,1)}, u32[]{:S(2)}, u32[]{:S(2)}) collective-permute-start(bf16[64,4096]{1,0:T(8,128)(2,1)} %collective-permute-done.5.refs_2_), channel_id=1, source_target_pairs={{0,448},{4,60},{8,456},{12,20},{16,464},{20,12},{24,472},{28,36},{... | collective-permute-start | bytes 1572872 | tf_op jit(solution)/shard_map/ppermute | solution.py:211
  62.1 10.5 %collective-permute-start.6 = (bf16[64,4096]{1,0:T(8,128)(2,1)}, bf16[64,4096]{1,0:T(8,128)(2,1)}, u32[]{:S(2)}, u32[]{:S(2)}) collective-permute-start(bf16[64,4096]{1,0:T(8,128)(2,1)} %collective-permute-done.4.refs_2_), channel_id=1, source_target_pairs={{0,64},{4,12},{8,72},{12,4},{16,80},{20,28},{24,88},{28,20},{32,96... | collective-permute-start | bytes 1572872 | tf_op jit(solution)/shard_map/ppermute | solution.py:211
  74.6 14.5 %copy-start = (bf16[256,4096]{1,0:T(8,128)(2,1)}, bf16[256,4096]{1,0:T(8,128)(2,1)S(1)}, u32[]{:S(2)}) copy-start(bf16[256,4096]{1,0:T(8,128)(2,1)S(1)} %shard_map.70.weight.refs_1_) | copy-start | bytes 6291460
  74.6 16.1 %collective-permute-start.9 = (bf16[256,4096]{1,0:T(8,128)(2,1)S(1)}, bf16[256,4096]{1,0:T(8,128)(2,1)S(1)}, u32[]{:S(2)}, u32[]{:S(2)}) collective-permute-start(bf16[256,4096]{1,0:T(8,128)(2,1)S(1)} %shard_map.70.weight.refs_1_), channel_id=1, source_target_pairs={{0,4},{4,0},{8,12},{12,8},{16,20},{20,16},{24,28},{28,24},{32,36},... | collective-permute-start | bytes 6291464 | tf_op jit(solution)/shard_map/ppermute | solution.py:234
  85.0 3.9 %copy-start.10 = (s32[128,1]{0,1:T(1,128)S(1)}, s32[128,1]{0,1:T(1,128)}, u32[]{:S(2)}) copy-start(s32[128,1]{0,1:T(1,128)} %param.9) | copy-start | bytes 1540
  87.0 3.0 %copy-start.2 = (bf16[256,4096]{1,0:T(8,128)(2,1)}, bf16[256,4096]{1,0:T(8,128)(2,1)S(1)}, u32[]{:S(2)}) copy-start(bf16[256,4096]{1,0:T(8,128)(2,1)S(1)} %shard_map.68.weight.refs_0_) | copy-start | bytes 6291460
  87.0 6.1 %collective-permute-start.8 = (bf16[256,4096]{1,0:T(8,128)(2,1)S(1)}, bf16[256,4096]{1,0:T(8,128)(2,1)S(1)}, u32[]{:S(2)}, u32[]{:S(2)}) collective-permute-start(bf16[256,4096]{1,0:T(8,128)(2,1)S(1)} %shard_map.68.weight.refs_0_), channel_id=1, source_target_pairs={{0,4},{4,0},{8,12},{12,8},{16,20},{20,16},{24,28},{28,24},{32,36},... | collective-permute-start | bytes 6291464 | tf_op jit(solution)/shard_map/ppermute | solution.py:234
  90.8 1.3 copy-start.4
  93.0 1.4 copy-start.6
  95.1 8.5 %all-to-all-start.2 = ((f32[4,2,128]{2,1,0:T(2,128)}), f32[4,2,128]{2,1,0:T(2,128)S(1)}, u32[]{:S(2)}, u32[]{:S(2)}) async-start(f32[4,2,128]{2,1,0:T(2,128)} %broadcast_in_dim.24), calls=%async_computation.2 | async-start | bytes 8192 | tf_op jit(solution)/shard_map/all_to_all | solution.py:28
  105.1 30.1 %all-to-all-start.3 = ((bf16[128,2,1024]{2,1,0:T(2,128)(2,1)}), bf16[128,2,1024]{2,1,0:T(2,128)(2,1)S(1)}, u32[]{:S(2)}, u32[]{:S(2)}) async-start(bf16[128,2,1024]{2,1,0:T(2,128)(2,1)} %reshape.120), calls=%async_computation.3 | async-start | bytes 1048576 | tf_op jit(solution)/shard_map/all_to_all | solution.py:28
  179.8 2.6 %copy-start.9 = (s32[128]{0:T(128)S(1)}, s32[128]{0:T(128)}, u32[]{:S(2)}) copy-start(s32[128]{0:T(128)} %param.8) | copy-start | bytes 1540
  180.2 3.2 %copy-start.7 = (bf16[256,4096]{1,0:T(8,128)(2,1)S(1)}, bf16[256,4096]{1,0:T(8,128)(2,1)}, u32[]{:S(2)}) copy-start(bf16[256,4096]{1,0:T(8,128)(2,1)} %copy-done.6) | copy-start | bytes 6291460
  182.7 1.6 copy-start.5
  182.9 2.1 copy-start.3
  183.2 2.5 %copy-start.1 = (bf16[256,4096]{1,0:T(8,128)(2,1)S(1)}, bf16[256,4096]{1,0:T(8,128)(2,1)}, u32[]{:S(2)}) copy-start(bf16[256,4096]{1,0:T(8,128)(2,1)} %copy-done) | copy-start | bytes 6291460
  (1 other events, 0.8 us)

commit v7 on v6

--- a/solution.py
+++ b/solution.py
@@ -201,23 +201,31 @@
 
     position = jnp.where(core == 0, z, y)
     halves = (line[: side * rows // 2], line[side * rows // 2 :])
-    states = jnp.concatenate([query_states, passage_states], axis=0)
-    states, *halves = lax.optimization_barrier((states, *halves))
-    states = from_all(states, "mp")
+    query_states, passage_states, *halves = lax.optimization_barrier(
+        (query_states, passage_states, *halves)
+    )
+    states = from_all(jnp.concatenate([query_states, passage_states], axis=0), "mp")
     blocks, places = ([], []), ([], [])
     held = halves
+
+    def placed(stream):
+        return place(jnp.stack(places[stream]).astype(jnp.int32), blocks[stream])
+
     for step in range(BLOCKS):
-        first, second = [
+        behind, ahead = [
             lax.ppermute(held[stream], "dp", matchings[(step + stream) % 2])
             for stream in range(2)
         ]
-        first, _ = lax.optimization_barrier((first, held[1]))
-        if step < BLOCKS - 1:
-            second, _ = lax.optimization_barrier((second, first))
-        else:
-            second, states, _ = lax.optimization_barrier((second, states, first))
-        held = []
-        for stream, came in enumerate((first, second)):
+        ahead, _ = lax.optimization_barrier((ahead, held[0]))
+        for stream in (1, 0):
+            if stream == 0 and step < BLOCKS - 1:
+                behind, _ = lax.optimization_barrier((behind, ahead))
+            elif stream == 0:
+                weight_ahead = placed(1)
+                behind, weight_ahead, states = lax.optimization_barrier(
+                    (behind, weight_ahead, states)
+                )
+            came = (behind, ahead)[stream]
             at, is_upper = (position + stream) // 2, (position + stream) % 2
             if step == 0:
                 half = halves[stream]
@@ -227,10 +235,8 @@
             move = (0, 2 * is_upper - 1, 1 - 2 * is_upper, 2)[step]
             places[stream].append((at + move) % BLOCKS)
             blocks[stream].append(came)
-            held.append(came)
-    weights = [
-        place(jnp.stack(places[stream]).astype(jnp.int32), blocks[stream]) for stream in range(2)
-    ]
+        held = [blocks[0][-1], blocks[1][-1]]
+    weights = [placed(0), weight_ahead]
     weights += [lax.ppermute(weight, "dp", other_core) for weight in weights]
 
     block = negatives.reshape(-1)
@@ -260,7 +266,8 @@
         message = message.reshape(shards, CAPACITY, columns_each)
         return swap(message, "dp").reshape(slots, columns_each)
 
-    arrived = exchange(dot(to_slot, query).astype(BF16))
+    outgoing, query = lax.optimization_barrier((dot(to_slot, query).astype(BF16), query))
+    arrived = exchange(outgoing)
 
     scores = jnp.concatenate([arrived, query], axis=0)
     scores = sum_all(dot(scores, passage, LAST_BOTH), "mp")

time: 221 us -> 218 us (0.986)
  blocking collectives: 71.4 us -> 126 us
  starting transfers between devices: 71.9 us -> 42.6 us
  waiting for transfers between devices: 46.5 us -> 19.7 us
    all_to_all x3 -> x5, blocking collectives: 71.4 us -> 126 us  [swap(): lax.all_to_all(x, axis, split_axis=0, concat_axis=0, tiled=True, axis_ind...]
    all_to_all x4 -> x2, waiting for transfers between devices: 34.8 us -> 3.91 us  [swap(): lax.all_to_all(x, axis, split_axis=0, concat_axis=0, tiled=True, axis_ind...]
    all_to_all x4 -> x2, starting transfers between devices: 31.2 us -> 8.07 us  [swap(): lax.all_to_all(x, axis, split_axis=0, concat_axis=0, tiled=True, axis_ind...]
    ppermute x8, starting transfers between devices: 28.5 us -> 22.8 us  [on_device(): lax.ppermute(held[stream], 'dp', matchings[(step + stream) % 2])]
    ppermute x8, waiting for transfers between devices: 10.8 us -> 14.8 us  [on_device(): lax.ppermute(held[stream], 'dp', matchings[(step + stream) % 2])]
    unnamed x24 -> x30, local copies, waits for them, and re-layouts: 3.7 us -> 5.01 us
  transfers between devices with their start and end apart: 14 -> 12, of which waited for: 8 -> 8; matrix products, arithmetic and copies ran while one was open for 2% -> 1% of each run, Pallas kernels for 2% -> 3%
where the time goes in v7:
time: 218 us; the launch traced here: 217 us
  blocking collectives  126 us (58%)
  starting transfers between devices  42.6 us (20%)
  waiting for transfers between devices  19.7 us (9%)
  Pallas kernels  10.7 us (5%)
  local copies, waits for them, and re-layouts  10.4 us (5%)
  matrix products  3.27 us (2%)
  other arithmetic  2.75 us (1%)
    all_to_all x5, blocking collectives, swap(): lax.all_to_all(x, axis, split_axis=0, concat_axis=0, tiled=True, axis_ind...  126 us
    ppermute x8, starting transfers between devices, on_device(): lax.ppermute(held[stream], 'dp', matchings[(step + stream) % 2])  22.8 us
    ppermute x8, waiting for transfers between devices, on_device(): lax.ppermute(held[stream], 'dp', matchings[(step + stream) % 2])  14.8 us
    ppermute x2, starting transfers between devices, on_device(): weights += [lax.ppermute(weight, 'dp', other_core) for weight in weights]  11.8 us
    all_to_all x2, starting transfers between devices, swap(): lax.all_to_all(x, axis, split_axis=0, concat_axis=0, tiled=True, axis_ind...  8.07 us
    unnamed x30, local copies, waits for them, and re-layouts  5.01 us
  transfers between devices with their start and end apart: 12, of which 8 were waited for; matrix products, arithmetic and copies ran while one was open for 1% of the time, Pallas kernels for 3%

profile of v7, /device:TPU:1, one launch (start us, length us, event | category | flops | bytes accessed | tf_op | source)
XLA Modules:
  0.0 216.8 jit_solution(16758018230525117128)
XLA Ops:
  1.5 24.9 %all_to_all.35 = bf16[32,8,1024]{2,1,0:T(8,128)(2,1)S(1)} all-to-all(bf16[32,8,1024]{2,1,0:T(8,128)(2,1)S(1)} %bitcast.29), channel_id=1, replica_groups={{0,8,16,24,32,40,48,56,1,9,17,25,33,41,49,57,2,10,18,26,34,42,50,58,3,1..., dimensions={0} | all-to-all | bytes 1048576 | tf_op jit(solution)/shard_map/all_to_all | solution.py:28
  26.5 5.1 %collective-permute-start.1 = (bf16[32,4096]{1,0:T(8,128)(2,1)S(1)}, bf16[32,4096]{1,0:T(8,128)(2,1)S(1)}, u32[]{:S(2)}, u32[]{:S(2)}) collective-permute-start(bf16[32,4096]{1,0:T(8,128)(2,1)S(1)} %bitcast.32), channel_id=1, source_target_pairs={{0,448},{4,60},{8,456},{12,20},{16,464},{20,12},{24,472},{28,36},{... | collective-permute-start | bytes 786440 | tf_op jit(solution)/shard_map/ppermute | solution.py:216
  31.7 2.1 collective-permute-start
  35.5 1.9 collective-permute-start.3
  37.4 1.9 collective-permute-done
  39.4 3.0 %collective-permute-start.2 = (bf16[64,4096]{1,0:T(8,128)(2,1)S(1)}, bf16[64,4096]{1,0:T(8,128)(2,1)}, u32[]{:S(2)}, u32[]{:S(2)}) collective-permute-start(bf16[64,4096]{1,0:T(8,128)(2,1)S(1)} %pad_maximum_fusion.1.refs_0_), channel_id=1, source_target_pairs={{0,448},{4,60},{8,456},{12,20},{16,464},{20,12},{24,472},{28,36},{... | collective-permute-start | bytes 1572872 | tf_op jit(solution)/shard_map/ppermute | solution.py:216
  44.0 3.6 %all-to-all-start.1 = ((bf16[4,256,1024]{2,1,0:T(8,128)(2,1)}), bf16[4,256,1024]{2,1,0:T(8,128)(2,1)S(1)}, u32[]{:S(2)}, u32[]{:S(2)}) async-start(bf16[4,256,1024]{2,1,0:T(8,128)(2,1)} %broadcast_in_dim.22), calls=%async_computation.1 | async-start | bytes 4194304 | tf_op jit(solution)/shard_map/all_to_all | solution.py:28
  47.7 3.5 %collective-permute-start.5 = (bf16[64,4096]{1,0:T(8,128)(2,1)}, bf16[64,4096]{1,0:T(8,128)(2,1)}, u32[]{:S(2)}, u32[]{:S(2)}) collective-permute-start(bf16[64,4096]{1,0:T(8,128)(2,1)} %collective-permute-done.3.refs_1_), channel_id=1, source_target_pairs={{0,448},{4,60},{8,456},{12,20},{16,464},{20,12},{24,472},{28,36},{... | collective-permute-start | bytes 1572872 | tf_op jit(solution)/shard_map/ppermute | solution.py:216
  51.2 1.9 collective-permute-start.4
  53.1 6.2 %collective-permute-done.5.refs_2_ = bf16[64,4096]{1,0:T(8,128)(2,1)} collective-permute-done((bf16[64,4096]{1,0:T(8,128)(2,1)}, bf16[64,4096]{1,0:T(8,128)(2,1)}, u32[]{:S(2)}, u32[]{:S(2)}) %collective-permute-start.5) | collective-permute-done | bytes 524320 | tf_op jit(solution)/shard_map/ppermute | solution.py:216
  59.3 1.9 collective-permute-start.7
  61.7 3.4 %collective-permute-start.6 = (bf16[64,4096]{1,0:T(8,128)(2,1)}, bf16[64,4096]{1,0:T(8,128)(2,1)}, u32[]{:S(2)}, u32[]{:S(2)}) collective-permute-start(bf16[64,4096]{1,0:T(8,128)(2,1)} %collective-permute-done.4.refs_2_), channel_id=1, source_target_pairs={{0,448},{4,60},{8,456},{12,20},{16,464},{20,12},{24,472},{28,36},{... | collective-permute-start | bytes 1572872 | tf_op jit(solution)/shard_map/ppermute | solution.py:216
  65.4 4.3 %collective-permute-done.7.refs_3_ = bf16[64,4096]{1,0:T(8,128)(2,1)} collective-permute-done((bf16[64,4096]{1,0:T(8,128)(2,1)}, bf16[64,4096]{1,0:T(8,128)(2,1)}, u32[]{:S(2)}, u32[]{:S(2)}) %collective-permute-start.7) | collective-permute-done | bytes 524320 | tf_op jit(solution)/shard_map/ppermute | solution.py:216
  69.7 2.0 shard_map.68.weight.refs_1_
  73.4 9.9 %collective-permute-start.9 = (bf16[256,4096]{1,0:T(8,128)(2,1)}, bf16[256,4096]{1,0:T(8,128)(2,1)S(1)}, u32[]{:S(2)}, u32[]{:S(2)}) collective-permute-start(bf16[256,4096]{1,0:T(8,128)(2,1)} %copy-done), channel_id=1, source_target_pairs={{0,4},{4,0},{8,12},{12,8},{16,20},{20,16},{24,28},{28,24},{32,36},... | collective-permute-start | bytes 6291464 | tf_op jit(solution)/shard_map/ppermute | solution.py:240
  83.3 2.0 shard_map.69.weight.refs_0_
  85.4 1.9 collective-permute-start.8
  93.5 4.5 %all-to-all-start.2 = ((f32[4,2,128]{2,1,0:T(2,128)}), f32[4,2,128]{2,1,0:T(2,128)S(1)}, u32[]{:S(2)}, u32[]{:S(2)}) async-start(f32[4,2,128]{2,1,0:T(2,128)} %broadcast_in_dim.24), calls=%async_computation.2 | async-start | bytes 8192 | tf_op jit(solution)/shard_map/all_to_all | solution.py:28
  98.2 3.9 %all-to-all-done.2 = f32[4,2,128]{2,1,0:T(2,128)S(1)} async-done(((f32[4,2,128]{2,1,0:T(2,128)}), f32[4,2,128]{2,1,0:T(2,128)S(1)}, u32[]{:S(2)}, u32[]{:S(2)}) %all-to-all-start.2) | async-done | bytes 4128 | tf_op jit(solution)/shard_map/all_to_all | solution.py:28
  102.8 29.5 %all_to_all.36 = bf16[128,2,1024]{2,1,0:T(2,128)(2,1)S(1)} all-to-all(bf16[128,2,1024]{2,1,0:T(2,128)(2,1)S(1)} %reshape.120), channel_id=1, replica_groups=mesh['dp'=128,'mp'=4] {'dp'}, dimensions={0} | all-to-all | bytes 1048576 | tf_op jit(solution)/shard_map/all_to_all | solution.py:28
  133.3 15.2 %all_to_all.37 = f32[4,384,128]{2,1,0:T(8,128)S(1)} all-to-all(f32[4,384,128]{2,1,0:T(8,128)S(1)} %broadcast_in_dim.25), channel_id=1, replica_groups=mesh['dp'=128,'mp'=4] {'mp'}, dimensions={0} | all-to-all | bytes 1572864 | tf_op jit(solution)/shard_map/all_to_all | solution.py:28
  149.8 27.1 %all_to_all.38 = bf16[128,2,1152]{2,1,0:T(2,128)(2,1)S(1)} all-to-all(bf16[128,2,1152]{2,1,0:T(2,128)(2,1)S(1)} %reshape.122), channel_id=1, replica_groups=mesh['dp'=128,'mp'=4] {'dp'}, dimensions={0} | all-to-all | bytes 1179648 | tf_op jit(solution)/shard_map/all_to_all | solution.py:28
  182.7 3.5 %shard_map.74 = bf16[4,256,1024]{2,1,0:T(8,128)(2,1)S(1)} custom-call(bf16[256,512]{1,0:T(8,128)(2,1)S(1)} %get-tuple-element.64.grad_own, bf16[256,512]{1,0:T(8,128)(2,1)S(1)} %get-tuple-element.63.grad_other, bf16[256,4096]{1,0:T(8,128)(2,1)S(1)} %copy-done.4, bf16[256,4096]{1,0:T(8,128)(2,1)S(1)} %copy-done.2, bf16[256,4096]{1,0:T(8,128)(2,1)S(1)} %copy-done.8, ...), custom_call_target="tpu_custom_call" | custom-call | flops 2147483648 | bytes 8388608 | tf_op jit(solution)/shard_map/pallas_call | solution.py:170
  186.2 29.2 %all_to_all.39 = bf16[4,256,1024]{2,1,0:T(8,128)(2,1)S(1)} all-to-all(bf16[4,256,1024]{2,1,0:T(8,128)(2,1)S(1)} %shard_map.74), channel_id=1, replica_groups=mesh['dp'=128,'mp'=4] {'mp'}, dimensions={0} | all-to-all | bytes 4194304 | tf_op jit(solution)/shard_map/all_to_all | solution.py:28
  (106 shorter events, 23.0 us)
Async XLA Ops:
  26.5 8.9 %collective-permute-start.1 = (bf16[32,4096]{1,0:T(8,128)(2,1)S(1)}, bf16[32,4096]{1,0:T(8,128)(2,1)S(1)}, u32[]{:S(2)}, u32[]{:S(2)}) collective-permute-start(bf16[32,4096]{1,0:T(8,128)(2,1)S(1)} %bitcast.32), channel_id=1, source_target_pairs={{0,448},{4,60},{8,456},{12,20},{16,464},{20,12},{24,472},{28,36},{... | collective-permute-start | bytes 786440 | tf_op jit(solution)/shard_map/ppermute | solution.py:216
  31.7 10.7 %copy-start.10 = (bf16[128,1024]{1,0:T(8,128)(2,1)S(1)}, bf16[128,1024]{1,0:T(8,128)(2,1)}, u32[]{:S(2)}) copy-start(bf16[128,1024]{1,0:T(8,128)(2,1)} %param.6) | copy-start | bytes 786436
  31.7 10.7 %copy-start.11 = (bf16[128,1024]{1,0:T(8,128)(2,1)S(1)}, bf16[128,1024]{1,0:T(8,128)(2,1)}, u32[]{:S(2)}) copy-start(bf16[128,1024]{1,0:T(8,128)(2,1)} %param.5) | copy-start | bytes 786436
  31.7 7.5 %collective-permute-start = (bf16[32,4096]{1,0:T(8,128)(2,1)S(1)}, bf16[32,4096]{1,0:T(8,128)(2,1)S(1)}, u32[]{:S(2)}, u32[]{:S(2)}) collective-permute-start(bf16[32,4096]{1,0:T(8,128)(2,1)S(1)} %bitcast.30), channel_id=1, source_target_pairs={{0,64},{4,12},{8,72},{12,4},{16,80},{20,28},{24,88},{28,20},{32,96... | collective-permute-start | bytes 786440 | tf_op jit(solution)/shard_map/ppermute | solution.py:216
  35.5 12.2 %collective-permute-start.3 = (bf16[64,4096]{1,0:T(8,128)(2,1)S(1)}, bf16[64,4096]{1,0:T(8,128)(2,1)}, u32[]{:S(2)}, u32[]{:S(2)}) collective-permute-start(bf16[64,4096]{1,0:T(8,128)(2,1)S(1)} %pad_maximum_fusion.2.refs_0_), channel_id=1, source_target_pairs={{0,64},{4,12},{8,72},{12,4},{16,80},{20,28},{24,88},{28,20},{32,96... | collective-permute-start | bytes 1572872 | tf_op jit(solution)/shard_map/ppermute | solution.py:216
  39.4 11.8 %collective-permute-start.2 = (bf16[64,4096]{1,0:T(8,128)(2,1)S(1)}, bf16[64,4096]{1,0:T(8,128)(2,1)}, u32[]{:S(2)}, u32[]{:S(2)}) collective-permute-start(bf16[64,4096]{1,0:T(8,128)(2,1)S(1)} %pad_maximum_fusion.1.refs_0_), channel_id=1, source_target_pairs={{0,448},{4,60},{8,456},{12,20},{16,464},{20,12},{24,472},{28,36},{... | collective-permute-start | bytes 1572872 | tf_op jit(solution)/shard_map/ppermute | solution.py:216
  44.0 29.0 %all-to-all-start.1 = ((bf16[4,256,1024]{2,1,0:T(8,128)(2,1)}), bf16[4,256,1024]{2,1,0:T(8,128)(2,1)S(1)}, u32[]{:S(2)}, u32[]{:S(2)}) async-start(bf16[4,256,1024]{2,1,0:T(8,128)(2,1)} %broadcast_in_dim.22), calls=%async_computation.1 | async-start | bytes 4194304 | tf_op jit(solution)/shard_map/all_to_all | solution.py:28
  47.7 11.6 %collective-permute-start.5 = (bf16[64,4096]{1,0:T(8,128)(2,1)}, bf16[64,4096]{1,0:T(8,128)(2,1)}, u32[]{:S(2)}, u32[]{:S(2)}) collective-permute-start(bf16[64,4096]{1,0:T(8,128)(2,1)} %collective-permute-done.3.refs_1_), channel_id=1, source_target_pairs={{0,448},{4,60},{8,456},{12,20},{16,464},{20,12},{24,472},{28,36},{... | collective-permute-start | bytes 1572872 | tf_op jit(solution)/shard_map/ppermute | solution.py:216
  51.2 10.5 %collective-permute-start.4 = (bf16[64,4096]{1,0:T(8,128)(2,1)}, bf16[64,4096]{1,0:T(8,128)(2,1)}, u32[]{:S(2)}, u32[]{:S(2)}) collective-permute-start(bf16[64,4096]{1,0:T(8,128)(2,1)} %collective-permute-done.2.refs_1_), channel_id=1, source_target_pairs={{0,64},{4,12},{8,72},{12,4},{16,80},{20,28},{24,88},{28,20},{32,96... | collective-permute-start | bytes 1572872 | tf_op jit(solution)/shard_map/ppermute | solution.py:216
  59.3 10.4 %collective-permute-start.7 = (bf16[64,4096]{1,0:T(8,128)(2,1)}, bf16[64,4096]{1,0:T(8,128)(2,1)}, u32[]{:S(2)}, u32[]{:S(2)}) collective-permute-start(bf16[64,4096]{1,0:T(8,128)(2,1)} %collective-permute-done.5.refs_2_), channel_id=1, source_target_pairs={{0,64},{4,12},{8,72},{12,4},{16,80},{20,28},{24,88},{28,20},{32,96... | collective-permute-start | bytes 1572872 | tf_op jit(solution)/shard_map/ppermute | solution.py:216
  61.7 11.6 %collective-permute-start.6 = (bf16[64,4096]{1,0:T(8,128)(2,1)}, bf16[64,4096]{1,0:T(8,128)(2,1)}, u32[]{:S(2)}, u32[]{:S(2)}) collective-permute-start(bf16[64,4096]{1,0:T(8,128)(2,1)} %collective-permute-done.4.refs_2_), channel_id=1, source_target_pairs={{0,448},{4,60},{8,456},{12,20},{16,464},{20,12},{24,472},{28,36},{... | collective-permute-start | bytes 1572872 | tf_op jit(solution)/shard_map/ppermute | solution.py:216
  73.4 15.8 %collective-permute-start.9 = (bf16[256,4096]{1,0:T(8,128)(2,1)}, bf16[256,4096]{1,0:T(8,128)(2,1)S(1)}, u32[]{:S(2)}, u32[]{:S(2)}) collective-permute-start(bf16[256,4096]{1,0:T(8,128)(2,1)} %copy-done), channel_id=1, source_target_pairs={{0,4},{4,0},{8,12},{12,8},{16,20},{20,16},{24,28},{28,24},{32,36},... | collective-permute-start | bytes 6291464 | tf_op jit(solution)/shard_map/ppermute | solution.py:240
  83.3 4.0 %copy-start.13 = (s32[128,1]{0,1:T(1,128)S(1)}, s32[128,1]{0,1:T(1,128)}, u32[]{:S(2)}) copy-start(s32[128,1]{0,1:T(1,128)} %param.9) | copy-start | bytes 1540
  83.3 4.2 %copy-start.1 = (bf16[256,4096]{1,0:T(8,128)(2,1)S(1)}, bf16[256,4096]{1,0:T(8,128)(2,1)}, u32[]{:S(2)}) copy-start(bf16[256,4096]{1,0:T(8,128)(2,1)} %copy-done) | copy-start | bytes 6291460
  85.4 3.0 %copy-start.3 = (bf16[256,4096]{1,0:T(8,128)(2,1)}, bf16[256,4096]{1,0:T(8,128)(2,1)S(1)}, u32[]{:S(2)}) copy-start(bf16[256,4096]{1,0:T(8,128)(2,1)S(1)} %shard_map.69.weight.refs_0_) | copy-start | bytes 6291460
  85.4 6.1 %collective-permute-start.8 = (bf16[256,4096]{1,0:T(8,128)(2,1)S(1)}, bf16[256,4096]{1,0:T(8,128)(2,1)S(1)}, u32[]{:S(2)}, u32[]{:S(2)}) collective-permute-start(bf16[256,4096]{1,0:T(8,128)(2,1)S(1)} %shard_map.69.weight.refs_0_), channel_id=1, source_target_pairs={{0,4},{4,0},{8,12},{12,8},{16,20},{20,16},{24,28},{28,24},{32,36},... | collective-permute-start | bytes 6291464 | tf_op jit(solution)/shard_map/ppermute | solution.py:240
  89.2 1.3 copy-start.5
  91.4 1.3 copy-start.7
  93.5 8.6 %all-to-all-start.2 = ((f32[4,2,128]{2,1,0:T(2,128)}), f32[4,2,128]{2,1,0:T(2,128)S(1)}, u32[]{:S(2)}, u32[]{:S(2)}) async-start(f32[4,2,128]{2,1,0:T(2,128)} %broadcast_in_dim.24), calls=%async_computation.2 | async-start | bytes 8192 | tf_op jit(solution)/shard_map/all_to_all | solution.py:28
  176.9 2.6 %copy-start.12 = (s32[128]{0:T(128)S(1)}, s32[128]{0:T(128)}, u32[]{:S(2)}) copy-start(s32[128]{0:T(128)} %param.8) | copy-start | bytes 1540
  177.3 3.2 %copy-start.8 = (bf16[256,4096]{1,0:T(8,128)(2,1)S(1)}, bf16[256,4096]{1,0:T(8,128)(2,1)}, u32[]{:S(2)}) copy-start(bf16[256,4096]{1,0:T(8,128)(2,1)} %copy-done.7) | copy-start | bytes 6291460
  179.7 1.6 copy-start.6
  180.0 2.1 copy-start.4
  180.2 2.5 %copy-start.2 = (bf16[256,4096]{1,0:T(8,128)(2,1)S(1)}, bf16[256,4096]{1,0:T(8,128)(2,1)}, u32[]{:S(2)}) copy-start(bf16[256,4096]{1,0:T(8,128)(2,1)} %copy-done) | copy-start | bytes 6291460
  (2 other events, 2.1 us)

commit v8 on v7

--- a/solution.py
+++ b/solution.py
@@ -213,7 +213,7 @@
 
     for step in range(BLOCKS):
         behind, ahead = [
-            lax.ppermute(held[stream], "dp", matchings[(step + stream) % 2])
+            lax.ppermute(held[stream], "dp", matchings[(step + 1 - stream) % 2])
             for stream in range(2)
         ]
         ahead, _ = lax.optimization_barrier((ahead, held[0]))
@@ -226,7 +226,7 @@
                     (behind, weight_ahead, states)
                 )
             came = (behind, ahead)[stream]
-            at, is_upper = (position + stream) // 2, (position + stream) % 2
+            at, is_upper = (position + 1 - stream) // 2, (position + 1 - stream) % 2
             if step == 0:
                 half = halves[stream]
                 came = jnp.concatenate(

time: 218 us -> 217 us (level)
  waiting for transfers between devices: 19.7 us -> 12.5 us
  starting transfers between devices: 42.6 us -> 48.4 us
    ppermute x8, waiting for transfers between devices: 14.8 us -> 7.67 us  [on_device(): lax.ppermute(held[stream], 'dp', matchings[(step + 1 - stream) % 2])]
    ppermute x8, starting transfers between devices: 22.8 us -> 28.4 us  [on_device(): lax.ppermute(held[stream], 'dp', matchings[(step + 1 - stream) % 2])]
  transfers between devices with their start and end apart: 12 -> 12, of which waited for: 8 -> 5; matrix products, arithmetic and copies ran while one was open for 1% -> 1% of each run, Pallas kernels for 3% -> 3%
where the time goes in v8:
time: 217 us; the launch traced here: 216 us
  blocking collectives  126 us (58%)
  starting transfers between devices  48.4 us (22%)
  waiting for transfers between devices  12.5 us (6%)
  Pallas kernels  10.7 us (5%)
  local copies, waits for them, and re-layouts  10.4 us (5%)
  matrix products  3.28 us (2%)
  other arithmetic  2.75 us (1%)
    all_to_all x5, blocking collectives, swap(): lax.all_to_all(x, axis, split_axis=0, concat_axis=0, tiled=True, axis_ind...  126 us
    ppermute x8, starting transfers between devices, on_device(): lax.ppermute(held[stream], 'dp', matchings[(step + 1 - stream) % 2])  28.4 us
    ppermute x2, starting transfers between devices, on_device(): weights += [lax.ppermute(weight, 'dp', other_core) for weight in weights]  11.9 us
    all_to_all x2, starting transfers between devices, swap(): lax.all_to_all(x, axis, split_axis=0, concat_axis=0, tiled=True, axis_ind...  8.07 us
    ppermute x8, waiting for transfers between devices, on_device(): lax.ppermute(held[stream], 'dp', matchings[(step + 1 - stream) % 2])  7.67 us
    unnamed x30, local copies, waits for them, and re-layouts  5 us
  transfers between devices with their start and end apart: 12, of which 5 were waited for; matrix products, arithmetic and copies ran while one was open for 1% of the time, Pallas kernels for 3%

profile of v8, /device:TPU:1, one launch (start us, length us, event | category | flops | bytes accessed | tf_op | source)
XLA Modules:
  0.0 216.0 jit_solution(11003023071959544086)
XLA Ops:
  1.5 24.9 %all_to_all.35 = bf16[32,8,1024]{2,1,0:T(8,128)(2,1)S(1)} all-to-all(bf16[32,8,1024]{2,1,0:T(8,128)(2,1)S(1)} %bitcast.29), channel_id=1, replica_groups={{0,8,16,24,32,40,48,56,1,9,17,25,33,41,49,57,2,10,18,26,34,42,50,58,3,1..., dimensions={0} | all-to-all | bytes 1048576 | tf_op jit(solution)/shard_map/all_to_all | solution.py:28
  26.5 3.2 %collective-permute-start.1 = (bf16[32,4096]{1,0:T(8,128)(2,1)S(1)}, bf16[32,4096]{1,0:T(8,128)(2,1)S(1)}, u32[]{:S(2)}, u32[]{:S(2)}) collective-permute-start(bf16[32,4096]{1,0:T(8,128)(2,1)S(1)} %bitcast.32), channel_id=1, source_target_pairs={{0,64},{4,12},{8,72},{12,4},{16,80},{20,28},{24,88},{28,20},{32,96... | collective-permute-start | bytes 786440 | tf_op jit(solution)/shard_map/ppermute | solution.py:216
  29.8 5.0 %collective-permute-start = (bf16[32,4096]{1,0:T(8,128)(2,1)S(1)}, bf16[32,4096]{1,0:T(8,128)(2,1)S(1)}, u32[]{:S(2)}, u32[]{:S(2)}) collective-permute-start(bf16[32,4096]{1,0:T(8,128)(2,1)S(1)} %bitcast.30), channel_id=1, source_target_pairs={{0,448},{4,60},{8,456},{12,20},{16,464},{20,12},{24,472},{28,36},{... | collective-permute-start | bytes 786440 | tf_op jit(solution)/shard_map/ppermute | solution.py:216
  35.0 3.9 %collective-permute-start.3 = (bf16[64,4096]{1,0:T(8,128)(2,1)S(1)}, bf16[64,4096]{1,0:T(8,128)(2,1)}, u32[]{:S(2)}, u32[]{:S(2)}) collective-permute-start(bf16[64,4096]{1,0:T(8,128)(2,1)S(1)} %pad_maximum_fusion.2.refs_0_), channel_id=1, source_target_pairs={{0,448},{4,60},{8,456},{12,20},{16,464},{20,12},{24,472},{28,36},{... | collective-permute-start | bytes 1572872 | tf_op jit(solution)/shard_map/ppermute | solution.py:216
  38.9 1.9 collective-permute-start.2
  40.9 1.6 broadcast_in_dim.22
  42.5 3.6 %all-to-all-start.1 = ((bf16[4,256,1024]{2,1,0:T(8,128)(2,1)}), bf16[4,256,1024]{2,1,0:T(8,128)(2,1)S(1)}, u32[]{:S(2)}, u32[]{:S(2)}) async-start(bf16[4,256,1024]{2,1,0:T(8,128)(2,1)} %broadcast_in_dim.22), calls=%async_computation.1 | async-start | bytes 4194304 | tf_op jit(solution)/shard_map/all_to_all | solution.py:28
  46.5 3.0 %collective-permute-start.5 = (bf16[64,4096]{1,0:T(8,128)(2,1)}, bf16[64,4096]{1,0:T(8,128)(2,1)}, u32[]{:S(2)}, u32[]{:S(2)}) collective-permute-start(bf16[64,4096]{1,0:T(8,128)(2,1)} %collective-permute-done.3.refs_1_), channel_id=1, source_target_pairs={{0,64},{4,12},{8,72},{12,4},{16,80},{20,28},{24,88},{28,20},{32,96... | collective-permute-start | bytes 1572872 | tf_op jit(solution)/shard_map/ppermute | solution.py:216
  49.5 4.6 %collective-permute-start.4 = (bf16[64,4096]{1,0:T(8,128)(2,1)}, bf16[64,4096]{1,0:T(8,128)(2,1)}, u32[]{:S(2)}, u32[]{:S(2)}) collective-permute-start(bf16[64,4096]{1,0:T(8,128)(2,1)} %collective-permute-done.2.refs_1_), channel_id=1, source_target_pairs={{0,448},{4,60},{8,456},{12,20},{16,464},{20,12},{24,472},{28,36},{... | collective-permute-start | bytes 1572872 | tf_op jit(solution)/shard_map/ppermute | solution.py:216
  54.2 2.7 %collective-permute-done.5.refs_2_ = bf16[64,4096]{1,0:T(8,128)(2,1)} collective-permute-done((bf16[64,4096]{1,0:T(8,128)(2,1)}, bf16[64,4096]{1,0:T(8,128)(2,1)}, u32[]{:S(2)}, u32[]{:S(2)}) %collective-permute-start.5) | collective-permute-done | bytes 524320 | tf_op jit(solution)/shard_map/ppermute | solution.py:216
  56.9 4.4 %collective-permute-start.7 = (bf16[64,4096]{1,0:T(8,128)(2,1)}, bf16[64,4096]{1,0:T(8,128)(2,1)}, u32[]{:S(2)}, u32[]{:S(2)}) collective-permute-start(bf16[64,4096]{1,0:T(8,128)(2,1)} %collective-permute-done.5.refs_2_), channel_id=1, source_target_pairs={{0,448},{4,60},{8,456},{12,20},{16,464},{20,12},{24,472},{28,36},{... | collective-permute-start | bytes 1572872 | tf_op jit(solution)/shard_map/ppermute | solution.py:216
  61.3 2.4 %collective-permute-start.6 = (bf16[64,4096]{1,0:T(8,128)(2,1)}, bf16[64,4096]{1,0:T(8,128)(2,1)}, u32[]{:S(2)}, u32[]{:S(2)}) collective-permute-start(bf16[64,4096]{1,0:T(8,128)(2,1)} %collective-permute-done.4.refs_2_), channel_id=1, source_target_pairs={{0,64},{4,12},{8,72},{12,4},{16,80},{20,28},{24,88},{28,20},{32,96... | collective-permute-start | bytes 1572872 | tf_op jit(solution)/shard_map/ppermute | solution.py:216
  64.0 4.6 %collective-permute-done.7.refs_3_ = bf16[64,4096]{1,0:T(8,128)(2,1)} collective-permute-done((bf16[64,4096]{1,0:T(8,128)(2,1)}, bf16[64,4096]{1,0:T(8,128)(2,1)}, u32[]{:S(2)}, u32[]{:S(2)}) %collective-permute-start.7) | collective-permute-done | bytes 524320 | tf_op jit(solution)/shard_map/ppermute | solution.py:216
  68.5 2.0 shard_map.68.weight.refs_1_
  71.9 10.0 %collective-permute-start.9 = (bf16[256,4096]{1,0:T(8,128)(2,1)}, bf16[256,4096]{1,0:T(8,128)(2,1)S(1)}, u32[]{:S(2)}, u32[]{:S(2)}) collective-permute-start(bf16[256,4096]{1,0:T(8,128)(2,1)} %copy-done), channel_id=1, source_target_pairs={{0,4},{4,0},{8,12},{12,8},{16,20},{20,16},{24,28},{28,24},{32,36},... | collective-permute-start | bytes 6291464 | tf_op jit(solution)/shard_map/ppermute | solution.py:240
  82.0 2.0 shard_map.69.weight.refs_0_
  84.0 1.9 collective-permute-start.8
  92.1 4.5 %all-to-all-start.2 = ((f32[4,2,128]{2,1,0:T(2,128)}), f32[4,2,128]{2,1,0:T(2,128)S(1)}, u32[]{:S(2)}, u32[]{:S(2)}) async-start(f32[4,2,128]{2,1,0:T(2,128)} %broadcast_in_dim.24), calls=%async_computation.2 | async-start | bytes 8192 | tf_op jit(solution)/shard_map/all_to_all | solution.py:28
  96.8 3.9 %all-to-all-done.2 = f32[4,2,128]{2,1,0:T(2,128)S(1)} async-done(((f32[4,2,128]{2,1,0:T(2,128)}), f32[4,2,128]{2,1,0:T(2,128)S(1)}, u32[]{:S(2)}, u32[]{:S(2)}) %all-to-all-start.2) | async-done | bytes 4128 | tf_op jit(solution)/shard_map/all_to_all | solution.py:28
  101.4 30.1 %all_to_all.36 = bf16[128,2,1024]{2,1,0:T(2,128)(2,1)S(1)} all-to-all(bf16[128,2,1024]{2,1,0:T(2,128)(2,1)S(1)} %reshape.120), channel_id=1, replica_groups=mesh['dp'=128,'mp'=4] {'dp'}, dimensions={0} | all-to-all | bytes 1048576 | tf_op jit(solution)/shard_map/all_to_all | solution.py:28
  132.5 15.2 %all_to_all.37 = f32[4,384,128]{2,1,0:T(8,128)S(1)} all-to-all(f32[4,384,128]{2,1,0:T(8,128)S(1)} %broadcast_in_dim.25), channel_id=1, replica_groups=mesh['dp'=128,'mp'=4] {'mp'}, dimensions={0} | all-to-all | bytes 1572864 | tf_op jit(solution)/shard_map/all_to_all | solution.py:28
  149.1 27.1 %all_to_all.38 = bf16[128,2,1152]{2,1,0:T(2,128)(2,1)S(1)} all-to-all(bf16[128,2,1152]{2,1,0:T(2,128)(2,1)S(1)} %reshape.122), channel_id=1, replica_groups=mesh['dp'=128,'mp'=4] {'dp'}, dimensions={0} | all-to-all | bytes 1179648 | tf_op jit(solution)/shard_map/all_to_all | solution.py:28
  181.9 3.5 %shard_map.74 = bf16[4,256,1024]{2,1,0:T(8,128)(2,1)S(1)} custom-call(bf16[256,512]{1,0:T(8,128)(2,1)S(1)} %get-tuple-element.64.grad_own, bf16[256,512]{1,0:T(8,128)(2,1)S(1)} %get-tuple-element.63.grad_other, bf16[256,4096]{1,0:T(8,128)(2,1)S(1)} %copy-done.4, bf16[256,4096]{1,0:T(8,128)(2,1)S(1)} %copy-done.2, bf16[256,4096]{1,0:T(8,128)(2,1)S(1)} %copy-done.8, ...), custom_call_target="tpu_custom_call" | custom-call | flops 2147483648 | bytes 8388608 | tf_op jit(solution)/shard_map/pallas_call | solution.py:170
  185.4 29.2 %all_to_all.39 = bf16[4,256,1024]{2,1,0:T(8,128)(2,1)S(1)} all-to-all(bf16[4,256,1024]{2,1,0:T(8,128)(2,1)S(1)} %shard_map.74), channel_id=1, replica_groups=mesh['dp'=128,'mp'=4] {'mp'}, dimensions={0} | all-to-all | bytes 4194304 | tf_op jit(solution)/shard_map/all_to_all | solution.py:28
  (106 shorter events, 19.4 us)
Async XLA Ops:
  26.5 8.3 %collective-permute-start.1 = (bf16[32,4096]{1,0:T(8,128)(2,1)S(1)}, bf16[32,4096]{1,0:T(8,128)(2,1)S(1)}, u32[]{:S(2)}, u32[]{:S(2)}) collective-permute-start(bf16[32,4096]{1,0:T(8,128)(2,1)S(1)} %bitcast.32), channel_id=1, source_target_pairs={{0,64},{4,12},{8,72},{12,4},{16,80},{20,28},{24,88},{28,20},{32,96... | collective-permute-start | bytes 786440 | tf_op jit(solution)/shard_map/ppermute | solution.py:216
  29.8 11.0 %copy-start.10 = (bf16[128,1024]{1,0:T(8,128)(2,1)S(1)}, bf16[128,1024]{1,0:T(8,128)(2,1)}, u32[]{:S(2)}) copy-start(bf16[128,1024]{1,0:T(8,128)(2,1)} %param.6) | copy-start | bytes 786436
  29.8 11.0 %copy-start.11 = (bf16[128,1024]{1,0:T(8,128)(2,1)S(1)}, bf16[128,1024]{1,0:T(8,128)(2,1)}, u32[]{:S(2)}) copy-start(bf16[128,1024]{1,0:T(8,128)(2,1)} %param.5) | copy-start | bytes 786436
  29.8 9.0 %collective-permute-start = (bf16[32,4096]{1,0:T(8,128)(2,1)S(1)}, bf16[32,4096]{1,0:T(8,128)(2,1)S(1)}, u32[]{:S(2)}, u32[]{:S(2)}) collective-permute-start(bf16[32,4096]{1,0:T(8,128)(2,1)S(1)} %bitcast.30), channel_id=1, source_target_pairs={{0,448},{4,60},{8,456},{12,20},{16,464},{20,12},{24,472},{28,36},{... | collective-permute-start | bytes 786440 | tf_op jit(solution)/shard_map/ppermute | solution.py:216
  35.0 11.5 %collective-permute-start.3 = (bf16[64,4096]{1,0:T(8,128)(2,1)S(1)}, bf16[64,4096]{1,0:T(8,128)(2,1)}, u32[]{:S(2)}, u32[]{:S(2)}) collective-permute-start(bf16[64,4096]{1,0:T(8,128)(2,1)S(1)} %pad_maximum_fusion.2.refs_0_), channel_id=1, source_target_pairs={{0,448},{4,60},{8,456},{12,20},{16,464},{20,12},{24,472},{28,36},{... | collective-permute-start | bytes 1572872 | tf_op jit(solution)/shard_map/ppermute | solution.py:216
  38.9 10.6 %collective-permute-start.2 = (bf16[64,4096]{1,0:T(8,128)(2,1)S(1)}, bf16[64,4096]{1,0:T(8,128)(2,1)}, u32[]{:S(2)}, u32[]{:S(2)}) collective-permute-start(bf16[64,4096]{1,0:T(8,128)(2,1)S(1)} %pad_maximum_fusion.1.refs_0_), channel_id=1, source_target_pairs={{0,64},{4,12},{8,72},{12,4},{16,80},{20,28},{24,88},{28,20},{32,96... | collective-permute-start | bytes 1572872 | tf_op jit(solution)/shard_map/ppermute | solution.py:216
  42.5 29.3 %all-to-all-start.1 = ((bf16[4,256,1024]{2,1,0:T(8,128)(2,1)}), bf16[4,256,1024]{2,1,0:T(8,128)(2,1)S(1)}, u32[]{:S(2)}, u32[]{:S(2)}) async-start(bf16[4,256,1024]{2,1,0:T(8,128)(2,1)} %broadcast_in_dim.22), calls=%async_computation.1 | async-start | bytes 4194304 | tf_op jit(solution)/shard_map/all_to_all | solution.py:28
  46.5 10.4 %collective-permute-start.5 = (bf16[64,4096]{1,0:T(8,128)(2,1)}, bf16[64,4096]{1,0:T(8,128)(2,1)}, u32[]{:S(2)}, u32[]{:S(2)}) collective-permute-start(bf16[64,4096]{1,0:T(8,128)(2,1)} %collective-permute-done.3.refs_1_), channel_id=1, source_target_pairs={{0,64},{4,12},{8,72},{12,4},{16,80},{20,28},{24,88},{28,20},{32,96... | collective-permute-start | bytes 1572872 | tf_op jit(solution)/shard_map/ppermute | solution.py:216
  49.5 11.8 %collective-permute-start.4 = (bf16[64,4096]{1,0:T(8,128)(2,1)}, bf16[64,4096]{1,0:T(8,128)(2,1)}, u32[]{:S(2)}, u32[]{:S(2)}) collective-permute-start(bf16[64,4096]{1,0:T(8,128)(2,1)} %collective-permute-done.2.refs_1_), channel_id=1, source_target_pairs={{0,448},{4,60},{8,456},{12,20},{16,464},{20,12},{24,472},{28,36},{... | collective-permute-start | bytes 1572872 | tf_op jit(solution)/shard_map/ppermute | solution.py:216
  56.9 11.6 %collective-permute-start.7 = (bf16[64,4096]{1,0:T(8,128)(2,1)}, bf16[64,4096]{1,0:T(8,128)(2,1)}, u32[]{:S(2)}, u32[]{:S(2)}) collective-permute-start(bf16[64,4096]{1,0:T(8,128)(2,1)} %collective-permute-done.5.refs_2_), channel_id=1, source_target_pairs={{0,448},{4,60},{8,456},{12,20},{16,464},{20,12},{24,472},{28,36},{... | collective-permute-start | bytes 1572872 | tf_op jit(solution)/shard_map/ppermute | solution.py:216
  61.3 10.5 %collective-permute-start.6 = (bf16[64,4096]{1,0:T(8,128)(2,1)}, bf16[64,4096]{1,0:T(8,128)(2,1)}, u32[]{:S(2)}, u32[]{:S(2)}) collective-permute-start(bf16[64,4096]{1,0:T(8,128)(2,1)} %collective-permute-done.4.refs_2_), channel_id=1, source_target_pairs={{0,64},{4,12},{8,72},{12,4},{16,80},{20,28},{24,88},{28,20},{32,96... | collective-permute-start | bytes 1572872 | tf_op jit(solution)/shard_map/ppermute | solution.py:216
  71.9 16.0 %collective-permute-start.9 = (bf16[256,4096]{1,0:T(8,128)(2,1)}, bf16[256,4096]{1,0:T(8,128)(2,1)S(1)}, u32[]{:S(2)}, u32[]{:S(2)}) collective-permute-start(bf16[256,4096]{1,0:T(8,128)(2,1)} %copy-done), channel_id=1, source_target_pairs={{0,4},{4,0},{8,12},{12,8},{16,20},{20,16},{24,28},{28,24},{32,36},... | collective-permute-start | bytes 6291464 | tf_op jit(solution)/shard_map/ppermute | solution.py:240
  82.0 4.0 %copy-start.13 = (s32[128,1]{0,1:T(1,128)S(1)}, s32[128,1]{0,1:T(1,128)}, u32[]{:S(2)}) copy-start(s32[128,1]{0,1:T(1,128)} %param.9) | copy-start | bytes 1540
  82.0 4.2 %copy-start.1 = (bf16[256,4096]{1,0:T(8,128)(2,1)S(1)}, bf16[256,4096]{1,0:T(8,128)(2,1)}, u32[]{:S(2)}) copy-start(bf16[256,4096]{1,0:T(8,128)(2,1)} %copy-done) | copy-start | bytes 6291460
  84.0 3.0 %copy-start.3 = (bf16[256,4096]{1,0:T(8,128)(2,1)}, bf16[256,4096]{1,0:T(8,128)(2,1)S(1)}, u32[]{:S(2)}) copy-start(bf16[256,4096]{1,0:T(8,128)(2,1)S(1)} %shard_map.69.weight.refs_0_) | copy-start | bytes 6291460
  84.0 6.1 %collective-permute-start.8 = (bf16[256,4096]{1,0:T(8,128)(2,1)S(1)}, bf16[256,4096]{1,0:T(8,128)(2,1)S(1)}, u32[]{:S(2)}, u32[]{:S(2)}) collective-permute-start(bf16[256,4096]{1,0:T(8,128)(2,1)S(1)} %shard_map.69.weight.refs_0_), channel_id=1, source_target_pairs={{0,4},{4,0},{8,12},{12,8},{16,20},{20,16},{24,28},{28,24},{32,36},... | collective-permute-start | bytes 6291464 | tf_op jit(solution)/shard_map/ppermute | solution.py:240
  87.8 1.3 copy-start.5
  90.1 1.3 copy-start.7
  92.1 8.6 %all-to-all-start.2 = ((f32[4,2,128]{2,1,0:T(2,128)}), f32[4,2,128]{2,1,0:T(2,128)S(1)}, u32[]{:S(2)}, u32[]{:S(2)}) async-start(f32[4,2,128]{2,1,0:T(2,128)} %broadcast_in_dim.24), calls=%async_computation.2 | async-start | bytes 8192 | tf_op jit(solution)/shard_map/all_to_all | solution.py:28
  176.1 2.6 %copy-start.12 = (s32[128]{0:T(128)S(1)}, s32[128]{0:T(128)}, u32[]{:S(2)}) copy-start(s32[128]{0:T(128)} %param.8) | copy-start | bytes 1540
  176.5 3.2 %copy-start.8 = (bf16[256,4096]{1,0:T(8,128)(2,1)S(1)}, bf16[256,4096]{1,0:T(8,128)(2,1)}, u32[]{:S(2)}) copy-start(bf16[256,4096]{1,0:T(8,128)(2,1)} %copy-done.7) | copy-start | bytes 6291460
  179.0 1.6 copy-start.6
  179.2 2.1 copy-start.4
  179.5 2.5 %copy-start.2 = (bf16[256,4096]{1,0:T(8,128)(2,1)S(1)}, bf16[256,4096]{1,0:T(8,128)(2,1)}, u32[]{:S(2)}) copy-start(bf16[256,4096]{1,0:T(8,128)(2,1)} %copy-done) | copy-start | bytes 6291460
  (2 other events, 2.1 us)

commit v9 on v8

--- a/solution.py
+++ b/solution.py
@@ -174,7 +174,7 @@
         in_specs=[pl.BlockSpec((rows, width), lambda n: (0, 0))] * 2
         + [pl.BlockSpec((depth, tile), lambda n: (0, n))] * len(weights),
         out_specs=pl.BlockSpec((1, rows, tile), lambda n: (n // per_part, 0, n % per_part)),
-        compiler_params=pltpu.CompilerParams(vmem_limit_bytes=24 * 2**20),
+        compiler_params=pltpu.CompilerParams(vmem_limit_bytes=46 * 2**20),
         cost_estimate=pl.CostEstimate(
             flops=4 * rows * width * columns_all,
             bytes_accessed=4 * width * columns_all,

time: 217 us -> 218 us (level)
    unnamed x30 -> x26, local copies, waits for them, and re-layouts: 5 us -> 4.55 us
where the time goes in v9:
time: 218 us; the launch traced here: 217 us
  blocking collectives  126 us (58%)
  starting transfers between devices  48.4 us (22%)
  waiting for transfers between devices  12.5 us (6%)
  Pallas kernels  12.1 us (6%)
  local copies, waits for them, and re-layouts  9.97 us (5%)
  matrix products  3.1 us (1%)
  other arithmetic  2.74 us (1%)
    all_to_all x5, blocking collectives, swap(): lax.all_to_all(x, axis, split_axis=0, concat_axis=0, tiled=True, axis_ind...  126 us
    ppermute x8, starting transfers between devices, on_device(): lax.ppermute(held[stream], 'dp', matchings[(step + 1 - stream) % 2])  28.5 us
    ppermute x2, starting transfers between devices, on_device(): weights += [lax.ppermute(weight, 'dp', other_core) for weight in weights]  11.9 us
    all_to_all x2, starting transfers between devices, swap(): lax.all_to_all(x, axis, split_axis=0, concat_axis=0, tiled=True, axis_ind...  8.07 us
    ppermute x8, waiting for transfers between devices, on_device(): lax.ppermute(held[stream], 'dp', matchings[(step + 1 - stream) % 2])  7.65 us
    pallas_call x1, Pallas kernels, spread(): pl.pallas_call(spread_kernel, grid=(parts * per_part,), out_shape=jax.Sha...  4.87 us
    unnamed x26, local copies, waits for them, and re-layouts  4.55 us
  transfers between devices with their start and end apart: 12, of which 5 were waited for; matrix products, arithmetic and copies ran while one was open for 1% of the time, Pallas kernels for 3%

profile of v9, /device:TPU:1, one launch (start us, length us, event | category | flops | bytes accessed | tf_op | source)
XLA Modules:
  0.0 216.8 jit_solution(3524615066445287412)
XLA Ops:
  1.5 24.9 %all_to_all.35 = bf16[32,8,1024]{2,1,0:T(8,128)(2,1)S(1)} all-to-all(bf16[32,8,1024]{2,1,0:T(8,128)(2,1)S(1)} %bitcast.29), channel_id=1, replica_groups={{0,8,16,24,32,40,48,56,1,9,17,25,33,41,49,57,2,10,18,26,34,42,50,58,3,1..., dimensions={0} | all-to-all | bytes 1048576 | tf_op jit(solution)/shard_map/all_to_all | solution.py:28
  26.5 3.2 %collective-permute-start.1 = (bf16[32,4096]{1,0:T(8,128)(2,1)S(1)}, bf16[32,4096]{1,0:T(8,128)(2,1)S(1)}, u32[]{:S(2)}, u32[]{:S(2)}) collective-permute-start(bf16[32,4096]{1,0:T(8,128)(2,1)S(1)} %bitcast.32), channel_id=1, source_target_pairs={{0,64},{4,12},{8,72},{12,4},{16,80},{20,28},{24,88},{28,20},{32,96... | collective-permute-start | bytes 786440 | tf_op jit(solution)/shard_map/ppermute | solution.py:216
  29.8 5.0 %collective-permute-start = (bf16[32,4096]{1,0:T(8,128)(2,1)S(1)}, bf16[32,4096]{1,0:T(8,128)(2,1)S(1)}, u32[]{:S(2)}, u32[]{:S(2)}) collective-permute-start(bf16[32,4096]{1,0:T(8,128)(2,1)S(1)} %bitcast.30), channel_id=1, source_target_pairs={{0,448},{4,60},{8,456},{12,20},{16,464},{20,12},{24,472},{28,36},{... | collective-permute-start | bytes 786440 | tf_op jit(solution)/shard_map/ppermute | solution.py:216
  35.0 3.9 %collective-permute-start.3 = (bf16[64,4096]{1,0:T(8,128)(2,1)S(1)}, bf16[64,4096]{1,0:T(8,128)(2,1)}, u32[]{:S(2)}, u32[]{:S(2)}) collective-permute-start(bf16[64,4096]{1,0:T(8,128)(2,1)S(1)} %pad_maximum_fusion.2.refs_0_), channel_id=1, source_target_pairs={{0,448},{4,60},{8,456},{12,20},{16,464},{20,12},{24,472},{28,36},{... | collective-permute-start | bytes 1572872 | tf_op jit(solution)/shard_map/ppermute | solution.py:216
  38.9 1.9 collective-permute-start.2
  40.9 1.6 broadcast_in_dim.22
  42.5 3.6 %all-to-all-start.1 = ((bf16[4,256,1024]{2,1,0:T(8,128)(2,1)}), bf16[4,256,1024]{2,1,0:T(8,128)(2,1)S(1)}, u32[]{:S(2)}, u32[]{:S(2)}) async-start(bf16[4,256,1024]{2,1,0:T(8,128)(2,1)} %broadcast_in_dim.22), calls=%async_computation.1 | async-start | bytes 4194304 | tf_op jit(solution)/shard_map/all_to_all | solution.py:28
  46.5 3.0 %collective-permute-start.5 = (bf16[64,4096]{1,0:T(8,128)(2,1)}, bf16[64,4096]{1,0:T(8,128)(2,1)}, u32[]{:S(2)}, u32[]{:S(2)}) collective-permute-start(bf16[64,4096]{1,0:T(8,128)(2,1)} %collective-permute-done.3.refs_1_), channel_id=1, source_target_pairs={{0,64},{4,12},{8,72},{12,4},{16,80},{20,28},{24,88},{28,20},{32,96... | collective-permute-start | bytes 1572872 | tf_op jit(solution)/shard_map/ppermute | solution.py:216
  49.6 4.6 %collective-permute-start.4 = (bf16[64,4096]{1,0:T(8,128)(2,1)}, bf16[64,4096]{1,0:T(8,128)(2,1)}, u32[]{:S(2)}, u32[]{:S(2)}) collective-permute-start(bf16[64,4096]{1,0:T(8,128)(2,1)} %collective-permute-done.2.refs_1_), channel_id=1, source_target_pairs={{0,448},{4,60},{8,456},{12,20},{16,464},{20,12},{24,472},{28,36},{... | collective-permute-start | bytes 1572872 | tf_op jit(solution)/shard_map/ppermute | solution.py:216
  54.2 2.7 %collective-permute-done.5.refs_2_ = bf16[64,4096]{1,0:T(8,128)(2,1)} collective-permute-done((bf16[64,4096]{1,0:T(8,128)(2,1)}, bf16[64,4096]{1,0:T(8,128)(2,1)}, u32[]{:S(2)}, u32[]{:S(2)}) %collective-permute-start.5) | collective-permute-done | bytes 524320 | tf_op jit(solution)/shard_map/ppermute | solution.py:216
  56.9 4.4 %collective-permute-start.7 = (bf16[64,4096]{1,0:T(8,128)(2,1)}, bf16[64,4096]{1,0:T(8,128)(2,1)}, u32[]{:S(2)}, u32[]{:S(2)}) collective-permute-start(bf16[64,4096]{1,0:T(8,128)(2,1)} %collective-permute-done.5.refs_2_), channel_id=1, source_target_pairs={{0,448},{4,60},{8,456},{12,20},{16,464},{20,12},{24,472},{28,36},{... | collective-permute-start | bytes 1572872 | tf_op jit(solution)/shard_map/ppermute | solution.py:216
  61.3 2.4 %collective-permute-start.6 = (bf16[64,4096]{1,0:T(8,128)(2,1)}, bf16[64,4096]{1,0:T(8,128)(2,1)}, u32[]{:S(2)}, u32[]{:S(2)}) collective-permute-start(bf16[64,4096]{1,0:T(8,128)(2,1)} %collective-permute-done.4.refs_2_), channel_id=1, source_target_pairs={{0,64},{4,12},{8,72},{12,4},{16,80},{20,28},{24,88},{28,20},{32,96... | collective-permute-start | bytes 1572872 | tf_op jit(solution)/shard_map/ppermute | solution.py:216
  64.0 4.5 %collective-permute-done.7.refs_3_ = bf16[64,4096]{1,0:T(8,128)(2,1)} collective-permute-done((bf16[64,4096]{1,0:T(8,128)(2,1)}, bf16[64,4096]{1,0:T(8,128)(2,1)}, u32[]{:S(2)}, u32[]{:S(2)}) %collective-permute-start.7) | collective-permute-done | bytes 524320 | tf_op jit(solution)/shard_map/ppermute | solution.py:216
  68.5 2.0 shard_map.68.weight.refs_1_
  71.9 10.0 %collective-permute-start.9 = (bf16[256,4096]{1,0:T(8,128)(2,1)}, bf16[256,4096]{1,0:T(8,128)(2,1)S(1)}, u32[]{:S(2)}, u32[]{:S(2)}) collective-permute-start(bf16[256,4096]{1,0:T(8,128)(2,1)} %copy-done), channel_id=1, source_target_pairs={{0,4},{4,0},{8,12},{12,8},{16,20},{20,16},{24,28},{28,24},{32,36},... | collective-permute-start | bytes 6291464 | tf_op jit(solution)/shard_map/ppermute | solution.py:240
  82.0 2.0 shard_map.69.weight.refs_0_
  84.0 1.9 collective-permute-start.8
  92.1 4.5 %all-to-all-start.2 = ((f32[4,2,128]{2,1,0:T(2,128)}), f32[4,2,128]{2,1,0:T(2,128)S(1)}, u32[]{:S(2)}, u32[]{:S(2)}) async-start(f32[4,2,128]{2,1,0:T(2,128)} %broadcast_in_dim.24), calls=%async_computation.2 | async-start | bytes 8192 | tf_op jit(solution)/shard_map/all_to_all | solution.py:28
  96.8 3.9 %all-to-all-done.2 = f32[4,2,128]{2,1,0:T(2,128)S(1)} async-done(((f32[4,2,128]{2,1,0:T(2,128)}), f32[4,2,128]{2,1,0:T(2,128)S(1)}, u32[]{:S(2)}, u32[]{:S(2)}) %all-to-all-start.2) | async-done | bytes 4128 | tf_op jit(solution)/shard_map/all_to_all | solution.py:28
  101.4 30.1 %all_to_all.36 = bf16[128,2,1024]{2,1,0:T(2,128)(2,1)S(1)} all-to-all(bf16[128,2,1024]{2,1,0:T(2,128)(2,1)S(1)} %reshape.120), channel_id=1, replica_groups=mesh['dp'=128,'mp'=4] {'dp'}, dimensions={0} | all-to-all | bytes 1048576 | tf_op jit(solution)/shard_map/all_to_all | solution.py:28
  132.5 15.2 %all_to_all.37 = f32[4,384,128]{2,1,0:T(8,128)S(1)} all-to-all(f32[4,384,128]{2,1,0:T(8,128)S(1)} %broadcast_in_dim.25), channel_id=1, replica_groups=mesh['dp'=128,'mp'=4] {'mp'}, dimensions={0} | all-to-all | bytes 1572864 | tf_op jit(solution)/shard_map/all_to_all | solution.py:28
  149.1 27.1 %all_to_all.38 = bf16[128,2,1152]{2,1,0:T(2,128)(2,1)S(1)} all-to-all(bf16[128,2,1152]{2,1,0:T(2,128)(2,1)S(1)} %reshape.122), channel_id=1, replica_groups=mesh['dp'=128,'mp'=4] {'dp'}, dimensions={0} | all-to-all | bytes 1179648 | tf_op jit(solution)/shard_map/all_to_all | solution.py:28
  181.3 4.9 %shard_map.74 = bf16[4,256,1024]{2,1,0:T(8,128)(2,1)S(1)} custom-call(bf16[256,512]{1,0:T(8,128)(2,1)S(1)} %get-tuple-element.64.grad_own, bf16[256,512]{1,0:T(8,128)(2,1)S(1)} %get-tuple-element.63.grad_other, bf16[256,4096]{1,0:T(8,128)(2,1)S(1)} %copy-done.4, bf16[256,4096]{1,0:T(8,128)(2,1)S(1)} %copy-done.2, bf16[256,4096]{1,0:T(8,128)(2,1)} %copy-done.6, ...), custom_call_target="tpu_custom_call" | custom-call | flops 2147483648 | bytes 8388608 | tf_op jit(solution)/shard_map/pallas_call | solution.py:170
  186.2 29.2 %all_to_all.39 = bf16[4,256,1024]{2,1,0:T(8,128)(2,1)S(1)} all-to-all(bf16[4,256,1024]{2,1,0:T(8,128)(2,1)S(1)} %shard_map.74), channel_id=1, replica_groups=mesh['dp'=128,'mp'=4] {'mp'}, dimensions={0} | all-to-all | bytes 4194304 | tf_op jit(solution)/shard_map/all_to_all | solution.py:28
  (102 shorter events, 18.7 us)
Async XLA Ops:
  26.5 8.3 %collective-permute-start.1 = (bf16[32,4096]{1,0:T(8,128)(2,1)S(1)}, bf16[32,4096]{1,0:T(8,128)(2,1)S(1)}, u32[]{:S(2)}, u32[]{:S(2)}) collective-permute-start(bf16[32,4096]{1,0:T(8,128)(2,1)S(1)} %bitcast.32), channel_id=1, source_target_pairs={{0,64},{4,12},{8,72},{12,4},{16,80},{20,28},{24,88},{28,20},{32,96... | collective-permute-start | bytes 786440 | tf_op jit(solution)/shard_map/ppermute | solution.py:216
  29.8 11.0 %copy-start.8 = (bf16[128,1024]{1,0:T(8,128)(2,1)S(1)}, bf16[128,1024]{1,0:T(8,128)(2,1)}, u32[]{:S(2)}) copy-start(bf16[128,1024]{1,0:T(8,128)(2,1)} %param.6) | copy-start | bytes 786436
  29.8 11.0 %copy-start.9 = (bf16[128,1024]{1,0:T(8,128)(2,1)S(1)}, bf16[128,1024]{1,0:T(8,128)(2,1)}, u32[]{:S(2)}) copy-start(bf16[128,1024]{1,0:T(8,128)(2,1)} %param.5) | copy-start | bytes 786436
  29.8 9.0 %collective-permute-start = (bf16[32,4096]{1,0:T(8,128)(2,1)S(1)}, bf16[32,4096]{1,0:T(8,128)(2,1)S(1)}, u32[]{:S(2)}, u32[]{:S(2)}) collective-permute-start(bf16[32,4096]{1,0:T(8,128)(2,1)S(1)} %bitcast.30), channel_id=1, source_target_pairs={{0,448},{4,60},{8,456},{12,20},{16,464},{20,12},{24,472},{28,36},{... | collective-permute-start | bytes 786440 | tf_op jit(solution)/shard_map/ppermute | solution.py:216
  35.0 11.5 %collective-permute-start.3 = (bf16[64,4096]{1,0:T(8,128)(2,1)S(1)}, bf16[64,4096]{1,0:T(8,128)(2,1)}, u32[]{:S(2)}, u32[]{:S(2)}) collective-permute-start(bf16[64,4096]{1,0:T(8,128)(2,1)S(1)} %pad_maximum_fusion.2.refs_0_), channel_id=1, source_target_pairs={{0,448},{4,60},{8,456},{12,20},{16,464},{20,12},{24,472},{28,36},{... | collective-permute-start | bytes 1572872 | tf_op jit(solution)/shard_map/ppermute | solution.py:216
  38.9 10.6 %collective-permute-start.2 = (bf16[64,4096]{1,0:T(8,128)(2,1)S(1)}, bf16[64,4096]{1,0:T(8,128)(2,1)}, u32[]{:S(2)}, u32[]{:S(2)}) collective-permute-start(bf16[64,4096]{1,0:T(8,128)(2,1)S(1)} %pad_maximum_fusion.1.refs_0_), channel_id=1, source_target_pairs={{0,64},{4,12},{8,72},{12,4},{16,80},{20,28},{24,88},{28,20},{32,96... | collective-permute-start | bytes 1572872 | tf_op jit(solution)/shard_map/ppermute | solution.py:216
  42.5 29.3 %all-to-all-start.1 = ((bf16[4,256,1024]{2,1,0:T(8,128)(2,1)}), bf16[4,256,1024]{2,1,0:T(8,128)(2,1)S(1)}, u32[]{:S(2)}, u32[]{:S(2)}) async-start(bf16[4,256,1024]{2,1,0:T(8,128)(2,1)} %broadcast_in_dim.22), calls=%async_computation.1 | async-start | bytes 4194304 | tf_op jit(solution)/shard_map/all_to_all | solution.py:28
  46.5 10.4 %collective-permute-start.5 = (bf16[64,4096]{1,0:T(8,128)(2,1)}, bf16[64,4096]{1,0:T(8,128)(2,1)}, u32[]{:S(2)}, u32[]{:S(2)}) collective-permute-start(bf16[64,4096]{1,0:T(8,128)(2,1)} %collective-permute-done.3.refs_1_), channel_id=1, source_target_pairs={{0,64},{4,12},{8,72},{12,4},{16,80},{20,28},{24,88},{28,20},{32,96... | collective-permute-start | bytes 1572872 | tf_op jit(solution)/shard_map/ppermute | solution.py:216
  49.6 11.8 %collective-permute-start.4 = (bf16[64,4096]{1,0:T(8,128)(2,1)}, bf16[64,4096]{1,0:T(8,128)(2,1)}, u32[]{:S(2)}, u32[]{:S(2)}) collective-permute-start(bf16[64,4096]{1,0:T(8,128)(2,1)} %collective-permute-done.2.refs_1_), channel_id=1, source_target_pairs={{0,448},{4,60},{8,456},{12,20},{16,464},{20,12},{24,472},{28,36},{... | collective-permute-start | bytes 1572872 | tf_op jit(solution)/shard_map/ppermute | solution.py:216
  56.9 11.6 %collective-permute-start.7 = (bf16[64,4096]{1,0:T(8,128)(2,1)}, bf16[64,4096]{1,0:T(8,128)(2,1)}, u32[]{:S(2)}, u32[]{:S(2)}) collective-permute-start(bf16[64,4096]{1,0:T(8,128)(2,1)} %collective-permute-done.5.refs_2_), channel_id=1, source_target_pairs={{0,448},{4,60},{8,456},{12,20},{16,464},{20,12},{24,472},{28,36},{... | collective-permute-start | bytes 1572872 | tf_op jit(solution)/shard_map/ppermute | solution.py:216
  61.3 10.5 %collective-permute-start.6 = (bf16[64,4096]{1,0:T(8,128)(2,1)}, bf16[64,4096]{1,0:T(8,128)(2,1)}, u32[]{:S(2)}, u32[]{:S(2)}) collective-permute-start(bf16[64,4096]{1,0:T(8,128)(2,1)} %collective-permute-done.4.refs_2_), channel_id=1, source_target_pairs={{0,64},{4,12},{8,72},{12,4},{16,80},{20,28},{24,88},{28,20},{32,96... | collective-permute-start | bytes 1572872 | tf_op jit(solution)/shard_map/ppermute | solution.py:216
  70.5 1.3 copy-start
  71.9 16.0 %collective-permute-start.9 = (bf16[256,4096]{1,0:T(8,128)(2,1)}, bf16[256,4096]{1,0:T(8,128)(2,1)S(1)}, u32[]{:S(2)}, u32[]{:S(2)}) collective-permute-start(bf16[256,4096]{1,0:T(8,128)(2,1)} %copy-done), channel_id=1, source_target_pairs={{0,4},{4,0},{8,12},{12,8},{16,20},{20,16},{24,28},{28,24},{32,36},... | collective-permute-start | bytes 6291464 | tf_op jit(solution)/shard_map/ppermute | solution.py:240
  82.0 4.0 %copy-start.11 = (s32[128,1]{0,1:T(1,128)S(1)}, s32[128,1]{0,1:T(1,128)}, u32[]{:S(2)}) copy-start(s32[128,1]{0,1:T(1,128)} %param.9) | copy-start | bytes 1540
  82.0 4.2 %copy-start.1 = (bf16[256,4096]{1,0:T(8,128)(2,1)S(1)}, bf16[256,4096]{1,0:T(8,128)(2,1)}, u32[]{:S(2)}) copy-start(bf16[256,4096]{1,0:T(8,128)(2,1)} %copy-done) | copy-start | bytes 6291460
  84.0 3.0 %copy-start.3 = (bf16[256,4096]{1,0:T(8,128)(2,1)}, bf16[256,4096]{1,0:T(8,128)(2,1)S(1)}, u32[]{:S(2)}) copy-start(bf16[256,4096]{1,0:T(8,128)(2,1)S(1)} %shard_map.69.weight.refs_0_) | copy-start | bytes 6291460
  84.0 6.1 %collective-permute-start.8 = (bf16[256,4096]{1,0:T(8,128)(2,1)S(1)}, bf16[256,4096]{1,0:T(8,128)(2,1)S(1)}, u32[]{:S(2)}, u32[]{:S(2)}) collective-permute-start(bf16[256,4096]{1,0:T(8,128)(2,1)S(1)} %shard_map.69.weight.refs_0_), channel_id=1, source_target_pairs={{0,4},{4,0},{8,12},{12,8},{16,20},{20,16},{24,28},{28,24},{32,36},... | collective-permute-start | bytes 6291464 | tf_op jit(solution)/shard_map/ppermute | solution.py:240
  87.8 1.3 copy-start.5
  90.1 1.3 copy-start.6
  92.1 8.6 %all-to-all-start.2 = ((f32[4,2,128]{2,1,0:T(2,128)}), f32[4,2,128]{2,1,0:T(2,128)S(1)}, u32[]{:S(2)}, u32[]{:S(2)}) async-start(f32[4,2,128]{2,1,0:T(2,128)} %broadcast_in_dim.24), calls=%async_computation.2 | async-start | bytes 8192 | tf_op jit(solution)/shard_map/all_to_all | solution.py:28
  131.7 0.8 copy-start.7
  176.1 2.4 %copy-start.10 = (s32[128]{0:T(128)S(1)}, s32[128]{0:T(128)}, u32[]{:S(2)}) copy-start(s32[128]{0:T(128)} %param.8) | copy-start | bytes 1540
  179.0 1.6 copy-start.4
  179.3 2.0 copy-start.2
